TPU v7x, 32 devices: a whole 2x2x4 slice. The times are simulated.
32 devices in a mesh: leaf: 8 (over y, x, core), col: 4 (over z).
Axes of the slice: x: 2, y: 2, z: 4, core: 2. Of those that a mesh axis runs over, the one named last changes fastest.
Arguments:
- basis: float32 [1024, 64, 256], P(('leaf', 'col')), may hold values from -0.4 to 0.4
- transfer: float32 [2040, 64, 64], P('leaf')
- top_transfer: float32 [6, 64, 64], replicated
- blocks0: bfloat16 [8192, 64, 64], P(('leaf', 'col')), may hold values from -6 to 6
- pairs0: int32 [8192, 2], P(('leaf', 'col')), may hold values from 0 to 1023, as said below
- counts0: int32 [32], P(('leaf', 'col')), may hold values from 128 to 256, as said below
- blocks1: bfloat16 [4096, 64, 64], P(('leaf', 'col')), may hold values from -6 to 6
- pairs1: int32 [4096, 2], P(('leaf', 'col')), may hold values from 0 to 511, as said below
- counts1: int32 [32], P(('leaf', 'col')), may hold values from 64 to 128, as said below
Outputs:
- projected0: bfloat16 [8192, 64, 64], P(('leaf', 'col'))
- projected1: bfloat16 [4096, 64, 64], P(('leaf', 'col'))
- root_factor: float32 [64, 64], replicated
- ancestor_factors: float32 [8, 3, 64, 64], P('leaf')
Inputs may be any that keep to these rules, and one draw needn't show every extreme that they name: `pairs0`: the rows of one device (leaf index i, col index j) name a row cluster of the level within i's subtree (i * 128 / 2^l to (i + 1) * 128 / 2^l - 1) and a column cluster whose index modulo 4 is j. `pairs1`: as for pairs0, on the level above the leaves. `counts0`: slots at or past a device's count are padding; some device uses all 256 slots in every draw. `counts1`: slots at or past a device's count are padding; some device uses all 128 slots in every draw.
All inputs are finite; a program needn't handle non-finite values.
Results may differ from a plain program's by a relative error of at most 0.0065.
Values may be sent and summed in bfloat16 or wider, within the bound.
No kernel may reach another device: no remote copies, remote signals or barrier semaphores. Data moves between devices by JAX's collectives and lax.ppermute only.
A program may use at most 128 MiB of HBM per device.

v0:
```python
import jax
import jax.numpy as jnp
from jax import lax
from jax.sharding import PartitionSpec as P


def swapped(block, axis, stride):
    count = lax.axis_size(axis)
    route = []
    for low in range(count):
        high = low | 1 << stride
        if high != low and high < count:
            route += [(low, high), (high, low)]
    return lax.ppermute(block, axis, route)


def lift_gram(gram, xfer):
    product = jnp.einsum("cab,cbj->caj", gram, xfer, precision=lax.Precision.HIGHEST)
    return jnp.einsum("cak,caj->ckj", xfer, product, precision=lax.Precision.HIGHEST)


def factor(gram):
    return jnp.swapaxes(jnp.linalg.cholesky(gram), -1, -2)


def project_level(blocks, pairs, counts, row_factors, col_factors, row_base, col_count):
    slots = blocks.shape[0]
    row_local = pairs[:, 0] - row_base
    col_local = pairs[:, 1] // col_count
    row_fac = jnp.take(row_factors, row_local, axis=0)
    col_fac = jnp.take(col_factors, col_local, axis=0)
    left = jnp.einsum("bik,bkj->bij", row_fac, blocks, preferred_element_type=jnp.float32).astype(
        jnp.bfloat16
    )
    result = jnp.einsum("bij,blj->bil", left, col_fac, preferred_element_type=jnp.float32)
    keep = jnp.arange(slots, dtype=jnp.int32) < counts[0]
    return jnp.where(keep[:, None, None], result, 0.0).astype(jnp.bfloat16)


def on_device(basis, transfer, top_transfer, blocks0, pairs0, counts0, blocks1, pairs1, counts1):
    own_count = basis.shape[0]
    rank = basis.shape[1]
    col_count = lax.axis_size("col")
    col_index = lax.axis_index("col")
    leaf_index = lax.axis_index("leaf")
    leaf_count = own_count * col_count
    own_gram = jnp.einsum("ckm,cjm->ckj", basis, basis, precision=lax.Precision.HIGHEST)
    gram_leaves = lax.all_gather(own_gram, "col", axis=0, tiled=True)
    factor0 = factor(gram_leaves).astype(jnp.bfloat16)
    lifted = lift_gram(gram_leaves, transfer[0:leaf_count])
    gram_now = lifted[0::2] + lifted[1::2]
    factor1 = factor(gram_now).astype(jnp.bfloat16)
    offset = leaf_count
    count = leaf_count // 2
    while count > 1:
        lifted = lift_gram(gram_now, transfer[offset : offset + count])
        gram_now = lifted[0::2] + lifted[1::2]
        offset += count
        count //= 2
    own_level0 = lax.dynamic_index_in_dim(
        factor0.reshape(leaf_count // col_count, col_count, rank, rank),
        col_index,
        axis=1,
        keepdims=False,
    )
    own_level1 = lax.dynamic_index_in_dim(
        factor1.reshape(leaf_count // (2 * col_count), col_count, rank, rank),
        col_index,
        axis=1,
        keepdims=False,
    )
    columns0, columns1 = (
        lax.all_gather(own_level0, "leaf", axis=0, tiled=True),
        lax.all_gather(own_level1, "leaf", axis=0, tiled=True),
    )
    projected0 = project_level(
        blocks0, pairs0, counts0, factor0, columns0, leaf_index * leaf_count, col_count
    )
    projected1 = project_level(
        blocks1, pairs1, counts1, factor1, columns1, leaf_index * (leaf_count // 2), col_count
    )
    leaf_total = lax.axis_size("leaf")
    top_height = leaf_total.bit_length() - 1
    root_xfer = transfer[offset : offset + 1]
    ancestors = []
    xfer_now = root_xfer
    off_top = 0
    for height in range(top_height):
        if height > 0:
            xfer_now = lax.dynamic_slice_in_dim(
                top_transfer, off_top + jnp.right_shift(leaf_index, height), 1, 0
            )
            off_top += leaf_total >> height
        lifted = lift_gram(gram_now, xfer_now)
        sibling = swapped(lifted, "leaf", height)
        gram_now = lifted + sibling
        ancestors.append(factor(gram_now))
    ancestor_factors = jnp.stack(ancestors, axis=1)
    root_factor = factor(gram_now[0])
    return (projected0, projected1, root_factor, ancestor_factors)


def solution(mesh):
    in_specs = (
        P(("leaf", "col"), None, None),
        P("leaf", None, None),
        P(),
        P(("leaf", "col"), None, None),
        P(("leaf", "col"), None),
        P(("leaf", "col")),
        P(("leaf", "col"), None, None),
        P(("leaf", "col"), None),
        P(("leaf", "col")),
    )
    out_specs = (
        P(("leaf", "col"), None, None),
        P(("leaf", "col"), None, None),
        P(),
        P("leaf", None, None, None),
    )
    return jax.shard_map(
        on_device, mesh=mesh, in_specs=in_specs, out_specs=out_specs, check_vma=False
    )
```

profile of v0, /device:TPU:0, one launch (start us, length us, event | category | flops | bytes accessed | tf_op | source)
XLA Modules:
  0.0 1377.5 jit_solution(12393514170900254783)
XLA Ops:
  8.8 3.0 fusion.83
  27.2 4.7 copy.301
  31.9 3.1 copy.303
  37.5 3.0 copy.305
  45.1 2.9 copy.308
  48.0 2.9 copy.309
  50.9 4.7 copy.247
  56.3 7.5 copy.239
  69.2 26.2 %all-gather.6.cloned.1.call-done = f32[128,64,64]{2,1,0:T(8,128)} async-done(((f32[32,64,64]{2,1,0:T(8,128)}), f32[128,64,64]{2,1,0:T(8,128)}) %all-gather.6.cloned.1.call-update) | async-done | bytes 2097168 | tf_op jit(solution)/shard_map/all_gather | solution.py:48
  95.4 10.9 fusion.84
  106.3 5.4 convolution_bitcast_fusion
  115.4 2.9 copy.245
  118.3 5.1 fusion.85
  135.5 375.7 %custom-call.15 = f32[64,64,64]{2,1,0:T(8,128)S(1)} custom-call(f32[64,64,64]{2,1,0:T(8,128)} %fusion.18), custom_call_target="Cholesky" | custom-call | tf_op jit(solution)/shard_map/jit(cholesky)/cholesky | solution.py:23
  512.9 5.6 copy.235
  518.6 7.0 fusion
  525.5 752.2 %custom-call.14 = f32[128,64,64]{2,1,0:T(8,128)} custom-call(f32[128,64,64]{2,1,0:T(8,128)} %fusion), custom_call_target="Cholesky" | custom-call | tf_op jit(solution)/shard_map/jit(cholesky)/cholesky | solution.py:23
  1277.8 3.0 select_reduce_fusion
  1281.3 2.9 select_convert_fusion.2
  1290.5 3.3 gather_fusion
  1296.0 5.8 custom-call.18
  1303.3 5.9 custom-call.19
  1314.4 5.8 custom-call.20
  1323.2 5.9 cholesky.129
  1331.1 2.7 gather_fusion.3
  1333.8 2.8 copy.249
  1336.6 4.6 select_convert_fusion.1
  1341.2 3.2 copy.278
  1344.4 5.4 gather_fusion.1
  1349.7 6.4 copy.241
  1356.1 8.8 select_convert_fusion
  1364.9 5.9 copy.277
  (133 shorter events, 66.6 us)
Async XLA Ops:
  7.2 1.6 copy-start
  7.2 88.3 %all-gather.6.cloned.1.call-start = ((), (), s32[]{:S(2)}) async-start(), calls=%async_computation | async-start | bytes 5242880 | tf_op jit(solution)/shard_map/all_gather | solution.py:48
  11.8 1319.3 %all-gather.10.cloned.1.call-start = ((), (), s32[]{:S(2)}) async-start(), calls=%async_computation.2 | async-start | bytes 2359296 | tf_op jit(solution)/shard_map/all_gather | solution.py:74
  11.9 2.2 copy-start.2
  25.3 1.9 slice-start
  56.3 9.3 copy-start.13
  56.3 11.1 copy-start.12
  95.4 10.9 copy-start.3
  111.8 2.0 copy-start.4
  127.6 1.2 copy-start.8
  127.6 5.8 copy-start.7
  128.8 3.3 copy-start.9
  129.9 3.0 copy-start.10
  129.9 3.6 copy-start.5
  133.3 1160.5 %collective-permute-start = (f32[1,64,64]{1,2,0:T(8,128)S(1)}, f32[1,64,64]{1,2,0:T(8,128)S(1)}, u32[]{:S(2)}, u32[]{:S(2)}) collective-permute-start(f32[1,64,64]{1,2,0:T(8,128)S(1)} %convolution_bitcast_fusion.9), channel_id=1, source_target_pairs={{0,4},{4,0},{8,12},{12,8},{16,20},{20,16},{24,28},{28,24},{1,5},{5... | collective-permute-start | bytes 49160 | tf_op jit(solution)/shard_map/ppermute | solution.py:14
  512.9 831.5 %all-gather.8.cloned.1.call-start = ((), (), s32[]{:S(2)}) async-start(), calls=%async_computation.1 | async-start | bytes 4718592 | tf_op jit(solution)/shard_map/all_gather | solution.py:73
  1281.3 3.5 copy-start.6
  1290.5 3.4 copy-start.11
  1294.4 8.8 collective-permute-start.1
  1309.7 4.6 collective-permute-start.2
  1333.8 2.8 copy-start.14
  1333.8 2.8 copy-start.15
  1333.8 2.8 copy-start.19
  1349.7 6.4 copy-start.16
  1349.7 6.4 copy-start.17
  1349.7 6.4 copy-start.18
  1356.1 14.7 %copy-start.1 = (f32[32,64,256]{2,1,0:T(8,128)S(1)}, f32[32,64,256]{2,1,0:T(8,128)}, u32[]{:S(2)}) copy-start(f32[32,64,256]{2,1,0:T(8,128)} %param.10) | copy-start | bytes 6291460
Sparse Core Ops, SparseCore 0:
  11.9 83.4 all-gather.5
  513.0 26.7 all-gather.9
  1290.6 35.9 all-gather.7
where the time goes:
time: 1380 us
  other arithmetic  1180 us (86%)
  local copies, waits for them, and re-layouts  101 us (7%)
  matrix products  48.5 us (4%)
  waiting for transfers between devices  28.7 us (2%)
  between operations  15.8 us (1%)
    another operation x19, other arithmetic, factor(): return jnp.swapaxes(jnp.linalg.cholesky(gram), -1, -2)  1160 us
    unnamed x56, local copies, waits for them, and re-layouts  55.5 us
  transfers between devices with their start and end apart: 6, of which 2 were waited for; matrix products, arithmetic and copies ran while one was open for 91% of the time, Pallas kernels for 0%

commit v1 on v0

v1 whole, which is shorter than its diff:
```python
import functools

import jax
import jax.numpy as jnp
from jax import lax
from jax.experimental import pallas as pl
from jax.experimental.pallas import tpu as pltpu
from jax.sharding import PartitionSpec as P

BF, F32 = jnp.bfloat16, jnp.float32
EXACT = lax.Precision.HIGHEST
NT = (((1,), (1,)), ((), ()))
NN = (((1,), (0,)), ((), ()))
K = 64
H = K // 2
LANES = 128
SMEM = pl.BlockSpec(memory_space=pltpu.SMEM)
VMEM = pl.BlockSpec(memory_space=pltpu.VMEM)
PARAMS = pltpu.CompilerParams(vmem_limit_bytes=48 * 2**20)


def unhalf(x):
    return jnp.concatenate([x[:, :K], x[:, K:]], axis=0)


def halve(x):
    return jnp.concatenate([x[:H], x[H:]], axis=1)


def mul(x, y, dims):
    return lax.dot_general(x, y, dims, precision=EXACT, preferred_element_type=F32)


def lift(gram, xfer_t):
    return mul(mul(xfer_t, gram, NN), xfer_t, NT)


def unpack_transfers(xfer_ref, xt):
    @pl.loop(0, H)
    def _(q):
        xt[:, q, :] = jnp.concatenate([xfer_ref[:, q, :], xfer_ref[:, q + H, :]], axis=0).T


def cholesky_lanes(a):
    sub = lax.broadcasted_iota(jnp.int32, (8, a.shape[2]), 0)

    def cols(block):
        return pl.ds(pl.multiple_of(8 * block, 8), 8)

    for panel in range(K // 8):
        base = 8 * panel
        scale = []
        rows = [a[base + k, pl.ds(base, 8), :] for k in range(8)]
        for k in range(8):
            scale.append(lax.rsqrt(rows[k][k : k + 1, :]))
            rows[k] = rows[k] * scale[k]
            for i in range(k + 1, 8):
                rows[i] = rows[i] - rows[k][i : i + 1, :] * rows[k]
        for k in range(8):
            a[base + k, pl.ds(base, 8), :] = jnp.where(sub >= k, rows[k], 0.0)
        for j in range(panel + 1, K // 8):
            new = []
            for k in range(8):
                acc = a[base + k, pl.ds(8 * j, 8), :]
                for p in range(k):
                    acc = acc - rows[p][k : k + 1, :] * new[p]
                new.append(acc * scale[k])
            for k in range(8):
                a[base + k, pl.ds(8 * j, 8), :] = new[k]
        if panel < K // 8 - 1:

            @pl.loop(panel + 1, K // 8)
            def _(i_block):
                left = [a[base + k, cols(i_block), :] for k in range(8)]

                @pl.loop(i_block, K // 8)
                def _(j_block):
                    right = [a[base + k, cols(j_block), :] for k in range(8)]
                    for i in range(8):
                        acc = a[8 * i_block + i, cols(j_block), :]
                        for k in range(8):
                            acc = acc - left[k][i : i + 1, :] * right[k]
                        a[8 * i_block + i, cols(j_block), :] = acc

    for i in range(8, K):
        a[i, pl.ds(0, i // 8 * 8), :] = jnp.zeros((i // 8 * 8, a.shape[2]), F32)


def factor_halved(s, a):
    @pl.loop(0, H)
    def _(q):
        y = s[:, q, :].T
        a[q] = y[:K]
        a[q + H] = y[K:]

    cholesky_lanes(a)

    @pl.loop(0, H)
    def _(q):
        s[:, q, :] = jnp.concatenate([a[q], a[q + H]], axis=0).T


def factor_kernel(own, at_ref, basis_ref, xfer_ref, fac_ref, gram1_ref, xt, s, a):
    first = at_ref[1] * own
    unpack_transfers(xfer_ref, xt)

    @pl.loop(0, own // 2)
    def _(p):
        total = None
        for c in range(2):
            points = basis_ref[2 * p + c]
            gram = mul(points, points, NT)
            s[2 * p + c] = halve(gram)
            lifted = lift(gram, unhalf(xt[first + 2 * p + c]))
            total = lifted if total is None else total + lifted
        gram1_ref[p] = total
        s[own + p] = halve(total)

    factor_halved(s, a)
    fac_ref[...] = s[0 : own + own // 2].astype(BF)


def own_factors(at, basis, xfer_lanes):
    own = basis.shape[0]
    count = own + own // 2
    return pl.pallas_call(
        functools.partial(factor_kernel, own),
        out_shape=(
            jax.ShapeDtypeStruct((count, H, 2 * K), BF),
            jax.ShapeDtypeStruct((own // 2, K, K), F32),
        ),
        grid=(1,),
        in_specs=[
            SMEM,
            pl.BlockSpec(basis.shape, lambda i: (0, 0, 0)),
            pl.BlockSpec((K, K, LANES), lambda i: (0, 0, 0)),
        ],
        out_specs=(
            pl.BlockSpec((count, H, 2 * K), lambda i: (0, 0, 0)),
            pl.BlockSpec((own // 2, K, K), lambda i: (0, 0, 0)),
        ),
        scratch_shapes=[pltpu.VMEM((LANES, H, 2 * K), F32)] * 2 + [pltpu.VMEM((K, K, LANES), F32)],
        compiler_params=PARAMS,
    )(at, basis, xfer_lanes)


def chain_kernel(own, cols, at_ref, gram1_ref, xfer_ref, out_ref, xt, g):
    col = at_ref[1]
    unpack_transfers(xfer_ref, xt)
    g[...] = gram1_ref[...]
    offset = 0
    here = own // 2
    width = own * cols // 2
    while here > 1:

        def step(p, _, first=offset + col * here):
            low = lift(g[2 * p], unhalf(xt[first + 2 * p]))
            high = lift(g[2 * p + 1], unhalf(xt[first + 2 * p + 1]))
            g[p] = low + high
            return 0

        lax.fori_loop(0, here // 2, step, 0)
        offset += width
        width //= 2
        here //= 2
    gram = g[0]
    shift = 0
    while width >= 1:
        gram = lift(gram, unhalf(xt[offset + jnp.right_shift(col, shift)]))
        offset += width
        width //= 2
        shift += 1
    out_ref[...] = halve(gram)


def lifted_root(at, gram1, xfer_lanes, own, cols):
    return pl.pallas_call(
        functools.partial(chain_kernel, own, cols),
        out_shape=jax.ShapeDtypeStruct((H, 2 * K), F32),
        grid=(1,),
        in_specs=[
            SMEM,
            pl.BlockSpec(gram1.shape, lambda i: (0, 0, 0)),
            pl.BlockSpec((K, K, LANES), lambda i: (0, 0, 1)),
        ],
        out_specs=pl.BlockSpec((H, 2 * K), lambda i: (0, 0)),
        scratch_shapes=[pltpu.VMEM((LANES, H, 2 * K), F32), pltpu.VMEM(gram1.shape, F32)],
        compiler_params=PARAMS,
    )(at, gram1, xfer_lanes)


def top_kernel(leaves, cols, at_ref, parts_ref, top_ref, anc_ref, root_ref, s, a):
    group = 2 * cols
    level = []
    for m in range(leaves // 2):
        total = parts_ref[m * group]
        for c in range(1, group):
            total = total + parts_ref[m * group + c]
        level.append(unhalf(total))
    heights = []
    slot = 0
    off_top = 0
    while True:
        heights.append(slot)
        for m, gram in enumerate(level):
            s[slot + m] = halve(gram)
        slot += len(level)
        if len(level) == 1:
            break
        lifted = []
        for m, gram in enumerate(level):
            xfer = top_ref[off_top + m]
            lifted.append(lift(gram, xfer.T))
        off_top += len(level)
        level = [lifted[2 * m] + lifted[2 * m + 1] for m in range(len(level) // 2)]
    factor_halved(s, a)
    for h, start in enumerate(heights):
        anc_ref[0, h] = unhalf(s[start + jnp.right_shift(at_ref[0], h + 1)])
    root_ref[...] = unhalf(s[heights[-1]])


def top_factors(at, parts, top_transfer, leaves, cols):
    height = leaves.bit_length() - 1
    return pl.pallas_call(
        functools.partial(top_kernel, leaves, cols),
        out_shape=(
            jax.ShapeDtypeStruct((1, height, K, K), F32),
            jax.ShapeDtypeStruct((K, K), F32),
        ),
        in_specs=[SMEM, VMEM, VMEM],
        out_specs=(VMEM, VMEM),
        scratch_shapes=[pltpu.VMEM((LANES, H, 2 * K), F32), pltpu.VMEM((K, K, LANES), F32)],
        compiler_params=PARAMS,
    )(at, parts, top_transfer)


UNROLL = 16


def lane_groups(sizes):
    return [(which, lane) for which, size in enumerate(sizes) for lane in range(0, size, LANES)]


def left_kernel(groups, index_ref, table_ref, *refs):
    blocks, left_ref, bt = refs[:-2], refs[-2], refs[-1]
    for g, (which, lane) in enumerate(groups):
        src = blocks[which]

        @pl.loop(0, H)
        def _(q):
            lanes = pl.ds(lane, LANES)
            x = jnp.concatenate([src[q, :, lanes], src[q + H, :, lanes]], axis=0)
            bt[:, q, :] = x.astype(F32).T

        @pl.loop(0, LANES // UNROLL)
        def _(step):
            for u in range(UNROLL):
                b = step * UNROLL + u
                row = unhalf(table_ref[index_ref[LANES * g + b]])
                block = unhalf(bt[b].astype(BF))
                y = lax.dot_general(row, block, NN, preferred_element_type=F32)
                left_ref[LANES * g + b] = halve(y.astype(BF))


def left_products(table, index, blocks):
    groups = lane_groups([x.shape[2] for x in blocks])
    return pl.pallas_call(
        functools.partial(left_kernel, groups),
        out_shape=jax.ShapeDtypeStruct((LANES * len(groups), H, 2 * K), BF),
        in_specs=[SMEM, VMEM] + [VMEM] * len(blocks),
        out_specs=VMEM,
        scratch_shapes=[pltpu.VMEM((LANES, H, 2 * K), F32)],
        compiler_params=PARAMS,
    )(index, table, *blocks)


def right_kernel(groups, outs, index_ref, counts_ref, table_ref, left_ref, *refs):
    out_refs, pt = refs[:outs], refs[outs]
    for g, (which, lane) in enumerate(groups):
        dst = out_refs[which]

        @pl.loop(0, LANES // UNROLL)
        def _(step):
            for u in range(UNROLL):
                b = step * UNROLL + u
                col = unhalf(table_ref[index_ref[LANES * g + b]])
                left = unhalf(left_ref[LANES * g + b])
                y = lax.dot_general(left, col, NT, preferred_element_type=F32)
                pt[b] = halve(y)

        keep = lax.broadcasted_iota(jnp.int32, (2 * K, LANES), 1) < counts_ref[which] - lane

        @pl.loop(0, H)
        def _(q):
            y = jnp.where(keep, pt[:, q, :].T, 0.0).astype(BF)
            dst[q, :, pl.ds(lane, LANES)] = y[:K]
            dst[q + H, :, pl.ds(lane, LANES)] = y[K:]


def right_products(table, index, counts, left, sizes):
    groups = lane_groups(sizes)
    return pl.pallas_call(
        functools.partial(right_kernel, groups, len(sizes)),
        out_shape=tuple(jax.ShapeDtypeStruct((K, K, size), BF) for size in sizes),
        in_specs=[SMEM, SMEM, VMEM, VMEM],
        out_specs=(VMEM,) * len(sizes),
        scratch_shapes=[pltpu.VMEM((LANES, H, 2 * K), F32)],
        compiler_params=PARAMS,
    )(index, counts, table, left)


def on_device(basis, transfer, top_transfer, blocks0, pairs0, counts0, blocks1, pairs1, counts1):
    own = basis.shape[0]
    cols = lax.axis_size("col")
    leaves = lax.axis_size("leaf")
    leaf, col = lax.axis_index("leaf"), lax.axis_index("col")
    at = jnp.stack([leaf, col]).astype(jnp.int32)
    xfer_lanes = jnp.transpose(transfer, (1, 2, 0))
    lanes0, lanes1 = jnp.transpose(blocks0, (1, 2, 0)), jnp.transpose(blocks1, (1, 2, 0))

    factors, gram1 = own_factors(at, basis, xfer_lanes)
    count = own + own // 2
    row_table = lax.all_gather(factors, "col", axis=0, tiled=True)

    parts = count // cols
    part = lax.dynamic_index_in_dim(
        row_table.reshape(cols * parts, cols, H, 2 * K), col, axis=1, keepdims=False
    )
    col_table = lax.all_gather(part, "leaf", axis=0, tiled=True)

    def indices(pairs, level):
        size = own >> level
        row = pairs[:, 0] - leaf * (size * cols)
        row = row // size * count + level * own + row % size
        column = pairs[:, 1] // size * parts + level * (own // cols) + pairs[:, 1] % size // cols
        return row, column

    row0, column0 = indices(pairs0, 0)
    row1, column1 = indices(pairs1, 1)
    left = left_products(row_table, jnp.concatenate([row0, row1]), (lanes0, lanes1))

    lifted = lifted_root(at, gram1, xfer_lanes, own, cols)
    lifted_all = lax.all_gather(lifted, ("leaf", "col"), axis=0)
    ancestors, root = top_factors(at, lifted_all, top_transfer, leaves, cols)

    out0, out1 = right_products(
        col_table,
        jnp.concatenate([column0, column1]),
        jnp.concatenate([counts0, counts1]),
        left,
        (blocks0.shape[0], blocks1.shape[0]),
    )
    return (jnp.transpose(out0, (2, 0, 1)), jnp.transpose(out1, (2, 0, 1)), root, ancestors)


def solution(mesh):
    in_specs = (
        P(("leaf", "col"), None, None),
        P("leaf", None, None),
        P(),
        P(("leaf", "col"), None, None),
        P(("leaf", "col"), None),
        P(("leaf", "col")),
        P(("leaf", "col"), None, None),
        P(("leaf", "col"), None),
        P(("leaf", "col")),
    )
    out_specs = (
        P(("leaf", "col"), None, None),
        P(("leaf", "col"), None, None),
        P(),
        P("leaf", None, None, None),
    )
    return jax.shard_map(
        on_device, mesh=mesh, in_specs=in_specs, out_specs=out_specs, check_vma=False
    )
```

time: 1380 us -> 252 us (0.18)
  other arithmetic: 1180 us -> 0.22 us
  Pallas kernels: 0 us -> 118 us
  local copies, waits for them, and re-layouts: 101 us -> 7.46 us
  blocking collectives: 0 us -> 70.6 us
  matrix products: 48.5 us -> 0 us
    another operation x22 -> x1, other arithmetic: 1160 us -> 0.08 us  [on_device(): at = jnp.stack([leaf, col]).astype(jnp.int32)]
    pallas_call x0 -> x5, Pallas kernels: none -> 118 us  [the longest x1 36.7 us: own_factors(): pl.pallas_call(functools.partial(factor_kernel, own), out_shape=(jax.Shap...]
    all_gather x0 -> x1, blocking collectives: none -> 70.6 us  [on_device(): lifted_all = lax.all_gather(lifted, ('leaf', 'col'), axis=0)]
    unnamed x56 -> x18, local copies, waits for them, and re-layouts: 55.5 us -> 5.69 us
    dot_general x23 -> x0, matrix products: 48.5 us -> none  [the longest x10 21 us: lift_gram(): jnp.einsum('cab,cbj->caj', gram, xfer, precision=lax.Precision.HIGHEST)]
    gather x6 -> x0, local copies, waits for them, and re-layouts: 22.8 us -> none  [the longest x4 17.2 us: project_level(): col_fac = jnp.take(col_factors, col_local, axis=0)]
    all_gather x3 -> x2, waiting for transfers between devices: 26.2 us -> 39.9 us  [the longest x1 39.9 us: on_device(): row_table = lax.all_gather(factors, 'col', axis=0, tiled=True)]
  transfers between devices with their start and end apart: 6 -> 2, of which waited for: 2 -> 1; matrix products, arithmetic and copies ran while one was open for 91% -> 0% of each run, Pallas kernels for 0% -> 22%
where the time goes in v1:
time: 252 us; the launch traced here: 251 us
  Pallas kernels  118 us (47%)
  blocking collectives  70.6 us (28%)
  waiting for transfers between devices  39.9 us (16%)
  between operations  15.4 us (6%)
  local copies, waits for them, and re-layouts  7.46 us (3%)
    all_gather x1, blocking collectives, on_device(): lifted_all = lax.all_gather(lifted, ('leaf', 'col'), axis=0)  70.6 us
    all_gather x1, waiting for transfers between devices, on_device(): row_table = lax.all_gather(factors, 'col', axis=0, tiled=True)  39.9 us
    pallas_call x1, Pallas kernels, own_factors(): pl.pallas_call(functools.partial(factor_kernel, own), out_shape=(jax.Shap...  36.7 us
    pallas_call x1, Pallas kernels, right_products(): pl.pallas_call(functools.partial(right_kernel, groups, len(sizes)), out_s...  26.4 us
    pallas_call x1, Pallas kernels, left_products(): pl.pallas_call(functools.partial(left_kernel, groups), out_shape=jax.Shap...  24.6 us
    pallas_call x1, Pallas kernels, top_factors(): pl.pallas_call(functools.partial(top_kernel, leaves, cols), out_shape=(ja...  15.2 us
    pallas_call x1, Pallas kernels, lifted_root(): pl.pallas_call(functools.partial(chain_kernel, own, cols), out_shape=jax....  14.6 us
    unnamed x18, local copies, waits for them, and re-layouts  5.69 us
  transfers between devices with their start and end apart: 2, of which 1 were waited for; matrix products, arithmetic and copies ran while one was open for 0% of the time, Pallas kernels for 22%

profile of v1, /device:TPU:0, one launch (start us, length us, event | category | flops | bytes accessed | tf_op | source)
XLA Modules:
  0.0 251.4 jit_solution(3291293801605260297)
XLA Ops:
  7.2 0.0 all-gather.5.cloned.1.call-start
  7.2 0.1 pad_add_fusion.3.at_ref
  7.3 0.0 copy-start.3
  7.3 1.6 copy-done.3
  8.9 36.7 %shard_map.120 = (bf16[48,32,128]{2,1,0:T(8,128)(2,1)}, f32[16,64,64]{2,1,0:T(8,128)S(1)}) custom-call(s32[2]{0:T(128)S(1)} %pad_add_fusion.3.at_ref, f32[32,64,256]{2,1,0:T(8,128)S(1)} %copy-done.3, f32[64,64,255]{2,1,0:T(8,128)} %bitcast.38), custom_call_target="tpu_custom_call" | custom-call | tf_op jit(solution)/shard_map/pallas_call | solution.py:126
  45.6 0.0 all-gather.5.cloned.1.call-update
  45.6 0.0 all-gather.7.cloned.1.call-start
  45.7 39.9 %all-gather.5.cloned.1.call-done.table_ref = bf16[192,32,128]{2,1,0:T(8,128)(2,1)} async-done(((bf16[48,32,128]{2,1,0:T(8,128)(2,1)}), bf16[192,32,128]{2,1,0:T(8,128)(2,1)}) %all-gather.5.cloned.1.call-update) | async-done | bytes 1572880 | tf_op jit(solution)/shard_map/all_gather | solution.py:323
  85.6 1.8 constant_dynamic-slice_fusion
  87.4 0.0 all-gather.7.cloned.1.call-update
  88.7 0.0 copy-start
  88.7 2.2 copy-done
  90.9 0.0 copy-start.6
  90.9 0.0 copy-start.7
  90.9 0.0 copy-start.8
  90.9 0.0 copy-start.2
  90.9 0.0 copy-start.4
  90.9 0.0 copy-start.5
  90.9 14.6 %shard_map.123 = f32[32,128]{1,0:T(8,128)S(1)} custom-call(s32[2]{0:T(128)S(1)} %pad_add_fusion.3.at_ref, f32[16,64,64]{2,1,0:T(8,128)S(1)} %get-tuple-element.13.gram1_ref, f32[64,64,255]{2,1,0:T(8,128)S(1)} %bitcast.39), custom_call_target="tpu_custom_call" | custom-call | tf_op jit(solution)/shard_map/pallas_call | solution.py:177
  105.6 70.6 %all-gather.1 = f32[1024,128]{1,0:T(8,128)S(1)} all-gather(f32[32,128]{1,0:T(8,128)S(1)} %shard_map.123), channel_id=3, replica_groups=mesh['leaf'=8,'col'=4] {'leaf','col'}, dimensions={0}, use_global_device_ids=true | all-gather | bytes 540672 | tf_op jit(solution)/shard_map/all_gather | solution.py:343
  176.2 0.0 copy-done.6
  176.2 15.2 %shard_map.124 = (f32[1,3,64,64]{3,2,1,0:T(8,128)}, f32[64,64]{1,0:T(8,128)}) custom-call(s32[2]{0:T(128)S(1)} %pad_add_fusion.3.at_ref, f32[32,32,128]{2,1,0:T(8,128)S(1)} %bitcast.43, f32[6,64,64]{2,1,0:T(8,128)S(1)} %copy-done.6), custom_call_target="tpu_custom_call" | custom-call | tf_op jit(solution)/shard_map/pallas_call | solution.py:224
  191.4 0.1 pad_add_fusion.2.counts_ref
  191.5 0.0 copy-done.7
  191.5 0.0 copy-done.8
  191.6 0.0 copy-done.2
  191.6 0.0 copy-done.4
  191.6 0.0 copy-done.5
  191.6 24.6 %shard_map.121.left_ref = bf16[384,32,128]{2,1,0:T(8,128)(2,1)} custom-call(s32[384]{0:T(512)S(1)} %get-tuple-element.21.index_ref, bf16[192,32,128]{2,1,0:T(8,128)(2,1)S(1)} %copy-done.2, bf16[64,64,256]{2,1,0:T(8,128)(2,1)S(1)} %bitcast.42, bf16[64,64,128]{2,1,0:T(8,128)(2,1)S(1)} %bitcast.44), custom_call_target="tpu_custom_call" | custom-call | tf_op jit(solution)/shard_map/pallas_call | solution.py:267
  216.2 0.0 all-gather.7.cloned.1.call-done
  216.2 1.9 copy-done.1
  218.1 26.4 %shard_map.122 = (bf16[64,64,256]{2,1,0:T(8,128)(2,1)}, bf16[64,64,128]{2,1,0:T(8,128)(2,1)}) custom-call(s32[384]{0:T(512)S(1)} %get-tuple-element.20.index_ref, s32[2]{0:T(128)S(1)} %pad_add_fusion.2.counts_ref, bf16[384,32,128]{2,1,0:T(8,128)(2,1)S(1)} %bitcast.40, bf16[384,32,128]{2,1,0:T(8,128)(2,1)} %shard_map.121.left_ref), custom_call_target="tpu_custom_call" | custom-call | tf_op jit(solution)/shard_map/pallas_call | solution.py:302
  (6 shorter events, 0.1 us)
Async XLA Ops:
  7.2 78.4 %all-gather.5.cloned.1.call-start = ((), (), s32[]{:S(2)}) async-start(), calls=%async_computation | async-start | bytes 1966080 | tf_op jit(solution)/shard_map/all_gather | solution.py:323
  7.3 1.6 copy-start.3
  45.6 170.6 %all-gather.7.cloned.1.call-start = ((), (), s32[]{:S(2)}) async-start(), calls=%async_computation.1 | async-start | bytes 3538944 | tf_op jit(solution)/shard_map/all_gather | solution.py:329
  88.7 2.2 copy-start
  90.9 85.3 %copy-start.6 = (f32[6,64,64]{2,1,0:T(8,128)S(1)}, f32[6,64,64]{2,1,0:T(8,128)}, u32[]{:S(2)}) copy-start(f32[6,64,64]{2,1,0:T(8,128)} %top_ref.1) | copy-start | bytes 294916
  90.9 100.6 %copy-start.7 = (s32[256,2]{0,1:T(2,128)S(1)}, s32[256,2]{0,1:T(2,128)}, u32[]{:S(2)}) copy-start(s32[256,2]{0,1:T(2,128)} %param.13) | copy-start | bytes 6148
  90.9 100.7 %copy-start.8 = (s32[128,2]{0,1:T(2,128)S(1)}, s32[128,2]{0,1:T(2,128)}, u32[]{:S(2)}) copy-start(s32[128,2]{0,1:T(2,128)} %param.16) | copy-start | bytes 3076
  90.9 100.7 %copy-start.2 = (bf16[192,32,128]{2,1,0:T(8,128)(2,1)S(1)}, bf16[192,32,128]{2,1,0:T(8,128)(2,1)}, u32[]{:S(2)}) copy-start(bf16[192,32,128]{2,1,0:T(8,128)(2,1)} %all-gather.5.cloned.1.call-done.table_ref) | copy-start | bytes 4718596
  90.9 100.7 %copy-start.4 = (bf16[256,64,64]{0,2,1:T(8,128)(2,1)S(1)}, bf16[256,64,64]{0,2,1:T(8,128)(2,1)}, u32[]{:S(2)}) copy-start(bf16[256,64,64]{0,2,1:T(8,128)(2,1)} %param.12) | copy-start | bytes 6291460
  90.9 100.7 %copy-start.5 = (bf16[128,64,64]{0,2,1:T(8,128)(2,1)S(1)}, bf16[128,64,64]{0,2,1:T(8,128)(2,1)}, u32[]{:S(2)}) copy-start(bf16[128,64,64]{0,2,1:T(8,128)(2,1)} %param.15) | copy-start | bytes 3145732
  216.2 1.9 copy-start.1
Sparse Core Ops, SparseCore 0:
  45.8 39.7 all-gather.4
  88.0 31.6 all-gather.6

commit v2 on v1

v2 whole, which is shorter than its diff:
```python
import functools

import jax
import jax.numpy as jnp
from jax import lax
from jax.experimental import pallas as pl
from jax.experimental.pallas import tpu as pltpu
from jax.sharding import PartitionSpec as P

BF, F32 = jnp.bfloat16, jnp.float32
EXACT = lax.Precision.HIGHEST
NT = (((1,), (1,)), ((), ()))
NN = (((1,), (0,)), ((), ()))
K = 64
H = K // 2
LANES = 128
SMEM = pl.BlockSpec(memory_space=pltpu.SMEM)
VMEM = pl.BlockSpec(memory_space=pltpu.VMEM)
ANY = pl.BlockSpec(memory_space=pl.ANY)
TURN = 8
SLOTS = 64
PAIRS = 4
PARAMS = pltpu.CompilerParams(vmem_limit_bytes=48 * 2**20)


def unhalf(x):
    return jnp.concatenate([x[:, :K], x[:, K:]], axis=0)


def halve(x):
    return jnp.concatenate([x[:H], x[H:]], axis=1)


def mul(x, y, dims):
    return lax.dot_general(x, y, dims, precision=EXACT, preferred_element_type=F32)


def lift_all(grams, xfers_t):
    halfway = [mul(f, g, NN) for f, g in zip(xfers_t, grams)]
    return [mul(t, f, NT) for t, f in zip(halfway, xfers_t)]


def lift_pairs(grams, xfers_t):
    lifted = lift_all(grams, xfers_t)
    return [low + high for low, high in zip(lifted[0::2], lifted[1::2])]


def cost(flops, size):
    return pl.CostEstimate(flops=flops, bytes_accessed=size, transcendentals=0)


def unpack_transfers(xfer_ref, xt):
    @pl.loop(0, H // TURN)
    def _(step):
        at = [step * TURN + v for v in range(TURN)]
        turned = [jnp.concatenate([xfer_ref[:, q, :], xfer_ref[:, q + H, :]], axis=0).T for q in at]
        for q, y in zip(at, turned):
            xt[:, q, :] = y


def cholesky_lanes(a):
    sub = lax.broadcasted_iota(jnp.int32, (8, a.shape[2]), 0)

    def cols(block):
        return pl.ds(pl.multiple_of(8 * block, 8), 8)

    for panel in range(K // 8):
        base = 8 * panel
        scale = []
        rows = [a[base + k, pl.ds(base, 8), :] for k in range(8)]
        for k in range(8):
            scale.append(lax.rsqrt(rows[k][k : k + 1, :]))
            rows[k] = rows[k] * scale[k]
            for i in range(k + 1, 8):
                rows[i] = rows[i] - rows[k][i : i + 1, :] * rows[k]
        for k in range(8):
            a[base + k, pl.ds(base, 8), :] = jnp.where(sub >= k, rows[k], 0.0)
        for j in range(panel + 1, K // 8):
            new = []
            for k in range(8):
                acc = a[base + k, pl.ds(8 * j, 8), :]
                for p in range(k):
                    acc = acc - rows[p][k : k + 1, :] * new[p]
                new.append(acc * scale[k])
            for k in range(8):
                a[base + k, pl.ds(8 * j, 8), :] = new[k]
        if panel < K // 8 - 1:

            @pl.loop(panel + 1, K // 8)
            def _(i_block):
                left = [a[base + k, cols(i_block), :] for k in range(8)]

                @pl.loop(i_block, K // 8)
                def _(j_block):
                    right = [a[base + k, cols(j_block), :] for k in range(8)]
                    for i in range(8):
                        acc = a[8 * i_block + i, cols(j_block), :]
                        for k in range(8):
                            acc = acc - left[k][i : i + 1, :] * right[k]
                        a[8 * i_block + i, cols(j_block), :] = acc

    for i in range(8, K):
        a[i, pl.ds(0, i // 8 * 8), :] = jnp.zeros((i // 8 * 8, a.shape[2]), F32)


def factor_halved(s, a):
    @pl.loop(0, H // TURN)
    def _(step):
        at = [step * TURN + v for v in range(TURN)]
        turned = [s[:, q, :].T for q in at]
        for q, y in zip(at, turned):
            a[q] = y[:K]
            a[q + H] = y[K:]

    cholesky_lanes(a)

    @pl.loop(0, H // TURN)
    def _(step):
        at = [step * TURN + v for v in range(TURN)]
        turned = [jnp.concatenate([a[q], a[q + H]], axis=0).T for q in at]
        for q, y in zip(at, turned):
            s[:, q, :] = y


def factor_kernel(own, cols, at_ref, basis_ref, xfer_ref, fac_ref, sent_ref, gram1_ref, xt, s, a):
    col = at_ref[1]
    first = col * own
    unpack_transfers(xfer_ref, xt)

    pairs = min(PAIRS, own // 2)

    @pl.loop(0, own // 2 // pairs)
    def _(step):
        base = step * pairs
        at = [2 * base + c for c in range(2 * pairs)]
        points = [basis_ref[c] for c in at]
        grams = [mul(x, x, NT) for x in points]
        parents = lift_pairs(grams, [unhalf(xt[first + c]) for c in at])
        for c, gram in zip(at, grams):
            s[c] = halve(gram)
        for p, gram in enumerate(parents):
            gram1_ref[base + p] = gram
            s[own + base + p] = halve(gram)

    factor_halved(s, a)
    count = own + own // 2
    fac_ref[...] = s[0:count].astype(BF)
    for e in range(cols):
        for r in range(count // cols):
            sent_ref[e, r] = s[r * cols + jnp.bitwise_xor(col, e)].astype(BF)


def own_factors(at, basis, xfer_lanes, cols):
    own = basis.shape[0]
    count = own + own // 2
    rows = (count + 7) // 8 * 8
    shapes = (
        jax.ShapeDtypeStruct((count, H, 2 * K), BF),
        jax.ShapeDtypeStruct((cols, count // cols, H, 2 * K), BF),
        jax.ShapeDtypeStruct((own // 2, K, K), F32),
    )
    return pl.pallas_call(
        functools.partial(factor_kernel, own, cols),
        out_shape=shapes,
        grid=(1,),
        in_specs=[
            SMEM,
            pl.BlockSpec(basis.shape, lambda i: (0, 0, 0)),
            pl.BlockSpec((K, K, LANES), lambda i: (0, 0, 0)),
        ],
        out_specs=tuple(
            pl.BlockSpec(x.shape, lambda i, rank=len(x.shape): (0,) * rank) for x in shapes
        ),
        scratch_shapes=[
            pltpu.VMEM((LANES, H, 2 * K), F32),
            pltpu.VMEM((rows, H, 2 * K), F32),
            pltpu.VMEM((K, K, rows), F32),
        ],
        compiler_params=PARAMS,
        cost_estimate=cost(own * 2**24, 2**23),
    )(at, basis, xfer_lanes)


def chain_kernel(own, cols, at_ref, gram1_ref, xfer_ref, out_ref, xt):
    col = at_ref[1]
    unpack_transfers(xfer_ref, xt)
    grams = [gram1_ref[c] for c in range(own // 2)]
    offset = 0
    width = own * cols // 2
    while len(grams) > 1:
        here = len(grams)
        first = offset + col * here
        grams = lift_pairs(grams, [unhalf(xt[first + c]) for c in range(here)])
        offset += width
        width //= 2
    shift = 0
    while width >= 1:
        grams = lift_all(grams, [unhalf(xt[offset + jnp.right_shift(col, shift)])])
        offset += width
        width //= 2
        shift += 1
    out_ref[...] = halve(grams[0])


def lifted_root(at, gram1, xfer_lanes, own, cols):
    return pl.pallas_call(
        functools.partial(chain_kernel, own, cols),
        out_shape=jax.ShapeDtypeStruct((H, 2 * K), F32),
        grid=(1,),
        in_specs=[
            SMEM,
            pl.BlockSpec(gram1.shape, lambda i: (0, 0, 0)),
            pl.BlockSpec((K, K, LANES), lambda i: (0, 0, 1)),
        ],
        out_specs=pl.BlockSpec((H, 2 * K), lambda i: (0, 0)),
        scratch_shapes=[pltpu.VMEM((LANES, H, 2 * K), F32)],
        compiler_params=PARAMS,
        cost_estimate=cost(own * 2**24, 2**22),
    )(at, gram1, xfer_lanes)


def top_kernel(leaves, at_ref, top_ref, *refs):
    pairs = leaves // 2
    parts, (anc_ref, root_ref, level_ref, s, a) = refs[:pairs], refs[pairs:]
    pair = jnp.right_shift(at_ref[0], 1)
    for m in range(pairs):
        level_ref[jnp.bitwise_xor(pair, m)] = parts[m][...]
    level = [unhalf(level_ref[m]) for m in range(pairs)]
    heights = []
    slot = 0
    off_top = 0
    while True:
        heights.append(slot)
        for m, gram in enumerate(level):
            s[slot + m] = halve(gram)
        slot += len(level)
        if len(level) == 1:
            break
        level_xfers = [top_ref[off_top + m].T for m in range(len(level))]
        off_top += len(level)
        level = lift_pairs(level, level_xfers)
    factor_halved(s, a)
    for h, start in enumerate(heights):
        anc_ref[0, h] = unhalf(s[start + jnp.right_shift(at_ref[0], h + 1)])
    root_ref[...] = unhalf(s[heights[-1]])


def top_factors(at, parts, top_transfer, leaves):
    height = leaves.bit_length() - 1
    rows = (leaves - 1 + 7) // 8 * 8
    return pl.pallas_call(
        functools.partial(top_kernel, leaves),
        out_shape=(
            jax.ShapeDtypeStruct((1, height, K, K), F32),
            jax.ShapeDtypeStruct((K, K), F32),
        ),
        in_specs=[SMEM, VMEM] + [VMEM] * len(parts),
        out_specs=(VMEM, VMEM),
        scratch_shapes=[
            pltpu.VMEM((leaves // 2, H, 2 * K), F32),
            pltpu.VMEM((rows, H, 2 * K), F32),
            pltpu.VMEM((K, K, rows), F32),
        ],
        compiler_params=PARAMS,
        cost_estimate=cost(2**28, 2**20),
    )(at, top_transfer, *parts)


def lane_groups(sizes):
    return [(which, lane) for which, size in enumerate(sizes) for lane in range(0, size, LANES)]


def fill(table, pieces, sem):
    start = 0
    copies = []
    for n, piece in enumerate(pieces):
        copies.append(
            pltpu.make_async_copy(piece, table.at[pl.ds(start, piece.shape[0])], sem.at[n])
        )
        start += piece.shape[0]
    for copy in copies:
        copy.start()
    return copies


def left_kernel(groups, inputs, index_ref, *refs):
    blocks, pieces = refs[: inputs[0]], refs[inputs[0] : sum(inputs)]
    left_ref, bt, table, sem = refs[sum(inputs) :]
    copies = fill(table, pieces, sem)
    for g, (which, lane) in enumerate(groups):
        src = blocks[which]

        @pl.loop(0, H // TURN)
        def _(step):
            lanes = pl.ds(lane, LANES)
            at = [step * TURN + v for v in range(TURN)]
            x = [jnp.concatenate([src[q, :, lanes], src[q + H, :, lanes]], axis=0) for q in at]
            turned = [y.astype(F32).T for y in x]
            for q, y in zip(at, turned):
                bt[:, q, :] = y

        if g == 0:
            for copy in copies:
                copy.wait()

        @pl.loop(0, LANES // SLOTS)
        def _(step):
            at = [step * SLOTS + u for u in range(SLOTS)]
            rows = [unhalf(table[index_ref[LANES * g + b]]) for b in at]
            cells = [unhalf(bt[b].astype(BF)) for b in at]
            y = [lax.dot_general(r, c, NN, preferred_element_type=F32) for r, c in zip(rows, cells)]
            y = [halve(z.astype(BF)) for z in y]
            for b, z in zip(at, y):
                left_ref[LANES * g + b] = z


def left_products(pieces, index, blocks):
    groups = lane_groups([x.shape[2] for x in blocks])
    entries = sum(x.shape[0] for x in pieces)
    return pl.pallas_call(
        functools.partial(left_kernel, groups, (len(blocks), len(pieces))),
        out_shape=jax.ShapeDtypeStruct((LANES * len(groups), H, 2 * K), BF),
        in_specs=[SMEM] + [VMEM] * len(blocks) + [ANY] * len(pieces),
        out_specs=VMEM,
        scratch_shapes=[
            pltpu.VMEM((LANES, H, 2 * K), F32),
            pltpu.VMEM((entries, H, 2 * K), BF),
            pltpu.SemaphoreType.DMA((len(pieces),)),
        ],
        compiler_params=PARAMS,
        cost_estimate=cost(len(groups) * 2**31, 2**24),
    )(index, *blocks, *pieces)


def right_kernel(groups, outs, count, index_ref, counts_ref, left_ref, *refs):
    pieces, out_refs = refs[:count], refs[count : count + outs]
    pt, table, sem = refs[count + outs :]
    for copy in fill(table, pieces, sem):
        copy.wait()
    for g, (which, lane) in enumerate(groups):
        dst = out_refs[which]

        @pl.loop(0, LANES // SLOTS)
        def _(step):
            at = [step * SLOTS + u for u in range(SLOTS)]
            cols = [unhalf(table[index_ref[LANES * g + b]]) for b in at]
            left = [unhalf(left_ref[LANES * g + b]) for b in at]
            y = [lax.dot_general(x, c, NT, preferred_element_type=F32) for x, c in zip(left, cols)]
            y = [halve(z) for z in y]
            for b, z in zip(at, y):
                pt[b] = z

        keep = lax.broadcasted_iota(jnp.int32, (2 * K, LANES), 1) < counts_ref[which] - lane

        @pl.loop(0, H // TURN)
        def _(step):
            lanes = pl.ds(lane, LANES)
            at = [step * TURN + v for v in range(TURN)]
            turned = [pt[:, q, :].T for q in at]
            for q, y in zip(at, turned):
                y = jnp.where(keep, y, 0.0).astype(BF)
                dst[q, :, lanes] = y[:K]
                dst[q + H, :, lanes] = y[K:]


def right_products(pieces, index, counts, left, sizes):
    groups = lane_groups(sizes)
    entries = sum(x.shape[0] for x in pieces)
    return pl.pallas_call(
        functools.partial(right_kernel, groups, len(sizes), len(pieces)),
        out_shape=tuple(jax.ShapeDtypeStruct((K, K, size), BF) for size in sizes),
        in_specs=[SMEM, SMEM, VMEM] + [ANY] * len(pieces),
        out_specs=(VMEM,) * len(sizes),
        scratch_shapes=[
            pltpu.VMEM((LANES, H, 2 * K), F32),
            pltpu.VMEM((entries, H, 2 * K), BF),
            pltpu.SemaphoreType.DMA((len(pieces),)),
        ],
        compiler_params=PARAMS,
        cost_estimate=cost(len(groups) * 2**31, 2**24),
    )(index, counts, left, *pieces)


def swapped(x, axis, d):
    return lax.ppermute(x, axis, [(i, i ^ d) for i in range(lax.axis_size(axis))])


def on_device(basis, transfer, top_transfer, blocks0, pairs0, counts0, blocks1, pairs1, counts1):
    own = basis.shape[0]
    cols = lax.axis_size("col")
    leaves = lax.axis_size("leaf")
    leaf, col = lax.axis_index("leaf"), lax.axis_index("col")
    at = jnp.stack([leaf, col]).astype(jnp.int32)
    xfer_lanes = jnp.transpose(transfer, (1, 2, 0))
    lanes0, lanes1 = jnp.transpose(blocks0, (1, 2, 0)), jnp.transpose(blocks1, (1, 2, 0))
    count = own + own // 2
    parts = count // cols

    def indices(pairs, level):
        size = own >> level
        row = pairs[:, 0] - leaf * (size * cols)
        row = (row // size ^ col) * count + level * own + row % size
        owner = pairs[:, 1] // size
        away = owner // cols ^ leaf
        piece = (away & 1) * (leaves // 2) + (away >> 1)
        column = (piece * cols + (owner % cols ^ col)) * parts
        return row, column + level * (own // cols) + pairs[:, 1] % size // cols

    row0, column0 = indices(pairs0, 0)
    row1, column1 = indices(pairs1, 1)

    factors, sent, gram1 = own_factors(at, basis, xfer_lanes, cols)
    part = [sent[0]] + [swapped(sent[d], "col", d) for d in range(1, cols)]
    part = jnp.concatenate(part, axis=0)
    row_pieces = [factors] + [swapped(factors, "col", d) for d in range(1, cols)]
    same_core = [part] + [swapped(part, "leaf", d) for d in range(2, leaves, 2)]
    other_core = swapped(jnp.concatenate(same_core, axis=0), "leaf", 1)

    gram = lifted_root(at, gram1, xfer_lanes, own, cols)
    for bit in range(cols.bit_length() - 1):
        gram = gram + swapped(gram, "col", 1 << bit)
    gram = gram + swapped(gram, "leaf", 1)
    tops = [gram] + [swapped(gram, "leaf", d) for d in range(2, leaves, 2)]
    ancestors, root = top_factors(at, tops, top_transfer, leaves)

    left = left_products(row_pieces, jnp.concatenate([row0, row1]), (lanes0, lanes1))
    out0, out1 = right_products(
        same_core + [other_core],
        jnp.concatenate([column0, column1]),
        jnp.concatenate([counts0, counts1]),
        left,
        (blocks0.shape[0], blocks1.shape[0]),
    )
    return (jnp.transpose(out0, (2, 0, 1)), jnp.transpose(out1, (2, 0, 1)), root, ancestors)


def solution(mesh):
    in_specs = (
        P(("leaf", "col"), None, None),
        P("leaf", None, None),
        P(),
        P(("leaf", "col"), None, None),
        P(("leaf", "col"), None),
        P(("leaf", "col")),
        P(("leaf", "col"), None, None),
        P(("leaf", "col"), None),
        P(("leaf", "col")),
    )
    out_specs = (
        P(("leaf", "col"), None, None),
        P(("leaf", "col"), None, None),
        P(),
        P("leaf", None, None, None),
    )
    return jax.shard_map(
        on_device, mesh=mesh, in_specs=in_specs, out_specs=out_specs, check_vma=False
    )
```

time: 252 us -> 151 us (0.60)
  blocking collectives: 70.6 us -> 0 us
  Pallas kernels: 118 us -> 53.5 us
  waiting for transfers between devices: 39.9 us -> 66.8 us
  starting transfers between devices: 0.08 us -> 16.5 us
  between operations: 15.4 us -> 2.2 us
  local copies, waits for them, and re-layouts: 7.46 us -> 11.6 us
    all_gather x1 -> x0, blocking collectives: 70.6 us -> none  [on_device(): lifted_all = lax.all_gather(lifted, ('leaf', 'col'), axis=0)]
    ppermute x0 -> x16, waiting for transfers between devices: none -> 66.8 us  [swapped(): lax.ppermute(x, axis, [(i, i ^ d) for i in range(lax.axis_size(axis))])]
    pallas_call x4, Pallas kernels: 103 us -> 46.5 us  [the longest x1 15.2 us: own_factors(): pl.pallas_call(functools.partial(factor_kernel, own, cols), out_shape=sha...]
    all_gather x2 -> x0, waiting for transfers between devices: 39.9 us -> none  [the longest x1 39.9 us: on_device(): row_table = lax.all_gather(factors, 'col', axis=0, tiled=True)]
    ppermute x0 -> x16, starting transfers between devices: none -> 16.5 us  [swapped(): lax.ppermute(x, axis, [(i, i ^ d) for i in range(lax.axis_size(axis))])]
    pallas_call x1, Pallas kernels: 14.6 us -> 6.93 us  [lifted_root(): pl.pallas_call(functools.partial(chain_kernel, own, cols), out_shape=jax....]
    unnamed x18 -> x20, local copies, waits for them, and re-layouts: 5.69 us -> 10.8 us
  transfers between devices with their start and end apart: 2 -> 16, of which waited for: 1 -> 9; matrix products, arithmetic and copies ran while one was open for 0% -> 3% of each run, Pallas kernels for 22% -> 16%
where the time goes in v2:
time: 151 us
  waiting for transfers between devices  66.8 us (44%)
  Pallas kernels  53.5 us (35%)
  starting transfers between devices  16.5 us (11%)
  local copies, waits for them, and re-layouts  11.6 us (8%)
  between operations  2.2 us (1%)
    ppermute x16, waiting for transfers between devices, swapped(): lax.ppermute(x, axis, [(i, i ^ d) for i in range(lax.axis_size(axis))])  66.8 us
    ppermute x16, starting transfers between devices, swapped(): lax.ppermute(x, axis, [(i, i ^ d) for i in range(lax.axis_size(axis))])  16.5 us
    pallas_call x1, Pallas kernels, own_factors(): pl.pallas_call(functools.partial(factor_kernel, own, cols), out_shape=sha...  15.2 us
    pallas_call x1, Pallas kernels, right_products(): pl.pallas_call(functools.partial(right_kernel, groups, len(sizes), len(pi...  13.4 us
    unnamed x20, local copies, waits for them, and re-layouts  10.8 us
    pallas_call x1, Pallas kernels, left_products(): pl.pallas_call(functools.partial(left_kernel, groups, (len(blocks), len(p...  10.2 us
    pallas_call x1, Pallas kernels, top_factors(): pl.pallas_call(functools.partial(top_kernel, leaves), out_shape=(jax.Shap...  7.71 us
    pallas_call x1, Pallas kernels, lifted_root(): pl.pallas_call(functools.partial(chain_kernel, own, cols), out_shape=jax....  6.93 us
  transfers between devices with their start and end apart: 16, of which 9 were waited for; matrix products, arithmetic and copies ran while one was open for 3% of the time, Pallas kernels for 16%

profile of v2, /device:TPU:0, one launch (start us, length us, event | category | flops | bytes accessed | tf_op | source)
XLA Modules:
  0.0 150.9 jit_solution(15621617556176837051)
XLA Ops:
  0.7 1.6 %copy-done.1 = f32[32,64,256]{2,1,0:T(8,128)S(1)} copy-done((f32[32,64,256]{2,1,0:T(8,128)S(1)}, f32[32,64,256]{2,1,0:T(8,128)}, u32[]{:S(2)}) %copy-start.1) | copy-done | bytes 2097176
  2.3 15.2 %shard_map.120 = (bf16[48,32,128]{2,1,0:T(8,128)(2,1)}, bf16[4,12,32,128]{3,2,1,0:T(8,128)(2,1)S(1)}, f32[16,64,64]{2,1,0:T(8,128)S(1)}) custom-call(s32[2]{0:T(128)S(1)} %pad_add_fusion.3.at_ref, f32[32,64,256]{2,1,0:T(8,128)S(1)} %copy-done.1, f32[64,64,255]{2,1,0:T(8,128)} %bitcast.45), custom_call_target="tpu_custom_call" | custom-call | flops 536870912 | bytes 8388608 | tf_op jit(solution)/shard_map/pallas_call | solution.py:162
  17.5 5.0 %collective-permute-start.2 = (bf16[48,32,128]{2,1,0:T(8,128)(2,1)}, bf16[48,32,128]{2,1,0:T(8,128)(2,1)}, u32[]{:S(2)}, u32[]{:S(2)}) collective-permute-start(bf16[48,32,128]{2,1,0:T(8,128)(2,1)} %get-tuple-element.11.refs_2_), channel_id=1, source_target_pairs={{0,3},{1,2},{2,1},{3,0},{4,7},{5,6},{6,5},{7,4},{8,11},{9,10},{10,... | collective-permute-start | bytes 1179656 | tf_op jit(solution)/shard_map/ppermute | solution.py:385
  22.6 2.0 %collective-permute-start.5 = (bf16[12,32,128]{2,1,0:T(8,128)(2,1)S(1)}, bf16[12,32,128]{2,1,0:T(8,128)(2,1)S(1)}, u32[]{:S(2)}, u32[]{:S(2)}) collective-permute-start(bf16[12,32,128]{2,1,0:T(8,128)(2,1)S(1)} %get-tuple-element.19), channel_id=1, source_target_pairs={{0,3},{1,2},{2,1},{3,0},{4,7},{5,6},{6,5},{7,4},{8,11},{9,10},{10,... | collective-permute-start | bytes 294920 | tf_op jit(solution)/shard_map/ppermute | solution.py:385
  24.6 1.1 collective-permute-start.4
  25.7 1.4 collective-permute-start.3
  27.1 0.6 constant_dynamic-update-slice_fusion.6
  27.7 15.7 %collective-permute-done.5 = bf16[12,32,128]{2,1,0:T(8,128)(2,1)S(1)} collective-permute-done((bf16[12,32,128]{2,1,0:T(8,128)(2,1)S(1)}, bf16[12,32,128]{2,1,0:T(8,128)(2,1)S(1)}, u32[]{:S(2)}, u32[]{:S(2)}) %collective-permute-start.5) | collective-permute-done | bytes 98336 | tf_op jit(solution)/shard_map/ppermute | solution.py:385
  43.4 21.4 %collective-permute-done.4 = bf16[12,32,128]{2,1,0:T(8,128)(2,1)S(1)} collective-permute-done((bf16[12,32,128]{2,1,0:T(8,128)(2,1)S(1)}, bf16[12,32,128]{2,1,0:T(8,128)(2,1)S(1)}, u32[]{:S(2)}, u32[]{:S(2)}) %collective-permute-start.4) | collective-permute-done | bytes 98336 | tf_op jit(solution)/shard_map/ppermute | solution.py:385
  64.8 1.6 %collective-permute-start.6 = (bf16[48,32,128]{2,1,0:T(8,128)(2,1)S(1)}, bf16[48,32,128]{2,1,0:T(8,128)(2,1)S(1)}, u32[]{:S(2)}, u32[]{:S(2)}) collective-permute-start(bf16[48,32,128]{2,1,0:T(8,128)(2,1)S(1)} %pad_maximum_fusion.refs_0_), channel_id=1, source_target_pairs={{0,8},{4,12},{8,0},{12,4},{16,24},{20,28},{24,16},{28,20},{1,9},{5... | collective-permute-start | bytes 1179656 | tf_op jit(solution)/shard_map/ppermute | solution.py:385
  66.4 2.2 %copy-done = f32[255,64,64]{0,2,1:T(8,128)S(1)} copy-done((f32[255,64,64]{0,2,1:T(8,128)S(1)}, f32[255,64,64]{0,2,1:T(8,128)}, u32[]{:S(2)}) %copy-start) | copy-done | bytes 4177944
  68.6 6.9 %shard_map.123 = f32[32,128]{1,0:T(8,128)S(1)} custom-call(s32[2]{0:T(128)S(1)} %pad_add_fusion.3.at_ref, f32[16,64,64]{2,1,0:T(8,128)S(1)} %get-tuple-element.15.gram1_ref, f32[64,64,255]{2,1,0:T(8,128)S(1)} %bitcast.46), custom_call_target="tpu_custom_call" | custom-call | flops 536870912 | bytes 4194304 | tf_op jit(solution)/shard_map/pallas_call | solution.py:206
  75.6 1.6 %collective-permute-start.8 = (bf16[48,32,128]{2,1,0:T(8,128)(2,1)S(1)}, bf16[48,32,128]{2,1,0:T(8,128)(2,1)S(1)}, u32[]{:S(2)}, u32[]{:S(2)}) collective-permute-start(bf16[48,32,128]{2,1,0:T(8,128)(2,1)S(1)} %pad_maximum_fusion.refs_0_), channel_id=1, source_target_pairs={{0,24},{4,28},{8,16},{12,20},{16,8},{20,12},{24,0},{28,4},{1,25},{... | collective-permute-start | bytes 1179656 | tf_op jit(solution)/shard_map/ppermute | solution.py:385
  77.6 0.6 constant_dynamic-update-slice_fusion.5
  78.3 0.6 constant_dynamic-update-slice_fusion.4
  79.6 0.8 constant_dynamic-update-slice_fusion.2
  80.4 14.5 %collective-permute-done.7.refs_2_ = bf16[48,32,128]{2,1,0:T(8,128)(2,1)S(1)} collective-permute-done((bf16[48,32,128]{2,1,0:T(8,128)(2,1)S(1)}, bf16[48,32,128]{2,1,0:T(8,128)(2,1)S(1)}, u32[]{:S(2)}, u32[]{:S(2)}) %collective-permute-start.7) | collective-permute-done | bytes 393248 | tf_op jit(solution)/shard_map/ppermute | solution.py:385
  94.9 0.8 constant_dynamic-update-slice_fusion.1
  95.7 0.8 constant_dynamic-update-slice_fusion
  96.4 2.2 %collective-permute-done.10 = f32[32,128]{1,0:T(8,128)S(1)} collective-permute-done((f32[32,128]{1,0:T(8,128)S(1)}, f32[32,128]{1,0:T(8,128)S(1)}, u32[]{:S(2)}, u32[]{:S(2)}) %collective-permute-start.10) | collective-permute-done | bytes 16416 | tf_op jit(solution)/shard_map/ppermute | solution.py:385
  99.2 4.1 %collective-permute-done.11 = f32[32,128]{1,0:T(8,128)S(1)} collective-permute-done((f32[32,128]{1,0:T(8,128)S(1)}, f32[32,128]{1,0:T(8,128)S(1)}, u32[]{:S(2)}, u32[]{:S(2)}) %collective-permute-start.11) | collective-permute-done | bytes 16416 | tf_op jit(solution)/shard_map/ppermute | solution.py:385
  103.3 1.1 collective-permute-done.12
  104.4 1.5 collective-permute-start.15
  106.0 3.1 %collective-permute-done.15.refs_3_ = f32[32,128]{1,0:T(8,128)S(1)} collective-permute-done((f32[32,128]{1,0:T(8,128)S(1)}, f32[32,128]{1,0:T(8,128)S(1)}, u32[]{:S(2)}, u32[]{:S(2)}) %collective-permute-start.15) | collective-permute-done | bytes 16416 | tf_op jit(solution)/shard_map/ppermute | solution.py:385
  109.1 0.8 collective-permute-start.14
  111.2 1.6 %collective-permute-done.14.refs_2_ = f32[32,128]{1,0:T(8,128)S(1)} collective-permute-done((f32[32,128]{1,0:T(8,128)S(1)}, f32[32,128]{1,0:T(8,128)S(1)}, u32[]{:S(2)}, u32[]{:S(2)}) %collective-permute-start.14) | collective-permute-done | bytes 16416 | tf_op jit(solution)/shard_map/ppermute | solution.py:385
  113.4 3.1 %collective-permute-done.13.refs_1_ = f32[32,128]{1,0:T(8,128)S(1)} collective-permute-done((f32[32,128]{1,0:T(8,128)S(1)}, f32[32,128]{1,0:T(8,128)S(1)}, u32[]{:S(2)}, u32[]{:S(2)}) %collective-permute-start.13) | collective-permute-done | bytes 16416 | tf_op jit(solution)/shard_map/ppermute | solution.py:385
  116.6 7.7 %shard_map.124 = (f32[1,3,64,64]{3,2,1,0:T(8,128)}, f32[64,64]{1,0:T(8,128)}) custom-call(s32[2]{0:T(128)S(1)} %pad_add_fusion.3.at_ref, f32[6,64,64]{2,1,0:T(8,128)S(1)} %copy-done.4, f32[32,128]{1,0:T(8,128)S(1)} %add.101.refs_0_, f32[32,128]{1,0:T(8,128)S(1)} %collective-permute-done.13.refs_1_, f32[32,128]{1,0:T(8,128)S(1)} %collective-permute-done.14.refs_2_, ...), custom_call_target="tpu_custom_call" | custom-call | flops 268435456 | bytes 1048576 | tf_op jit(solution)/shard_map/pallas_call | solution.py:251
  124.3 1.6 %copy-done.2 = bf16[256,64,64]{0,2,1:T(8,128)(2,1)S(1)} copy-done((bf16[256,64,64]{0,2,1:T(8,128)(2,1)S(1)}, bf16[256,64,64]{0,2,1:T(8,128)(2,1)}, u32[]{:S(2)}) %copy-start.2) | copy-done | bytes 2097176
  125.9 1.2 copy-done.3
  127.1 10.2 %shard_map.121.left_ref = bf16[384,32,128]{2,1,0:T(8,128)(2,1)} custom-call(s32[384]{0:T(512)S(1)} %get-tuple-element.27.index_ref, bf16[64,64,256]{2,1,0:T(8,128)(2,1)S(1)} %bitcast.47, bf16[64,64,128]{2,1,0:T(8,128)(2,1)S(1)} %bitcast.48, bf16[48,32,128]{2,1,0:T(8,128)(2,1)} %get-tuple-element.11.refs_2_, ...), custom_call_target="tpu_custom_call" | custom-call | flops 6442450944 | bytes 16777216 | tf_op jit(solution)/shard_map/pallas_call | solution.py:320
  137.3 13.4 %shard_map.122 = (bf16[64,64,256]{2,1,0:T(8,128)(2,1)}, bf16[64,64,128]{2,1,0:T(8,128)(2,1)}) custom-call(s32[384]{0:T(512)S(1)} %get-tuple-element.26.index_ref, s32[2]{0:T(128)S(1)} %pad_add_fusion.2.counts_ref, bf16[384,32,128]{2,1,0:T(8,128)(2,1)} %shard_map.121.left_ref, bf16[48,32,128]{2,1,0:T(8,128)(2,1)S(1)} %pad_maximum_fusion.refs_0_, ...), custom_call_target="tpu_custom_call" | custom-call | flops 6442450944 | bytes 16777216 | tf_op jit(solution)/shard_map/pallas_call | solution.py:369
  (38 shorter events, 2.6 us)
Async XLA Ops:
  0.7 1.6 %copy-start.1 = (f32[32,64,256]{2,1,0:T(8,128)S(1)}, f32[32,64,256]{2,1,0:T(8,128)}, u32[]{:S(2)}) copy-start(f32[32,64,256]{2,1,0:T(8,128)} %basis_ref.1) | copy-start | bytes 6291460
  17.5 106.7 %collective-permute-start.2 = (bf16[48,32,128]{2,1,0:T(8,128)(2,1)}, bf16[48,32,128]{2,1,0:T(8,128)(2,1)}, u32[]{:S(2)}, u32[]{:S(2)}) collective-permute-start(bf16[48,32,128]{2,1,0:T(8,128)(2,1)} %get-tuple-element.11.refs_2_), channel_id=1, source_target_pairs={{0,3},{1,2},{2,1},{3,0},{4,7},{5,6},{6,5},{7,4},{8,11},{9,10},{10,... | collective-permute-start | bytes 1179656 | tf_op jit(solution)/shard_map/ppermute | solution.py:385
  22.6 101.7 %collective-permute-start.1 = (bf16[48,32,128]{2,1,0:T(8,128)(2,1)}, bf16[48,32,128]{2,1,0:T(8,128)(2,1)}, u32[]{:S(2)}, u32[]{:S(2)}) collective-permute-start(bf16[48,32,128]{2,1,0:T(8,128)(2,1)} %get-tuple-element.11.refs_2_), channel_id=1, source_target_pairs={{0,2},{1,3},{2,0},{3,1},{4,6},{5,7},{6,4},{7,5},{8,10},{9,11},{10,... | collective-permute-start | bytes 1179656 | tf_op jit(solution)/shard_map/ppermute | solution.py:385
  22.6 20.8 %collective-permute-start.5 = (bf16[12,32,128]{2,1,0:T(8,128)(2,1)S(1)}, bf16[12,32,128]{2,1,0:T(8,128)(2,1)S(1)}, u32[]{:S(2)}, u32[]{:S(2)}) collective-permute-start(bf16[12,32,128]{2,1,0:T(8,128)(2,1)S(1)} %get-tuple-element.19), channel_id=1, source_target_pairs={{0,3},{1,2},{2,1},{3,0},{4,7},{5,6},{6,5},{7,4},{8,11},{9,10},{10,... | collective-permute-start | bytes 294920 | tf_op jit(solution)/shard_map/ppermute | solution.py:385
  24.6 40.2 %collective-permute-start.4 = (bf16[12,32,128]{2,1,0:T(8,128)(2,1)S(1)}, bf16[12,32,128]{2,1,0:T(8,128)(2,1)S(1)}, u32[]{:S(2)}, u32[]{:S(2)}) collective-permute-start(bf16[12,32,128]{2,1,0:T(8,128)(2,1)S(1)} %get-tuple-element.20), channel_id=1, source_target_pairs={{0,2},{1,3},{2,0},{3,1},{4,6},{5,7},{6,4},{7,5},{8,10},{9,11},{10,... | collective-permute-start | bytes 294920 | tf_op jit(solution)/shard_map/ppermute | solution.py:385
  25.7 39.1 %collective-permute-start.3 = (bf16[12,32,128]{2,1,0:T(8,128)(2,1)S(1)}, bf16[12,32,128]{2,1,0:T(8,128)(2,1)S(1)}, u32[]{:S(2)}, u32[]{:S(2)}) collective-permute-start(bf16[12,32,128]{2,1,0:T(8,128)(2,1)S(1)} %get-tuple-element.21), channel_id=1, source_target_pairs={{0,1},{1,0},{2,3},{3,2},{4,5},{5,4},{6,7},{7,6},{8,9},{9,8},{10,11... | collective-permute-start | bytes 294920 | tf_op jit(solution)/shard_map/ppermute | solution.py:385
  64.8 14.8 %collective-permute-start.6 = (bf16[48,32,128]{2,1,0:T(8,128)(2,1)S(1)}, bf16[48,32,128]{2,1,0:T(8,128)(2,1)S(1)}, u32[]{:S(2)}, u32[]{:S(2)}) collective-permute-start(bf16[48,32,128]{2,1,0:T(8,128)(2,1)S(1)} %pad_maximum_fusion.refs_0_), channel_id=1, source_target_pairs={{0,8},{4,12},{8,0},{12,4},{16,24},{20,28},{24,16},{28,20},{1,9},{5... | collective-permute-start | bytes 1179656 | tf_op jit(solution)/shard_map/ppermute | solution.py:385
  66.4 2.2 %copy-start = (f32[255,64,64]{0,2,1:T(8,128)S(1)}, f32[255,64,64]{0,2,1:T(8,128)}, u32[]{:S(2)}) copy-start(f32[255,64,64]{0,2,1:T(8,128)} %param.10) | copy-start | bytes 12533764
  75.5 20.9 %copy-start.5 = (s32[256,2]{0,1:T(2,128)S(1)}, s32[256,2]{0,1:T(2,128)}, u32[]{:S(2)}) copy-start(s32[256,2]{0,1:T(2,128)} %param.13) | copy-start | bytes 6148
  75.5 30.4 %copy-start.6 = (s32[128,2]{0,1:T(2,128)S(1)}, s32[128,2]{0,1:T(2,128)}, u32[]{:S(2)}) copy-start(s32[128,2]{0,1:T(2,128)} %param.16) | copy-start | bytes 3076
  75.5 41.0 %copy-start.4 = (f32[6,64,64]{2,1,0:T(8,128)S(1)}, f32[6,64,64]{2,1,0:T(8,128)}, u32[]{:S(2)}) copy-start(f32[6,64,64]{2,1,0:T(8,128)} %top_ref.1) | copy-start | bytes 294916
  75.6 20.1 %collective-permute-start.8 = (bf16[48,32,128]{2,1,0:T(8,128)(2,1)S(1)}, bf16[48,32,128]{2,1,0:T(8,128)(2,1)S(1)}, u32[]{:S(2)}, u32[]{:S(2)}) collective-permute-start(bf16[48,32,128]{2,1,0:T(8,128)(2,1)S(1)} %pad_maximum_fusion.refs_0_), channel_id=1, source_target_pairs={{0,24},{4,28},{8,16},{12,20},{16,8},{20,12},{24,0},{28,4},{1,25},{... | collective-permute-start | bytes 1179656 | tf_op jit(solution)/shard_map/ppermute | solution.py:385
  77.1 17.7 %collective-permute-start.7 = (bf16[48,32,128]{2,1,0:T(8,128)(2,1)S(1)}, bf16[48,32,128]{2,1,0:T(8,128)(2,1)S(1)}, u32[]{:S(2)}, u32[]{:S(2)}) collective-permute-start(bf16[48,32,128]{2,1,0:T(8,128)(2,1)S(1)} %pad_maximum_fusion.refs_0_), channel_id=1, source_target_pairs={{0,16},{4,20},{8,24},{12,28},{16,0},{20,4},{24,8},{28,12},{1,17},{... | collective-permute-start | bytes 1179656 | tf_op jit(solution)/shard_map/ppermute | solution.py:385
  79.6 44.7 %collective-permute-start = (bf16[48,32,128]{2,1,0:T(8,128)(2,1)}, bf16[48,32,128]{2,1,0:T(8,128)(2,1)}, u32[]{:S(2)}, u32[]{:S(2)}) collective-permute-start(bf16[48,32,128]{2,1,0:T(8,128)(2,1)} %get-tuple-element.11.refs_2_), channel_id=1, source_target_pairs={{0,1},{1,0},{2,3},{3,2},{4,5},{5,4},{6,7},{7,6},{8,9},{9,8},{10,11... | collective-permute-start | bytes 1179656 | tf_op jit(solution)/shard_map/ppermute | solution.py:385
  94.9 3.7 %collective-permute-start.10 = (f32[32,128]{1,0:T(8,128)S(1)}, f32[32,128]{1,0:T(8,128)S(1)}, u32[]{:S(2)}, u32[]{:S(2)}) collective-permute-start(f32[32,128]{1,0:T(8,128)S(1)} %shard_map.123), channel_id=1, source_target_pairs={{0,1},{1,0},{2,3},{3,2},{4,5},{5,4},{6,7},{7,6},{8,9},{9,8},{10,11... | collective-permute-start | bytes 49160 | tf_op jit(solution)/shard_map/ppermute | solution.py:385
  96.4 40.9 %collective-permute-start.9 = (bf16[192,32,128]{2,1,0:T(8,128)(2,1)}, bf16[192,32,128]{2,1,0:T(8,128)(2,1)S(1)}, u32[]{:S(2)}, u32[]{:S(2)}) collective-permute-start(bf16[192,32,128]{2,1,0:T(8,128)(2,1)} %constant_dynamic-update-slice_fusion), channel_id=1, source_target_pairs={{0,4},{4,0},{8,12},{12,8},{16,20},{20,16},{24,28},{28,24},{1,5},{5... | collective-permute-start | bytes 4718600 | tf_op jit(solution)/shard_map/ppermute | solution.py:385
  98.6 4.6 %collective-permute-start.11 = (f32[32,128]{1,0:T(8,128)S(1)}, f32[32,128]{1,0:T(8,128)S(1)}, u32[]{:S(2)}, u32[]{:S(2)}) collective-permute-start(f32[32,128]{1,0:T(8,128)S(1)} %add.99), channel_id=1, source_target_pairs={{0,2},{1,3},{2,0},{3,1},{4,6},{5,7},{6,4},{7,5},{8,10},{9,11},{10,... | collective-permute-start | bytes 49160 | tf_op jit(solution)/shard_map/ppermute | solution.py:385
  103.3 1.2 collective-permute-start.12
  104.4 4.6 %collective-permute-start.15 = (f32[32,128]{1,0:T(8,128)S(1)}, f32[32,128]{1,0:T(8,128)S(1)}, u32[]{:S(2)}, u32[]{:S(2)}) collective-permute-start(f32[32,128]{1,0:T(8,128)S(1)} %add.101.refs_0_), channel_id=1, source_target_pairs={{0,24},{4,28},{8,16},{12,20},{16,8},{20,12},{24,0},{28,4},{1,25},{... | collective-permute-start | bytes 49160 | tf_op jit(solution)/shard_map/ppermute | solution.py:385
  109.1 3.7 %collective-permute-start.14 = (f32[32,128]{1,0:T(8,128)S(1)}, f32[32,128]{1,0:T(8,128)S(1)}, u32[]{:S(2)}, u32[]{:S(2)}) collective-permute-start(f32[32,128]{1,0:T(8,128)S(1)} %add.101.refs_0_), channel_id=1, source_target_pairs={{0,16},{4,20},{8,24},{12,28},{16,0},{20,4},{24,8},{28,12},{1,17},{... | collective-permute-start | bytes 49160 | tf_op jit(solution)/shard_map/ppermute | solution.py:385
  112.8 3.7 %collective-permute-start.13 = (f32[32,128]{1,0:T(8,128)S(1)}, f32[32,128]{1,0:T(8,128)S(1)}, u32[]{:S(2)}, u32[]{:S(2)}) collective-permute-start(f32[32,128]{1,0:T(8,128)S(1)} %add.101.refs_0_), channel_id=1, source_target_pairs={{0,8},{4,12},{8,0},{12,4},{16,24},{20,28},{24,16},{28,20},{1,9},{5... | collective-permute-start | bytes 49160 | tf_op jit(solution)/shard_map/ppermute | solution.py:385
  124.3 1.6 %copy-start.2 = (bf16[256,64,64]{0,2,1:T(8,128)(2,1)S(1)}, bf16[256,64,64]{0,2,1:T(8,128)(2,1)}, u32[]{:S(2)}) copy-start(bf16[256,64,64]{0,2,1:T(8,128)(2,1)} %param.12) | copy-start | bytes 6291460
  125.9 1.2 copy-start.3

commit v3 on v2

--- a/solution.py
+++ b/solution.py
@@ -13,6 +13,7 @@
 NN = (((1,), (0,)), ((), ()))
 K = 64
 H = K // 2
+Q = K // 4
 LANES = 128
 SMEM = pl.BlockSpec(memory_space=pltpu.SMEM)
 VMEM = pl.BlockSpec(memory_space=pltpu.VMEM)
@@ -122,6 +123,43 @@
             s[:, q, :] = y
 
 
+def lane(low, high):
+    at = lax.broadcasted_iota(jnp.int32, (Q, 2 * K), 1)
+    return (at >= low) & (at < high)
+
+
+def pack(four):
+    top = [x[:Q] for x in four]
+    low = [jnp.where(lane(0, Q), pltpu.roll(x[Q:], Q, 1), x[Q:]) for x in four]
+    gap = lane(K, K + H)
+    return jnp.concatenate(
+        [
+            jnp.where(gap, pltpu.roll(top[3], K, 1), top[0]),
+            jnp.where(gap, pltpu.roll(top[3], H, 1), top[1]),
+            jnp.where(gap, pltpu.roll(top[3], 2 * K - H, 1), top[2]),
+            jnp.where(lane(0, K), low[0], pltpu.roll(low[1], K, 1)),
+            jnp.where(lane(0, K), low[2], pltpu.roll(low[3], K, 1)),
+        ],
+        axis=0,
+    )
+
+
+def unpack(x):
+    unit = [x[Q * n : Q * (n + 1)] for n in range(5)]
+    full = []
+    for m in range(3):
+        full.append((unit[m], jnp.where(lane(H, K), pltpu.roll(unit[m], K, 1), 0.0)))
+    first = jnp.where(lane(0, H), pltpu.roll(unit[0], K, 1), pltpu.roll(unit[1], 2 * K - H, 1))
+    full.append((first, jnp.where(lane(H, K), pltpu.roll(unit[2], 2 * K - H, 1), 0.0)))
+    out = []
+    for m, (block0, block2) in enumerate(full):
+        low = unit[3 + m // 2] if m % 2 == 0 else pltpu.roll(unit[3 + m // 2], K, 1)
+        block1 = jnp.where(lane(Q, K), low, 0.0)
+        block3 = jnp.where(lane(K - Q, K), pltpu.roll(low, K - Q, 1), 0.0)
+        out.append(jnp.concatenate([block0, block1, block2, block3], axis=0)[:, :K])
+    return out
+
+
 def factor_kernel(own, cols, at_ref, basis_ref, xfer_ref, fac_ref, sent_ref, gram1_ref, xt, s, a):
     col = at_ref[1]
     first = col * own
@@ -144,7 +182,8 @@
 
     factor_halved(s, a)
     count = own + own // 2
-    fac_ref[...] = s[0:count].astype(BF)
+    for g in range(count // 4):
+        fac_ref[g] = pack([s[4 * g + m] for m in range(4)]).astype(BF)
     for e in range(cols):
         for r in range(count // cols):
             sent_ref[e, r] = s[r * cols + jnp.bitwise_xor(col, e)].astype(BF)
@@ -155,7 +194,7 @@
     count = own + own // 2
     rows = (count + 7) // 8 * 8
     shapes = (
-        jax.ShapeDtypeStruct((count, H, 2 * K), BF),
+        jax.ShapeDtypeStruct((count // 4, 5 * Q, 2 * K), BF),
         jax.ShapeDtypeStruct((cols, count // cols, H, 2 * K), BF),
         jax.ShapeDtypeStruct((own // 2, K, K), F32),
     )
@@ -262,7 +301,7 @@
             pltpu.VMEM((K, K, rows), F32),
         ],
         compiler_params=PARAMS,
-        cost_estimate=cost(2**28, 2**20),
+        cost_estimate=cost(2**22, 2**17),
     )(at, top_transfer, *parts)
 
 
@@ -270,115 +309,126 @@
     return [(which, lane) for which, size in enumerate(sizes) for lane in range(0, size, LANES)]
 
 
-def fill(table, pieces, sem):
-    start = 0
-    copies = []
-    for n, piece in enumerate(pieces):
-        copies.append(
-            pltpu.make_async_copy(piece, table.at[pl.ds(start, piece.shape[0])], sem.at[n])
-        )
-        start += piece.shape[0]
-    for copy in copies:
-        copy.start()
-    return copies
-
-
-def left_kernel(groups, inputs, index_ref, *refs):
-    blocks, pieces = refs[: inputs[0]], refs[inputs[0] : sum(inputs)]
-    left_ref, bt, table, sem = refs[sum(inputs) :]
-    copies = fill(table, pieces, sem)
-    for g, (which, lane) in enumerate(groups):
+def turn_kernel(groups, *refs):
+    blocks, cells_ref, bt = refs[:-2], refs[-2], refs[-1]
+    for g, (which, first) in enumerate(groups):
         src = blocks[which]
 
         @pl.loop(0, H // TURN)
         def _(step):
-            lanes = pl.ds(lane, LANES)
+            lanes = pl.ds(first, LANES)
             at = [step * TURN + v for v in range(TURN)]
             x = [jnp.concatenate([src[q, :, lanes], src[q + H, :, lanes]], axis=0) for q in at]
             turned = [y.astype(F32).T for y in x]
             for q, y in zip(at, turned):
                 bt[:, q, :] = y
 
-        if g == 0:
-            for copy in copies:
-                copy.wait()
+        cells_ref[pl.ds(LANES * g, LANES)] = bt[...].astype(BF)
+
+
+def turned_blocks(blocks):
+    groups = lane_groups([x.shape[2] for x in blocks])
+    return pl.pallas_call(
+        functools.partial(turn_kernel, groups),
+        out_shape=jax.ShapeDtypeStruct((LANES * len(groups), H, 2 * K), BF),
+        in_specs=[VMEM] * len(blocks),
+        out_specs=VMEM,
+        scratch_shapes=[pltpu.VMEM((LANES, H, 2 * K), F32)],
+        compiler_params=PARAMS,
+        cost_estimate=cost(2**20, 2**20),
+    )(*blocks)
+
+
+def middle_kernel(index_ref, cells_ref, same_ref, other_ref, out_ref):
+    entries = same_ref.shape[0]
+
+    @pl.loop(0, cells_ref.shape[0] // SLOTS)
+    def _(step):
+        at = [step * SLOTS + u for u in range(SLOTS)]
+        cols = []
+        for b in at:
+            n = index_ref[b]
+            there = n >= entries
+            n = jnp.where(there, n - entries, n)
+            cols.append(unhalf(jnp.where(there, other_ref[n], same_ref[n])))
+        cells = [unhalf(cells_ref[b]) for b in at]
+        y = [lax.dot_general(x, c, NT, preferred_element_type=F32) for x, c in zip(cells, cols)]
+        y = [halve(z.astype(BF)) for z in y]
+        for b, z in zip(at, y):
+            out_ref[b] = z
+
+
+def middle_products(index, cells, same_core, other_core):
+    return pl.pallas_call(
+        middle_kernel,
+        out_shape=jax.ShapeDtypeStruct(cells.shape, BF),
+        in_specs=[SMEM] + [VMEM] * 3,
+        out_specs=VMEM,
+        compiler_params=PARAMS,
+        cost_estimate=cost(cells.shape[0] * 2**19, 2**20),
+    )(index, cells, same_core, other_core)
+
+
+def outer_kernel(groups, outs, index_ref, counts_ref, middle_ref, *refs):
+    pieces, out_refs = refs[:-outs - 4], refs[-outs - 4 : -4]
+    pt, table, ready, sem = refs[-4:]
+    packs = pieces[0].shape[0]
+    for e, piece in enumerate(pieces):
+
+        @pl.loop(0, packs)
+        def _(g):
+            four = unpack(piece[g].astype(F32))
+            for m in range(4):
+                table[4 * (e * packs + g) + m] = four[m].astype(BF)
+
+    copies = []
+    for g, (which, first) in enumerate(groups):
 
         @pl.loop(0, LANES // SLOTS)
         def _(step):
             at = [step * SLOTS + u for u in range(SLOTS)]
-            rows = [unhalf(table[index_ref[LANES * g + b]]) for b in at]
-            cells = [unhalf(bt[b].astype(BF)) for b in at]
-            y = [lax.dot_general(r, c, NN, preferred_element_type=F32) for r, c in zip(rows, cells)]
-            y = [halve(z.astype(BF)) for z in y]
-            for b, z in zip(at, y):
-                left_ref[LANES * g + b] = z
-
-
-def left_products(pieces, index, blocks):
-    groups = lane_groups([x.shape[2] for x in blocks])
-    entries = sum(x.shape[0] for x in pieces)
-    return pl.pallas_call(
-        functools.partial(left_kernel, groups, (len(blocks), len(pieces))),
-        out_shape=jax.ShapeDtypeStruct((LANES * len(groups), H, 2 * K), BF),
-        in_specs=[SMEM] + [VMEM] * len(blocks) + [ANY] * len(pieces),
-        out_specs=VMEM,
-        scratch_shapes=[
-            pltpu.VMEM((LANES, H, 2 * K), F32),
-            pltpu.VMEM((entries, H, 2 * K), BF),
-            pltpu.SemaphoreType.DMA((len(pieces),)),
-        ],
-        compiler_params=PARAMS,
-        cost_estimate=cost(len(groups) * 2**31, 2**24),
-    )(index, *blocks, *pieces)
-
-
-def right_kernel(groups, outs, count, index_ref, counts_ref, left_ref, *refs):
-    pieces, out_refs = refs[:count], refs[count : count + outs]
-    pt, table, sem = refs[count + outs :]
-    for copy in fill(table, pieces, sem):
-        copy.wait()
-    for g, (which, lane) in enumerate(groups):
-        dst = out_refs[which]
-
-        @pl.loop(0, LANES // SLOTS)
-        def _(step):
-            at = [step * SLOTS + u for u in range(SLOTS)]
-            cols = [unhalf(table[index_ref[LANES * g + b]]) for b in at]
-            left = [unhalf(left_ref[LANES * g + b]) for b in at]
-            y = [lax.dot_general(x, c, NT, preferred_element_type=F32) for x, c in zip(left, cols)]
+            rows = [table[index_ref[LANES * g + b]] for b in at]
+            right = [unhalf(middle_ref[LANES * g + b]) for b in at]
+            y = [lax.dot_general(r, x, NN, preferred_element_type=F32) for r, x in zip(rows, right)]
             y = [halve(z) for z in y]
             for b, z in zip(at, y):
                 pt[b] = z
 
-        keep = lax.broadcasted_iota(jnp.int32, (2 * K, LANES), 1) < counts_ref[which] - lane
+        keep = lax.broadcasted_iota(jnp.int32, (2 * K, LANES), 1) < counts_ref[which] - first
 
         @pl.loop(0, H // TURN)
         def _(step):
-            lanes = pl.ds(lane, LANES)
             at = [step * TURN + v for v in range(TURN)]
             turned = [pt[:, q, :].T for q in at]
             for q, y in zip(at, turned):
                 y = jnp.where(keep, y, 0.0).astype(BF)
-                dst[q, :, lanes] = y[:K]
-                dst[q + H, :, lanes] = y[K:]
-
-
-def right_products(pieces, index, counts, left, sizes):
+                ready[g, q] = y[:K]
+                ready[g, q + H] = y[K:]
+
+        out = out_refs[which].at[:, :, pl.ds(first, LANES)]
+        copies.append(pltpu.make_async_copy(ready.at[g], out, sem.at[g]))
+        copies[-1].start()
+    for copy in copies:
+        copy.wait()
+
+
+def outer_products(pieces, index, counts, middle, sizes):
     groups = lane_groups(sizes)
-    entries = sum(x.shape[0] for x in pieces)
+    entries = 4 * sum(x.shape[0] for x in pieces)
     return pl.pallas_call(
-        functools.partial(right_kernel, groups, len(sizes), len(pieces)),
+        functools.partial(outer_kernel, groups, len(sizes)),
         out_shape=tuple(jax.ShapeDtypeStruct((K, K, size), BF) for size in sizes),
-        in_specs=[SMEM, SMEM, VMEM] + [ANY] * len(pieces),
-        out_specs=(VMEM,) * len(sizes),
+        in_specs=[SMEM, SMEM, VMEM] + [VMEM] * len(pieces),
+        out_specs=(ANY,) * len(sizes),
         scratch_shapes=[
             pltpu.VMEM((LANES, H, 2 * K), F32),
-            pltpu.VMEM((entries, H, 2 * K), BF),
-            pltpu.SemaphoreType.DMA((len(pieces),)),
+            pltpu.VMEM((entries, K, K), BF),
+            pltpu.VMEM((len(groups), K, K, LANES), BF),
+            pltpu.SemaphoreType.DMA((len(groups),)),
         ],
         compiler_params=PARAMS,
-        cost_estimate=cost(len(groups) * 2**31, 2**24),
-    )(index, counts, left, *pieces)
+        cost_estimate=cost(len(groups) * 2**26, 2**22),
+    )(index, counts, middle, *pieces)
 
 
 def swapped(x, axis, d):
@@ -410,25 +460,31 @@
     row1, column1 = indices(pairs1, 1)
 
     factors, sent, gram1 = own_factors(at, basis, xfer_lanes, cols)
-    part = [sent[0]] + [swapped(sent[d], "col", d) for d in range(1, cols)]
-    part = jnp.concatenate(part, axis=0)
-    row_pieces = [factors] + [swapped(factors, "col", d) for d in range(1, cols)]
-    same_core = [part] + [swapped(part, "leaf", d) for d in range(2, leaves, 2)]
-    other_core = swapped(jnp.concatenate(same_core, axis=0), "leaf", 1)
-
+    received = [swapped(sent[d], "col", d) for d in range(1, cols)]
     gram = lifted_root(at, gram1, xfer_lanes, own, cols)
+    cells = turned_blocks((lanes0, lanes1))
+    received, gram, factors, cells = lax.optimization_barrier((received, gram, factors, cells))
+
+    part = jnp.concatenate([sent[0]] + received, axis=0)
+    chips = [swapped(part, "leaf", d) for d in range(2, leaves, 2)]
+    row_pieces = [factors] + [swapped(factors, "col", d) for d in range(1, cols - 1)]
     for bit in range(cols.bit_length() - 1):
         gram = gram + swapped(gram, "col", 1 << bit)
     gram = gram + swapped(gram, "leaf", 1)
+    chips, row_pieces, gram = lax.optimization_barrier((chips, row_pieces, gram))
+
+    row_pieces = row_pieces + [swapped(factors, "col", cols - 1)]
+    same_core = jnp.concatenate([part] + chips, axis=0)
+    other_core = swapped(same_core, "leaf", 1)
     tops = [gram] + [swapped(gram, "leaf", d) for d in range(2, leaves, 2)]
     ancestors, root = top_factors(at, tops, top_transfer, leaves)
 
-    left = left_products(row_pieces, jnp.concatenate([row0, row1]), (lanes0, lanes1))
-    out0, out1 = right_products(
-        same_core + [other_core],
-        jnp.concatenate([column0, column1]),
+    middle = middle_products(jnp.concatenate([column0, column1]), cells, same_core, other_core)
+    out0, out1 = outer_products(
+        row_pieces,
+        jnp.concatenate([row0, row1]),
         jnp.concatenate([counts0, counts1]),
-        left,
+        middle,
         (blocks0.shape[0], blocks1.shape[0]),
     )
     return (jnp.transpose(out0, (2, 0, 1)), jnp.transpose(out1, (2, 0, 1)), root, ancestors)

time: 151 us -> 110 us (0.73)
  waiting for transfers between devices: 66.8 us -> 20.2 us
  Pallas kernels: 53.5 us -> 60.5 us
  local copies, waits for them, and re-layouts: 11.6 us -> 5.22 us
  starting transfers between devices: 16.5 us -> 20.9 us
    ppermute x16, waiting for transfers between devices: 66.8 us -> 20.2 us  [swapped(): lax.ppermute(x, axis, [(i, i ^ d) for i in range(lax.axis_size(axis))])]
    pallas_call x2 -> x3, Pallas kernels: 23.6 us -> 30.9 us  [the longest x1 15.9 us: outer_products(): pl.pallas_call(functools.partial(outer_kernel, groups, len(sizes)), out_s...]
    unnamed x20 -> x30, local copies, waits for them, and re-layouts: 10.8 us -> 5.14 us
    ppermute x16, starting transfers between devices: 16.5 us -> 20.9 us  [swapped(): lax.ppermute(x, axis, [(i, i ^ d) for i in range(lax.axis_size(axis))])]
  transfers between devices with their start and end apart: 16 -> 16, of which waited for: 9 -> 7; matrix products, arithmetic and copies ran while one was open for 3% -> 0% of each run, Pallas kernels for 16% -> 27%
where the time goes in v3:
time: 110 us; the launch traced here: 109 us
  Pallas kernels  60.5 us (55%)
  starting transfers between devices  20.9 us (19%)
  waiting for transfers between devices  20.2 us (18%)
  local copies, waits for them, and re-layouts  5.22 us (5%)
  between operations  2.34 us (2%)
    ppermute x16, starting transfers between devices, swapped(): lax.ppermute(x, axis, [(i, i ^ d) for i in range(lax.axis_size(axis))])  20.9 us
    ppermute x16, waiting for transfers between devices, swapped(): lax.ppermute(x, axis, [(i, i ^ d) for i in range(lax.axis_size(axis))])  20.2 us
    pallas_call x1, Pallas kernels, outer_products(): pl.pallas_call(functools.partial(outer_kernel, groups, len(sizes)), out_s...  15.9 us
    pallas_call x1, Pallas kernels, own_factors(): pl.pallas_call(functools.partial(factor_kernel, own, cols), out_shape=sha...  14.9 us
    pallas_call x1, Pallas kernels, middle_products(): pl.pallas_call(middle_kernel, out_shape=jax.ShapeDtypeStruct(cells.shape,...  8.77 us
    pallas_call x1, Pallas kernels, top_factors(): pl.pallas_call(functools.partial(top_kernel, leaves), out_shape=(jax.Shap...  7.71 us
    pallas_call x1, Pallas kernels, lifted_root(): pl.pallas_call(functools.partial(chain_kernel, own, cols), out_shape=jax....  6.93 us
    pallas_call x1, Pallas kernels, turned_blocks(): pl.pallas_call(functools.partial(turn_kernel, groups), out_shape=jax.Shap...  6.25 us
  transfers between devices with their start and end apart: 16, of which 7 were waited for; matrix products, arithmetic and copies ran while one was open for 0% of the time, Pallas kernels for 27%

profile of v3, /device:TPU:0, one launch (start us, length us, event | category | flops | bytes accessed | tf_op | source)
XLA Modules:
  0.0 109.5 jit_solution(17780168481483766606)
XLA Ops:
  0.6 0.1 pad_add_fusion.3.at_ref
  0.7 1.6 %copy-done.2 = f32[32,64,256]{2,1,0:T(8,128)S(1)} copy-done((f32[32,64,256]{2,1,0:T(8,128)S(1)}, f32[32,64,256]{2,1,0:T(8,128)}, u32[]{:S(2)}) %copy-start.2) | copy-done | bytes 2097176
  2.3 14.9 %shard_map.120 = (bf16[12,80,128]{2,1,0:T(8,128)(2,1)S(1)}, bf16[4,12,32,128]{3,2,1,0:T(8,128)(2,1)S(1)}, f32[16,64,64]{2,1,0:T(8,128)S(1)}) custom-call(s32[2]{0:T(128)S(1)} %pad_add_fusion.3.at_ref, f32[32,64,256]{2,1,0:T(8,128)S(1)} %copy-done.2, f32[64,64,255]{2,1,0:T(8,128)} %bitcast.45), custom_call_target="tpu_custom_call" | custom-call | flops 536870912 | bytes 8388608 | tf_op jit(solution)/shard_map/pallas_call | solution.py:201
  17.3 3.1 %collective-permute-start = (bf16[12,32,128]{2,1,0:T(8,128)(2,1)S(1)}, bf16[12,32,128]{2,1,0:T(8,128)(2,1)S(1)}, u32[]{:S(2)}, u32[]{:S(2)}) collective-permute-start(bf16[12,32,128]{2,1,0:T(8,128)(2,1)S(1)} %get-tuple-element.47), channel_id=1, source_target_pairs={{0,1},{1,0},{2,3},{3,2},{4,5},{5,4},{6,7},{7,6},{8,9},{9,8},{10,11... | collective-permute-start | bytes 294920 | tf_op jit(solution)/shard_map/ppermute | solution.py:435
  20.4 2.6 %collective-permute-start.1 = (bf16[12,32,128]{2,1,0:T(8,128)(2,1)S(1)}, bf16[12,32,128]{2,1,0:T(8,128)(2,1)S(1)}, u32[]{:S(2)}, u32[]{:S(2)}) collective-permute-start(bf16[12,32,128]{2,1,0:T(8,128)(2,1)S(1)} %get-tuple-element.46), channel_id=1, source_target_pairs={{0,2},{1,3},{2,0},{3,1},{4,6},{5,7},{6,4},{7,5},{8,10},{9,11},{10,... | collective-permute-start | bytes 294920 | tf_op jit(solution)/shard_map/ppermute | solution.py:435
  23.0 6.2 %shard_map.122.cells_ref = bf16[384,32,128]{2,1,0:T(8,128)(2,1)} custom-call(bf16[64,64,256]{2,1,0:T(8,128)(2,1)S(1)} %bitcast.47, bf16[64,64,128]{2,1,0:T(8,128)(2,1)S(1)} %bitcast.48), custom_call_target="tpu_custom_call" | custom-call | flops 1048576 | bytes 1048576 | tf_op jit(solution)/shard_map/pallas_call | solution.py:331
  29.2 6.9 %shard_map.121 = f32[32,128]{1,0:T(8,128)S(1)} custom-call(s32[2]{0:T(128)S(1)} %pad_add_fusion.3.at_ref, f32[16,64,64]{2,1,0:T(8,128)S(1)} %get-tuple-element.25.gram1_ref, f32[64,64,255]{2,1,0:T(8,128)S(1)} %bitcast.46), custom_call_target="tpu_custom_call" | custom-call | flops 536870912 | bytes 4194304 | tf_op jit(solution)/shard_map/pallas_call | solution.py:245
  36.2 0.9 collective-permute-start.8
  37.2 2.9 %collective-permute-done.8 = f32[32,128]{1,0:T(8,128)S(1)} collective-permute-done((f32[32,128]{1,0:T(8,128)S(1)}, f32[32,128]{1,0:T(8,128)S(1)}, u32[]{:S(2)}, u32[]{:S(2)}) %collective-permute-start.8) | collective-permute-done | bytes 16416 | tf_op jit(solution)/shard_map/ppermute | solution.py:435
  40.1 2.4 %collective-permute-start.9 = (f32[32,128]{1,0:T(8,128)S(1)}, f32[32,128]{1,0:T(8,128)S(1)}, u32[]{:S(2)}, u32[]{:S(2)}) collective-permute-start(f32[32,128]{1,0:T(8,128)S(1)} %add.99), channel_id=1, source_target_pairs={{0,2},{1,3},{2,0},{3,1},{4,6},{5,7},{6,4},{7,5},{8,10},{9,11},{10,... | collective-permute-start | bytes 49160 | tf_op jit(solution)/shard_map/ppermute | solution.py:435
  42.5 1.6 %collective-permute-start.3 = (bf16[48,32,128]{2,1,0:T(8,128)(2,1)S(1)}, bf16[48,32,128]{2,1,0:T(8,128)(2,1)S(1)}, u32[]{:S(2)}, u32[]{:S(2)}) collective-permute-start(bf16[48,32,128]{2,1,0:T(8,128)(2,1)S(1)} %pad_maximum_fusion), channel_id=1, source_target_pairs={{0,8},{4,12},{8,0},{12,4},{16,24},{20,28},{24,16},{28,20},{1,9},{5... | collective-permute-start | bytes 1179656 | tf_op jit(solution)/shard_map/ppermute | solution.py:435
  44.0 1.5 %collective-permute-start.4 = (bf16[48,32,128]{2,1,0:T(8,128)(2,1)S(1)}, bf16[48,32,128]{2,1,0:T(8,128)(2,1)S(1)}, u32[]{:S(2)}, u32[]{:S(2)}) collective-permute-start(bf16[48,32,128]{2,1,0:T(8,128)(2,1)S(1)} %pad_maximum_fusion), channel_id=1, source_target_pairs={{0,16},{4,20},{8,24},{12,28},{16,0},{20,4},{24,8},{28,12},{1,17},{... | collective-permute-start | bytes 1179656 | tf_op jit(solution)/shard_map/ppermute | solution.py:435
  45.5 0.5 collective-permute-start.5
  46.0 0.1 collective-permute-start.10
  46.1 2.1 %collective-permute-start.6 = (bf16[12,80,128]{2,1,0:T(8,128)(2,1)S(1)}, bf16[12,80,128]{2,1,0:T(8,128)(2,1)S(1)}, u32[]{:S(2)}, u32[]{:S(2)}) collective-permute-start(bf16[12,80,128]{2,1,0:T(8,128)(2,1)S(1)} %get-tuple-element.36.refs_0_), channel_id=1, source_target_pairs={{0,1},{1,0},{2,3},{3,2},{4,5},{5,4},{6,7},{7,6},{8,9},{9,8},{10,11... | collective-permute-start | bytes 737288 | tf_op jit(solution)/shard_map/ppermute | solution.py:435
  48.2 1.0 collective-permute-start.7
  49.3 8.9 %collective-permute-done.6.refs_1_ = bf16[12,80,128]{2,1,0:T(8,128)(2,1)S(1)} collective-permute-done((bf16[12,80,128]{2,1,0:T(8,128)(2,1)S(1)}, bf16[12,80,128]{2,1,0:T(8,128)(2,1)S(1)}, u32[]{:S(2)}, u32[]{:S(2)}) %collective-permute-start.6) | collective-permute-done | bytes 245792 | tf_op jit(solution)/shard_map/ppermute | solution.py:435
  58.2 4.3 %collective-permute-done.7.refs_2_ = bf16[12,80,128]{2,1,0:T(8,128)(2,1)S(1)} collective-permute-done((bf16[12,80,128]{2,1,0:T(8,128)(2,1)S(1)}, bf16[12,80,128]{2,1,0:T(8,128)(2,1)S(1)}, u32[]{:S(2)}, u32[]{:S(2)}) %collective-permute-start.7) | collective-permute-done | bytes 245792 | tf_op jit(solution)/shard_map/ppermute | solution.py:435
  62.7 0.5 copy-done.7
  63.5 1.6 %collective-permute-start.12 = (bf16[12,80,128]{2,1,0:T(8,128)(2,1)S(1)}, bf16[12,80,128]{2,1,0:T(8,128)(2,1)S(1)}, u32[]{:S(2)}, u32[]{:S(2)}) collective-permute-start(bf16[12,80,128]{2,1,0:T(8,128)(2,1)S(1)} %get-tuple-element.36.refs_0_), channel_id=1, source_target_pairs={{0,3},{1,2},{2,1},{3,0},{4,7},{5,6},{6,5},{7,4},{8,11},{9,10},{10,... | collective-permute-start | bytes 737288 | tf_op jit(solution)/shard_map/ppermute | solution.py:435
  66.3 1.6 %collective-permute-start.13 = (f32[32,128]{1,0:T(8,128)S(1)}, f32[32,128]{1,0:T(8,128)S(1)}, u32[]{:S(2)}, u32[]{:S(2)}) collective-permute-start(f32[32,128]{1,0:T(8,128)S(1)} %add.101.refs_0_), channel_id=1, source_target_pairs={{0,8},{4,12},{8,0},{12,4},{16,24},{20,28},{24,16},{28,20},{1,9},{5... | collective-permute-start | bytes 49160 | tf_op jit(solution)/shard_map/ppermute | solution.py:435
  67.9 1.5 %collective-permute-start.14 = (f32[32,128]{1,0:T(8,128)S(1)}, f32[32,128]{1,0:T(8,128)S(1)}, u32[]{:S(2)}, u32[]{:S(2)}) collective-permute-start(f32[32,128]{1,0:T(8,128)S(1)} %add.101.refs_0_), channel_id=1, source_target_pairs={{0,16},{4,20},{8,24},{12,28},{16,0},{20,4},{24,8},{28,12},{1,17},{... | collective-permute-start | bytes 49160 | tf_op jit(solution)/shard_map/ppermute | solution.py:435
  69.4 0.5 collective-permute-start.15
  69.9 0.1 pad_add_fusion.2.counts_ref
  70.0 0.2 collective-permute-done.13.refs_1_
  70.1 1.5 %collective-permute-done.14.refs_2_ = f32[32,128]{1,0:T(8,128)S(1)} collective-permute-done((f32[32,128]{1,0:T(8,128)S(1)}, f32[32,128]{1,0:T(8,128)S(1)}, u32[]{:S(2)}, u32[]{:S(2)}) %collective-permute-start.14) | collective-permute-done | bytes 16416 | tf_op jit(solution)/shard_map/ppermute | solution.py:435
  71.6 2.4 %collective-permute-done.15.refs_3_ = f32[32,128]{1,0:T(8,128)S(1)} collective-permute-done((f32[32,128]{1,0:T(8,128)S(1)}, f32[32,128]{1,0:T(8,128)S(1)}, u32[]{:S(2)}, u32[]{:S(2)}) %collective-permute-start.15) | collective-permute-done | bytes 16416 | tf_op jit(solution)/shard_map/ppermute | solution.py:435
  74.1 0.9 copy-done.9
  75.0 7.7 %shard_map.125 = (f32[1,3,64,64]{3,2,1,0:T(8,128)}, f32[64,64]{1,0:T(8,128)}) custom-call(s32[2]{0:T(128)S(1)} %pad_add_fusion.3.at_ref, f32[6,64,64]{2,1,0:T(8,128)S(1)} %copy-done.9, f32[32,128]{1,0:T(8,128)S(1)} %add.101.refs_0_, f32[32,128]{1,0:T(8,128)S(1)} %collective-permute-done.13.refs_1_, f32[32,128]{1,0:T(8,128)S(1)} %collective-permute-done.14.refs_2_, ...), custom_call_target="tpu_custom_call" | custom-call | flops 4194304 | bytes 131072 | tf_op jit(solution)/shard_map/pallas_call | solution.py:290
  82.7 8.8 %shard_map.123.middle_ref = bf16[384,32,128]{2,1,0:T(8,128)(2,1)} custom-call(s32[384]{0:T(512)S(1)} %pad_add_fusion.1.index_ref, bf16[384,32,128]{2,1,0:T(8,128)(2,1)} %shard_map.122.cells_ref, bf16[192,32,128]{2,1,0:T(8,128)(2,1)S(1)} %constant_dynamic-update-slice_fusion.same_ref, bf16[192,32,128]{2,1,0:T(8,128)(2,1)S(1)} %collective-permute-done.11.other_ref), custom_call_target="tpu_custom_call" | custom-call | flops 201326592 | bytes 1048576 | tf_op jit(solution)/shard_map/pallas_call | solution.py:362
  91.5 1.9 %copy-done.1 = bf16[384,32,128]{2,1,0:T(8,128)(2,1)S(1)} copy-done((bf16[384,32,128]{2,1,0:T(8,128)(2,1)S(1)}, bf16[384,32,128]{2,1,0:T(8,128)(2,1)}, u32[]{:S(2)}) %copy-start.1) | copy-done | bytes 3145752
  93.4 15.9 %shard_map.124 = (bf16[64,64,256]{2,1,0:T(8,128)(2,1)}, bf16[64,64,128]{2,1,0:T(8,128)(2,1)}) custom-call(s32[384]{0:T(512)S(1)} %pad_add_fusion.index_ref, s32[2]{0:T(128)S(1)} %pad_add_fusion.2.counts_ref, bf16[384,32,128]{2,1,0:T(8,128)(2,1)S(1)} %copy-done.1, bf16[12,80,128]{2,1,0:T(8,128)(2,1)S(1)} %get-tuple-element.36.refs_0_, ...), custom_call_target="tpu_custom_call" | custom-call | flops 201326592 | bytes 4194304 | tf_op jit(solution)/shard_map/pallas_call | solution.py:418
  (50 shorter events, 0.6 us)
Async XLA Ops:
  0.7 1.6 %copy-start.2 = (f32[32,64,256]{2,1,0:T(8,128)S(1)}, f32[32,64,256]{2,1,0:T(8,128)}, u32[]{:S(2)}) copy-start(f32[32,64,256]{2,1,0:T(8,128)} %basis_ref.1) | copy-start | bytes 6291460
  2.3 20.6 %copy-start.3 = (bf16[256,64,64]{0,2,1:T(8,128)(2,1)S(1)}, bf16[256,64,64]{0,2,1:T(8,128)(2,1)}, u32[]{:S(2)}) copy-start(bf16[256,64,64]{0,2,1:T(8,128)(2,1)} %param.12) | copy-start | bytes 6291460
  2.3 20.6 %copy-start.4 = (bf16[128,64,64]{0,2,1:T(8,128)(2,1)S(1)}, bf16[128,64,64]{0,2,1:T(8,128)(2,1)}, u32[]{:S(2)}) copy-start(bf16[128,64,64]{0,2,1:T(8,128)(2,1)} %param.15) | copy-start | bytes 3145732
  17.3 18.9 %collective-permute-start = (bf16[12,32,128]{2,1,0:T(8,128)(2,1)S(1)}, bf16[12,32,128]{2,1,0:T(8,128)(2,1)S(1)}, u32[]{:S(2)}, u32[]{:S(2)}) collective-permute-start(bf16[12,32,128]{2,1,0:T(8,128)(2,1)S(1)} %get-tuple-element.47), channel_id=1, source_target_pairs={{0,1},{1,0},{2,3},{3,2},{4,5},{5,4},{6,7},{7,6},{8,9},{9,8},{10,11... | collective-permute-start | bytes 294920 | tf_op jit(solution)/shard_map/ppermute | solution.py:435
  20.4 15.9 %collective-permute-start.1 = (bf16[12,32,128]{2,1,0:T(8,128)(2,1)S(1)}, bf16[12,32,128]{2,1,0:T(8,128)(2,1)S(1)}, u32[]{:S(2)}, u32[]{:S(2)}) collective-permute-start(bf16[12,32,128]{2,1,0:T(8,128)(2,1)S(1)} %get-tuple-element.46), channel_id=1, source_target_pairs={{0,2},{1,3},{2,0},{3,1},{4,6},{5,7},{6,4},{7,5},{8,10},{9,11},{10,... | collective-permute-start | bytes 294920 | tf_op jit(solution)/shard_map/ppermute | solution.py:435
  22.9 13.3 %collective-permute-start.2 = (bf16[12,32,128]{2,1,0:T(8,128)(2,1)S(1)}, bf16[12,32,128]{2,1,0:T(8,128)(2,1)S(1)}, u32[]{:S(2)}, u32[]{:S(2)}) collective-permute-start(bf16[12,32,128]{2,1,0:T(8,128)(2,1)S(1)} %get-tuple-element.45), channel_id=1, source_target_pairs={{0,3},{1,2},{2,1},{3,0},{4,7},{5,6},{6,5},{7,4},{8,11},{9,10},{10,... | collective-permute-start | bytes 294920 | tf_op jit(solution)/shard_map/ppermute | solution.py:435
  23.0 6.3 %copy-start = (f32[255,64,64]{0,2,1:T(8,128)S(1)}, f32[255,64,64]{0,2,1:T(8,128)}, u32[]{:S(2)}) copy-start(f32[255,64,64]{0,2,1:T(8,128)} %param.10) | copy-start | bytes 12533764
  36.2 3.8 %collective-permute-start.8 = (f32[32,128]{1,0:T(8,128)S(1)}, f32[32,128]{1,0:T(8,128)S(1)}, u32[]{:S(2)}, u32[]{:S(2)}) collective-permute-start(f32[32,128]{1,0:T(8,128)S(1)} %shard_map.121), channel_id=1, source_target_pairs={{0,1},{1,0},{2,3},{3,2},{4,5},{5,4},{6,7},{7,6},{8,9},{9,8},{10,11... | collective-permute-start | bytes 49160 | tf_op jit(solution)/shard_map/ppermute | solution.py:435
  40.1 6.0 %collective-permute-start.9 = (f32[32,128]{1,0:T(8,128)S(1)}, f32[32,128]{1,0:T(8,128)S(1)}, u32[]{:S(2)}, u32[]{:S(2)}) collective-permute-start(f32[32,128]{1,0:T(8,128)S(1)} %add.99), channel_id=1, source_target_pairs={{0,2},{1,3},{2,0},{3,1},{4,6},{5,7},{6,4},{7,5},{8,10},{9,11},{10,... | collective-permute-start | bytes 49160 | tf_op jit(solution)/shard_map/ppermute | solution.py:435
  42.5 20.0 %collective-permute-start.3 = (bf16[48,32,128]{2,1,0:T(8,128)(2,1)S(1)}, bf16[48,32,128]{2,1,0:T(8,128)(2,1)S(1)}, u32[]{:S(2)}, u32[]{:S(2)}) collective-permute-start(bf16[48,32,128]{2,1,0:T(8,128)(2,1)S(1)} %pad_maximum_fusion), channel_id=1, source_target_pairs={{0,8},{4,12},{8,0},{12,4},{16,24},{20,28},{24,16},{28,20},{1,9},{5... | collective-permute-start | bytes 1179656 | tf_op jit(solution)/shard_map/ppermute | solution.py:435
  44.0 18.5 %collective-permute-start.4 = (bf16[48,32,128]{2,1,0:T(8,128)(2,1)S(1)}, bf16[48,32,128]{2,1,0:T(8,128)(2,1)S(1)}, u32[]{:S(2)}, u32[]{:S(2)}) collective-permute-start(bf16[48,32,128]{2,1,0:T(8,128)(2,1)S(1)} %pad_maximum_fusion), channel_id=1, source_target_pairs={{0,16},{4,20},{8,24},{12,28},{16,0},{20,4},{24,8},{28,12},{1,17},{... | collective-permute-start | bytes 1179656 | tf_op jit(solution)/shard_map/ppermute | solution.py:435
  45.5 17.0 %collective-permute-start.5 = (bf16[48,32,128]{2,1,0:T(8,128)(2,1)S(1)}, bf16[48,32,128]{2,1,0:T(8,128)(2,1)S(1)}, u32[]{:S(2)}, u32[]{:S(2)}) collective-permute-start(bf16[48,32,128]{2,1,0:T(8,128)(2,1)S(1)} %pad_maximum_fusion), channel_id=1, source_target_pairs={{0,24},{4,28},{8,16},{12,20},{16,8},{20,12},{24,0},{28,4},{1,25},{... | collective-permute-start | bytes 1179656 | tf_op jit(solution)/shard_map/ppermute | solution.py:435
  46.0 17.3 %copy-start.10 = (s32[256,2]{0,1:T(2,128)S(1)}, s32[256,2]{0,1:T(2,128)}, u32[]{:S(2)}) copy-start(s32[256,2]{0,1:T(2,128)} %param.13) | copy-start | bytes 6148
  46.0 17.4 %copy-start.11 = (s32[128,2]{0,1:T(2,128)S(1)}, s32[128,2]{0,1:T(2,128)}, u32[]{:S(2)}) copy-start(s32[128,2]{0,1:T(2,128)} %param.16) | copy-start | bytes 3076
  46.0 2.2 %collective-permute-start.10 = (f32[32,128]{1,0:T(8,128)S(1)}, f32[32,128]{1,0:T(8,128)S(1)}, u32[]{:S(2)}, u32[]{:S(2)}) collective-permute-start(f32[32,128]{1,0:T(8,128)S(1)} %add.100), channel_id=1, source_target_pairs={{0,4},{4,0},{8,12},{12,8},{16,20},{20,16},{24,28},{28,24},{1,5},{5... | collective-permute-start | bytes 49160 | tf_op jit(solution)/shard_map/ppermute | solution.py:435
  46.1 12.1 %collective-permute-start.6 = (bf16[12,80,128]{2,1,0:T(8,128)(2,1)S(1)}, bf16[12,80,128]{2,1,0:T(8,128)(2,1)S(1)}, u32[]{:S(2)}, u32[]{:S(2)}) collective-permute-start(bf16[12,80,128]{2,1,0:T(8,128)(2,1)S(1)} %get-tuple-element.36.refs_0_), channel_id=1, source_target_pairs={{0,1},{1,0},{2,3},{3,2},{4,5},{5,4},{6,7},{7,6},{8,9},{9,8},{10,11... | collective-permute-start | bytes 737288 | tf_op jit(solution)/shard_map/ppermute | solution.py:435
  48.2 14.3 %collective-permute-start.7 = (bf16[12,80,128]{2,1,0:T(8,128)(2,1)S(1)}, bf16[12,80,128]{2,1,0:T(8,128)(2,1)S(1)}, u32[]{:S(2)}, u32[]{:S(2)}) collective-permute-start(bf16[12,80,128]{2,1,0:T(8,128)(2,1)S(1)} %get-tuple-element.36.refs_0_), channel_id=1, source_target_pairs={{0,2},{1,3},{2,0},{3,1},{4,6},{5,7},{6,4},{7,5},{8,10},{9,11},{10,... | collective-permute-start | bytes 737288 | tf_op jit(solution)/shard_map/ppermute | solution.py:435
  58.2 4.4 %copy-start.5 = (bf16[12,80,128]{2,1,0:T(8,128)(2,1)}, bf16[12,80,128]{2,1,0:T(8,128)(2,1)S(1)}, u32[]{:S(2)}) copy-start(bf16[12,80,128]{2,1,0:T(8,128)(2,1)S(1)} %collective-permute-done.6.refs_1_) | copy-start | bytes 737284
  62.5 0.7 copy-start.7
  63.3 19.5 %collective-permute-start.11 = (bf16[192,32,128]{2,1,0:T(8,128)(2,1)S(1)}, bf16[192,32,128]{2,1,0:T(8,128)(2,1)S(1)}, u32[]{:S(2)}, u32[]{:S(2)}) collective-permute-start(bf16[192,32,128]{2,1,0:T(8,128)(2,1)S(1)} %constant_dynamic-update-slice_fusion.same_ref), channel_id=1, source_target_pairs={{0,4},{4,0},{8,12},{12,8},{16,20},{20,16},{24,28},{28,24},{1,5},{5... | collective-permute-start | bytes 4718600 | tf_op jit(solution)/shard_map/ppermute | solution.py:435
  63.5 28.0 %collective-permute-start.12 = (bf16[12,80,128]{2,1,0:T(8,128)(2,1)S(1)}, bf16[12,80,128]{2,1,0:T(8,128)(2,1)S(1)}, u32[]{:S(2)}, u32[]{:S(2)}) collective-permute-start(bf16[12,80,128]{2,1,0:T(8,128)(2,1)S(1)} %get-tuple-element.36.refs_0_), channel_id=1, source_target_pairs={{0,3},{1,2},{2,1},{3,0},{4,7},{5,6},{6,5},{7,4},{8,11},{9,10},{10,... | collective-permute-start | bytes 737288 | tf_op jit(solution)/shard_map/ppermute | solution.py:435
  66.3 3.8 %collective-permute-start.13 = (f32[32,128]{1,0:T(8,128)S(1)}, f32[32,128]{1,0:T(8,128)S(1)}, u32[]{:S(2)}, u32[]{:S(2)}) collective-permute-start(f32[32,128]{1,0:T(8,128)S(1)} %add.101.refs_0_), channel_id=1, source_target_pairs={{0,8},{4,12},{8,0},{12,4},{16,24},{20,28},{24,16},{28,20},{1,9},{5... | collective-permute-start | bytes 49160 | tf_op jit(solution)/shard_map/ppermute | solution.py:435
  67.9 3.7 %collective-permute-start.14 = (f32[32,128]{1,0:T(8,128)S(1)}, f32[32,128]{1,0:T(8,128)S(1)}, u32[]{:S(2)}, u32[]{:S(2)}) collective-permute-start(f32[32,128]{1,0:T(8,128)S(1)} %add.101.refs_0_), channel_id=1, source_target_pairs={{0,16},{4,20},{8,24},{12,28},{16,0},{20,4},{24,8},{28,12},{1,17},{... | collective-permute-start | bytes 49160 | tf_op jit(solution)/shard_map/ppermute | solution.py:435
  69.4 4.6 %collective-permute-start.15 = (f32[32,128]{1,0:T(8,128)S(1)}, f32[32,128]{1,0:T(8,128)S(1)}, u32[]{:S(2)}, u32[]{:S(2)}) collective-permute-start(f32[32,128]{1,0:T(8,128)S(1)} %add.101.refs_0_), channel_id=1, source_target_pairs={{0,24},{4,28},{8,16},{12,20},{16,8},{20,12},{24,0},{28,4},{1,25},{... | collective-permute-start | bytes 49160 | tf_op jit(solution)/shard_map/ppermute | solution.py:435
  74.1 0.9 copy-start.9
  82.7 8.8 %copy-start.6 = (bf16[12,80,128]{2,1,0:T(8,128)(2,1)S(1)}, bf16[12,80,128]{2,1,0:T(8,128)(2,1)}, u32[]{:S(2)}) copy-start(bf16[12,80,128]{2,1,0:T(8,128)(2,1)} %copy-done.5) | copy-start | bytes 737284
  82.7 8.8 %copy-start.8 = (bf16[12,80,128]{2,1,0:T(8,128)(2,1)S(1)}, bf16[12,80,128]{2,1,0:T(8,128)(2,1)}, u32[]{:S(2)}) copy-start(bf16[12,80,128]{2,1,0:T(8,128)(2,1)} %copy-done.7) | copy-start | bytes 737284
  91.5 1.9 %copy-start.1 = (bf16[384,32,128]{2,1,0:T(8,128)(2,1)S(1)}, bf16[384,32,128]{2,1,0:T(8,128)(2,1)}, u32[]{:S(2)}) copy-start(bf16[384,32,128]{2,1,0:T(8,128)(2,1)} %shard_map.123.middle_ref) | copy-start | bytes 9437188

commit v4 on v3

--- a/solution.py
+++ b/solution.py
@@ -1,4 +1,5 @@
 import functools
+import math
 
 import jax
 import jax.numpy as jnp
@@ -18,10 +19,12 @@
 SMEM = pl.BlockSpec(memory_space=pltpu.SMEM)
 VMEM = pl.BlockSpec(memory_space=pltpu.VMEM)
 ANY = pl.BlockSpec(memory_space=pl.ANY)
+HBM = pl.BlockSpec(memory_space=pltpu.HBM)
+TERMS = 3
 TURN = 8
 SLOTS = 64
 PAIRS = 4
-PARAMS = pltpu.CompilerParams(vmem_limit_bytes=48 * 2**20)
+PARAMS = pltpu.CompilerParams(vmem_limit_bytes=24 * 2**20)
 
 
 def unhalf(x):
@@ -160,22 +163,55 @@
     return out
 
 
-def factor_kernel(own, cols, at_ref, basis_ref, xfer_ref, fac_ref, sent_ref, gram1_ref, xt, s, a):
+def factor_kernel(
+    own,
+    cols,
+    at_ref,
+    all_basis_ref,
+    all_xfer_ref,
+    fac_ref,
+    sent_ref,
+    gram1_ref,
+    xt,
+    s,
+    a,
+    g0,
+    basis_ref,
+    xfer_ref,
+    basis_sem,
+    sem,
+):
     col = at_ref[1]
     first = col * own
+    pairs = min(PAIRS, own // 2)
+
+    def chunk(step):
+        rows = pl.ds(2 * pairs * step, 2 * pairs)
+        return pltpu.make_async_copy(all_basis_ref.at[rows], basis_ref.at[rows], basis_sem.at[step])
+
+    for step in range(own // 2 // pairs):
+        chunk(step).start()
+    copy = pltpu.make_async_copy(all_xfer_ref.at[:, :, pl.ds(0, LANES)], xfer_ref, sem)
+    copy.start()
+
+    @pl.loop(0, own // 2 // pairs)
+    def _(step):
+        chunk(step).wait()
+        at = [2 * step * pairs + c for c in range(2 * pairs)]
+        points = [basis_ref[c] for c in at]
+        grams = [mul(x, x, NT) for x in points]
+        for c, gram in zip(at, grams):
+            g0[c] = gram
+            s[c] = halve(gram)
+
+    copy.wait()
     unpack_transfers(xfer_ref, xt)
-
-    pairs = min(PAIRS, own // 2)
 
     @pl.loop(0, own // 2 // pairs)
     def _(step):
         base = step * pairs
         at = [2 * base + c for c in range(2 * pairs)]
-        points = [basis_ref[c] for c in at]
-        grams = [mul(x, x, NT) for x in points]
-        parents = lift_pairs(grams, [unhalf(xt[first + c]) for c in at])
-        for c, gram in zip(at, grams):
-            s[c] = halve(gram)
+        parents = lift_pairs([g0[c] for c in at], [unhalf(xt[first + c]) for c in at])
         for p, gram in enumerate(parents):
             gram1_ref[base + p] = gram
             s[own + base + p] = halve(gram)
@@ -201,21 +237,23 @@
     return pl.pallas_call(
         functools.partial(factor_kernel, own, cols),
         out_shape=shapes,
-        grid=(1,),
         in_specs=[
             SMEM,
-            pl.BlockSpec(basis.shape, lambda i: (0, 0, 0)),
-            pl.BlockSpec((K, K, LANES), lambda i: (0, 0, 0)),
+            HBM,
+            HBM,
         ],
-        out_specs=tuple(
-            pl.BlockSpec(x.shape, lambda i, rank=len(x.shape): (0,) * rank) for x in shapes
-        ),
+        out_specs=(VMEM,) * len(shapes),
         scratch_shapes=[
             pltpu.VMEM((LANES, H, 2 * K), F32),
             pltpu.VMEM((rows, H, 2 * K), F32),
             pltpu.VMEM((K, K, rows), F32),
+            pltpu.VMEM((own, K, K), F32),
+            pltpu.VMEM(basis.shape, F32),
+            pltpu.VMEM((K, K, LANES), F32),
+            pltpu.SemaphoreType.DMA((own // 2 // min(PAIRS, own // 2),)),
+            pltpu.SemaphoreType.DMA,
         ],
-        compiler_params=PARAMS,
+        compiler_params=pltpu.CompilerParams(vmem_limit_bytes=52 * 2**20),
         cost_estimate=cost(own * 2**24, 2**23),
     )(at, basis, xfer_lanes)
 
@@ -238,20 +276,24 @@
         offset += width
         width //= 2
         shift += 1
-    out_ref[...] = halve(grams[0])
+    rest = halve(grams[0])
+    for n in range(TERMS):
+        term = rest.astype(BF)
+        out_ref[n] = term
+        rest = rest - term.astype(F32)
 
 
 def lifted_root(at, gram1, xfer_lanes, own, cols):
     return pl.pallas_call(
         functools.partial(chain_kernel, own, cols),
-        out_shape=jax.ShapeDtypeStruct((H, 2 * K), F32),
+        out_shape=jax.ShapeDtypeStruct((TERMS, H, 2 * K), BF),
         grid=(1,),
         in_specs=[
             SMEM,
             pl.BlockSpec(gram1.shape, lambda i: (0, 0, 0)),
             pl.BlockSpec((K, K, LANES), lambda i: (0, 0, 1)),
         ],
-        out_specs=pl.BlockSpec((H, 2 * K), lambda i: (0, 0)),
+        out_specs=pl.BlockSpec((TERMS, H, 2 * K), lambda i: (0, 0, 0)),
         scratch_shapes=[pltpu.VMEM((LANES, H, 2 * K), F32)],
         compiler_params=PARAMS,
         cost_estimate=cost(own * 2**24, 2**22),
@@ -260,10 +302,13 @@
 
 def top_kernel(leaves, at_ref, top_ref, *refs):
     pairs = leaves // 2
-    parts, (anc_ref, root_ref, level_ref, s, a) = refs[:pairs], refs[pairs:]
+    parts, (anc_ref, root_ref, level_ref, s, a) = refs[:-5], refs[-5:]
     pair = jnp.right_shift(at_ref[0], 1)
     for m in range(pairs):
-        level_ref[jnp.bitwise_xor(pair, m)] = parts[m][...]
+        terms = [part[m] for part in parts]
+        while len(terms) > 1:
+            terms = [x + y for x, y in zip(terms[0::2], terms[1::2])]
+        level_ref[jnp.bitwise_xor(pair, m)] = terms[0]
     level = [unhalf(level_ref[m]) for m in range(pairs)]
     heights = []
     slot = 0
@@ -373,13 +418,16 @@
     pieces, out_refs = refs[:-outs - 4], refs[-outs - 4 : -4]
     pt, table, ready, sem = refs[-4:]
     packs = pieces[0].shape[0]
+    together = math.gcd(packs, 6)
     for e, piece in enumerate(pieces):
 
-        @pl.loop(0, packs)
-        def _(g):
-            four = unpack(piece[g].astype(F32))
-            for m in range(4):
-                table[4 * (e * packs + g) + m] = four[m].astype(BF)
+        @pl.loop(0, packs // together)
+        def _(step):
+            at = [step * together + g for g in range(together)]
+            full = [unpack(piece[g].astype(F32)) for g in at]
+            for g, four in zip(at, full):
+                for m in range(4):
+                    table[4 * (e * packs + g) + m] = four[m].astype(BF)
 
     copies = []
     for g, (which, first) in enumerate(groups):
@@ -453,7 +501,7 @@
         owner = pairs[:, 1] // size
         away = owner // cols ^ leaf
         piece = (away & 1) * (leaves // 2) + (away >> 1)
-        column = (piece * cols + (owner % cols ^ col)) * parts
+        column = piece * (count + TERMS) + (owner % cols ^ col) * parts
         return row, column + level * (own // cols) + pairs[:, 1] % size // cols
 
     row0, column0 = indices(pairs0, 0)
@@ -461,22 +509,26 @@
 
     factors, sent, gram1 = own_factors(at, basis, xfer_lanes, cols)
     received = [swapped(sent[d], "col", d) for d in range(1, cols)]
-    gram = lifted_root(at, gram1, xfer_lanes, own, cols)
-    cells = turned_blocks((lanes0, lanes1))
-    received, gram, factors, cells = lax.optimization_barrier((received, gram, factors, cells))
-
-    part = jnp.concatenate([sent[0]] + received, axis=0)
+    terms = lifted_root(at, gram1, xfer_lanes, own, cols)
+    received, terms, factors, lanes0, lanes1 = lax.optimization_barrier(
+        (received, terms, factors, lanes0, lanes1)
+    )
+
+    part = jnp.concatenate([sent[0]] + received + [terms], axis=0)
     chips = [swapped(part, "leaf", d) for d in range(2, leaves, 2)]
     row_pieces = [factors] + [swapped(factors, "col", d) for d in range(1, cols - 1)]
-    for bit in range(cols.bit_length() - 1):
-        gram = gram + swapped(gram, "col", 1 << bit)
-    gram = gram + swapped(gram, "leaf", 1)
-    chips, row_pieces, gram = lax.optimization_barrier((chips, row_pieces, gram))
+    cells = turned_blocks((lanes0, lanes1))
+    chips, row_pieces, cells = lax.optimization_barrier((chips, row_pieces, cells))
 
     row_pieces = row_pieces + [swapped(factors, "col", cols - 1)]
     same_core = jnp.concatenate([part] + chips, axis=0)
     other_core = swapped(same_core, "leaf", 1)
-    tops = [gram] + [swapped(gram, "leaf", d) for d in range(2, leaves, 2)]
+
+    def sums(x):
+        return x.reshape(leaves // 2, count + TERMS, H, 2 * K)[:, count:].astype(F32).sum(axis=1)
+
+    pair_part = sums(same_core) + sums(other_core)
+    tops = [pair_part] + [swapped(pair_part, "col", d) for d in range(1, cols)]
     ancestors, root = top_factors(at, tops, top_transfer, leaves)
 
     middle = middle_products(jnp.concatenate([column0, column1]), cells, same_core, other_core)

time: 110 us -> 93.2 us (0.85)
  waiting for transfers between devices: 20.2 us -> 7.25 us
  Pallas kernels: 60.5 us -> 52.9 us
  local copies, waits for them, and re-layouts: 5.22 us -> 7.1 us
  other arithmetic: 0.31 us -> 2.09 us
    ppermute x16 -> x13, waiting for transfers between devices: 20.2 us -> 7.25 us  [swapped(): lax.ppermute(x, axis, [(i, i ^ d) for i in range(lax.axis_size(axis))])]
    pallas_call x1, Pallas kernels: 15.9 us -> 10.6 us  [outer_products(): pl.pallas_call(functools.partial(outer_kernel, groups, len(sizes)), out_s...]
    pallas_call x1, Pallas kernels: 8.77 us -> 6.93 us  [middle_products(): pl.pallas_call(middle_kernel, out_shape=jax.ShapeDtypeStruct(cells.shape,...]
    reduce_sum x0 -> x2, other arithmetic: none -> 1.83 us  [sums(): x.reshape(leaves // 2, count + TERMS, H, 2 * K)[:, count:].astype(F32)]
    pallas_call x1, Pallas kernels: 6.25 us -> 4.61 us  [turned_blocks(): pl.pallas_call(functools.partial(turn_kernel, groups), out_shape=jax.Shap...]
    pallas_call x1, Pallas kernels: 14.9 us -> 16.1 us  [own_factors(): pl.pallas_call(functools.partial(factor_kernel, own, cols), out_shape=sha...]
    unnamed x30 -> x27, local copies, waits for them, and re-layouts: 5.14 us -> 6.3 us
    ppermute x16 -> x13, starting transfers between devices: 20.9 us -> 21.5 us  [swapped(): lax.ppermute(x, axis, [(i, i ^ d) for i in range(lax.axis_size(axis))])]
  transfers between devices with their start and end apart: 16 -> 13, of which waited for: 7 -> 5; matrix products, arithmetic and copies ran while one was open for 0% -> 3% of each run, Pallas kernels for 27% -> 31%
where the time goes in v4:
time: 93.2 us; the launch traced here: 93 us
  Pallas kernels  52.9 us (57%)
  starting transfers between devices  21.5 us (23%)
  waiting for transfers between devices  7.25 us (8%)
  local copies, waits for them, and re-layouts  7.1 us (8%)
  between operations  2.16 us (2%)
  other arithmetic  2.09 us (2%)
    ppermute x13, starting transfers between devices, swapped(): lax.ppermute(x, axis, [(i, i ^ d) for i in range(lax.axis_size(axis))])  21.5 us
    pallas_call x1, Pallas kernels, own_factors(): pl.pallas_call(functools.partial(factor_kernel, own, cols), out_shape=sha...  16.1 us
    pallas_call x1, Pallas kernels, outer_products(): pl.pallas_call(functools.partial(outer_kernel, groups, len(sizes)), out_s...  10.6 us
    pallas_call x1, Pallas kernels, top_factors(): pl.pallas_call(functools.partial(top_kernel, leaves), out_shape=(jax.Shap...  7.72 us
    ppermute x13, waiting for transfers between devices, swapped(): lax.ppermute(x, axis, [(i, i ^ d) for i in range(lax.axis_size(axis))])  7.25 us
    pallas_call x1, Pallas kernels, lifted_root(): pl.pallas_call(functools.partial(chain_kernel, own, cols), out_shape=jax....  6.95 us
    pallas_call x1, Pallas kernels, middle_products(): pl.pallas_call(middle_kernel, out_shape=jax.ShapeDtypeStruct(cells.shape,...  6.93 us
    unnamed x27, local copies, waits for them, and re-layouts  6.3 us
  transfers between devices with their start and end apart: 13, of which 5 were waited for; matrix products, arithmetic and copies ran while one was open for 3% of the time, Pallas kernels for 31%

profile of v4, /device:TPU:0, one launch (start us, length us, event | category | flops | bytes accessed | tf_op | source)
XLA Modules:
  0.0 93.0 jit_solution(10033589660987299032)
XLA Ops:
  0.7 16.1 %shard_map.120 = (bf16[12,80,128]{2,1,0:T(8,128)(2,1)S(1)}, bf16[4,12,32,128]{3,2,1,0:T(8,128)(2,1)S(1)}, f32[16,64,64]{2,1,0:T(8,128)S(1)}) custom-call(s32[2]{0:T(128)S(1)} %pad_add_fusion.3.at_ref, f32[32,64,256]{2,1,0:T(8,128)} %all_basis_ref.1, f32[64,64,255]{2,1,0:T(8,128)} %bitcast.46), custom_call_target="tpu_custom_call" | custom-call | flops 536870912 | bytes 8388608 | tf_op jit(solution)/shard_map/pallas_call | solution.py:237
  16.8 3.1 %collective-permute-start = (bf16[12,32,128]{2,1,0:T(8,128)(2,1)S(1)}, bf16[12,32,128]{2,1,0:T(8,128)(2,1)S(1)}, u32[]{:S(2)}, u32[]{:S(2)}) collective-permute-start(bf16[12,32,128]{2,1,0:T(8,128)(2,1)S(1)} %get-tuple-element.50), channel_id=1, source_target_pairs={{0,1},{1,0},{2,3},{3,2},{4,5},{5,4},{6,7},{7,6},{8,9},{9,8},{10,11... | collective-permute-start | bytes 294920 | tf_op jit(solution)/shard_map/ppermute | solution.py:483
  19.9 2.6 %collective-permute-start.1 = (bf16[12,32,128]{2,1,0:T(8,128)(2,1)S(1)}, bf16[12,32,128]{2,1,0:T(8,128)(2,1)S(1)}, u32[]{:S(2)}, u32[]{:S(2)}) collective-permute-start(bf16[12,32,128]{2,1,0:T(8,128)(2,1)S(1)} %get-tuple-element.49), channel_id=1, source_target_pairs={{0,2},{1,3},{2,0},{3,1},{4,6},{5,7},{6,4},{7,5},{8,10},{9,11},{10,... | collective-permute-start | bytes 294920 | tf_op jit(solution)/shard_map/ppermute | solution.py:483
  22.5 0.7 bitcast_dynamic-update-slice_fusion
  23.2 7.0 %shard_map.121 = bf16[3,32,128]{2,1,0:T(8,128)(2,1)S(1)} custom-call(s32[2]{0:T(128)S(1)} %pad_add_fusion.3.at_ref, f32[16,64,64]{2,1,0:T(8,128)S(1)} %get-tuple-element.26.gram1_ref, f32[64,64,255]{2,1,0:T(8,128)S(1)} %bitcast.47), custom_call_target="tpu_custom_call" | custom-call | flops 536870912 | bytes 4194304 | tf_op jit(solution)/shard_map/pallas_call | solution.py:287
  30.2 0.1 collective-permute-done.1
  30.4 0.7 constant_dynamic-update-slice_fusion.10
  31.0 0.7 constant_dynamic-update-slice_fusion.9
  31.7 0.7 constant_dynamic-update-slice_fusion.8
  32.4 0.6 constant_dynamic-update-slice_fusion.7
  33.0 1.6 %collective-permute-start.3 = (bf16[51,32,128]{2,1,0:T(8,128)(2,1)S(1)}, bf16[51,32,128]{2,1,0:T(8,128)(2,1)S(1)}, u32[]{:S(2)}, u32[]{:S(2)}) collective-permute-start(bf16[51,32,128]{2,1,0:T(8,128)(2,1)S(1)} %get-tuple-element.58), channel_id=1, source_target_pairs={{0,8},{4,12},{8,0},{12,4},{16,24},{20,28},{24,16},{28,20},{1,9},{5... | collective-permute-start | bytes 1253384 | tf_op jit(solution)/shard_map/ppermute | solution.py:483
  34.6 1.5 %collective-permute-start.4 = (bf16[51,32,128]{2,1,0:T(8,128)(2,1)S(1)}, bf16[51,32,128]{2,1,0:T(8,128)(2,1)S(1)}, u32[]{:S(2)}, u32[]{:S(2)}) collective-permute-start(bf16[51,32,128]{2,1,0:T(8,128)(2,1)S(1)} %get-tuple-element.58), channel_id=1, source_target_pairs={{0,16},{4,20},{8,24},{12,28},{16,0},{20,4},{24,8},{28,12},{1,17},{... | collective-permute-start | bytes 1253384 | tf_op jit(solution)/shard_map/ppermute | solution.py:483
  36.1 0.4 collective-permute-start.5
  36.5 1.6 %collective-permute-start.6 = (bf16[12,80,128]{2,1,0:T(8,128)(2,1)S(1)}, bf16[12,80,128]{2,1,0:T(8,128)(2,1)S(1)}, u32[]{:S(2)}, u32[]{:S(2)}) collective-permute-start(bf16[12,80,128]{2,1,0:T(8,128)(2,1)S(1)} %get-tuple-element.39.refs_0_), channel_id=1, source_target_pairs={{0,1},{1,0},{2,3},{3,2},{4,5},{5,4},{6,7},{7,6},{8,9},{9,8},{10,11... | collective-permute-start | bytes 737288 | tf_op jit(solution)/shard_map/ppermute | solution.py:483
  38.1 2.7 %collective-permute-start.7 = (bf16[12,80,128]{2,1,0:T(8,128)(2,1)S(1)}, bf16[12,80,128]{2,1,0:T(8,128)(2,1)S(1)}, u32[]{:S(2)}, u32[]{:S(2)}) collective-permute-start(bf16[12,80,128]{2,1,0:T(8,128)(2,1)S(1)} %get-tuple-element.39.refs_0_), channel_id=1, source_target_pairs={{0,2},{1,3},{2,0},{3,1},{4,6},{5,7},{6,4},{7,5},{8,10},{9,11},{10,... | collective-permute-start | bytes 737288 | tf_op jit(solution)/shard_map/ppermute | solution.py:483
  40.8 4.6 %shard_map.122.cells_ref = bf16[384,32,128]{2,1,0:T(8,128)(2,1)S(1)} custom-call(bf16[64,64,256]{2,1,0:T(8,128)(2,1)S(1)} %bitcast.48, bf16[64,64,128]{2,1,0:T(8,128)(2,1)S(1)} %bitcast.49), custom_call_target="tpu_custom_call" | custom-call | flops 1048576 | bytes 1048576 | tf_op jit(solution)/shard_map/pallas_call | solution.py:376
  45.4 2.2 %collective-permute-done.6.refs_1_ = bf16[12,80,128]{2,1,0:T(8,128)(2,1)S(1)} collective-permute-done((bf16[12,80,128]{2,1,0:T(8,128)(2,1)S(1)}, bf16[12,80,128]{2,1,0:T(8,128)(2,1)S(1)}, u32[]{:S(2)}, u32[]{:S(2)}) %collective-permute-start.6) | collective-permute-done | bytes 245792 | tf_op jit(solution)/shard_map/ppermute | solution.py:483
  47.6 0.7 copy-done.3
  48.3 1.8 %collective-permute-done.7.refs_2_ = bf16[12,80,128]{2,1,0:T(8,128)(2,1)S(1)} collective-permute-done((bf16[12,80,128]{2,1,0:T(8,128)(2,1)S(1)}, bf16[12,80,128]{2,1,0:T(8,128)(2,1)S(1)}, u32[]{:S(2)}, u32[]{:S(2)}) %collective-permute-start.7) | collective-permute-done | bytes 245792 | tf_op jit(solution)/shard_map/ppermute | solution.py:483
  50.0 0.7 copy-done.5
  50.8 3.1 %collective-permute-done.4 = bf16[51,32,128]{2,1,0:T(8,128)(2,1)S(1)} collective-permute-done((bf16[51,32,128]{2,1,0:T(8,128)(2,1)S(1)}, bf16[51,32,128]{2,1,0:T(8,128)(2,1)S(1)}, u32[]{:S(2)}, u32[]{:S(2)}) %collective-permute-start.4) | collective-permute-done | bytes 417824 | tf_op jit(solution)/shard_map/ppermute | solution.py:483
  53.9 0.8 constant_dynamic-update-slice_fusion.6
  54.7 0.8 constant_dynamic-update-slice_fusion.5
  55.4 0.8 constant_dynamic-update-slice_fusion.4.same_ref
  57.7 3.6 %collective-permute-start.9 = (bf16[12,80,128]{2,1,0:T(8,128)(2,1)S(1)}, bf16[12,80,128]{2,1,0:T(8,128)(2,1)S(1)}, u32[]{:S(2)}, u32[]{:S(2)}) collective-permute-start(bf16[12,80,128]{2,1,0:T(8,128)(2,1)S(1)} %get-tuple-element.39.refs_0_), channel_id=1, source_target_pairs={{0,3},{1,2},{2,1},{3,0},{4,7},{5,6},{6,5},{7,4},{8,11},{9,10},{10,... | collective-permute-start | bytes 737288 | tf_op jit(solution)/shard_map/ppermute | solution.py:483
  61.3 0.9 convert_reduce_fusion.1
  62.2 0.9 convert_reduce_fusion
  63.2 2.0 %collective-permute-start.11 = (f32[4,32,128]{2,1,0:T(8,128)S(1)}, f32[4,32,128]{2,1,0:T(8,128)S(1)}, u32[]{:S(2)}, u32[]{:S(2)}) collective-permute-start(f32[4,32,128]{2,1,0:T(8,128)S(1)} %add.93.refs_0_), channel_id=1, source_target_pairs={{0,2},{1,3},{2,0},{3,1},{4,6},{5,7},{6,4},{7,5},{8,10},{9,11},{10,... | collective-permute-start | bytes 196616 | tf_op jit(solution)/shard_map/ppermute | solution.py:483
  65.2 2.4 %collective-permute-start.12 = (f32[4,32,128]{2,1,0:T(8,128)S(1)}, f32[4,32,128]{2,1,0:T(8,128)S(1)}, u32[]{:S(2)}, u32[]{:S(2)}) collective-permute-start(f32[4,32,128]{2,1,0:T(8,128)S(1)} %add.93.refs_0_), channel_id=1, source_target_pairs={{0,3},{1,2},{2,1},{3,0},{4,7},{5,6},{6,5},{7,4},{8,11},{9,10},{10,... | collective-permute-start | bytes 196616 | tf_op jit(solution)/shard_map/ppermute | solution.py:483
  67.7 6.9 %shard_map.123.middle_ref = bf16[384,32,128]{2,1,0:T(8,128)(2,1)S(1)} custom-call(s32[384]{0:T(512)S(1)} %pad_add_fusion.1.index_ref, bf16[384,32,128]{2,1,0:T(8,128)(2,1)S(1)} %shard_map.122.cells_ref, bf16[204,32,128]{2,1,0:T(8,128)(2,1)} %constant_dynamic-update-slice_fusion.4.same_ref, bf16[204,32,128]{2,1,0:T(8,128)(2,1)} %collective-permute-done.8.other_ref), custom_call_target="tpu_custom_call" | custom-call | flops 201326592 | bytes 1048576 | tf_op jit(solution)/shard_map/pallas_call | solution.py:407
  74.6 10.6 %shard_map.124 = (bf16[64,64,256]{2,1,0:T(8,128)(2,1)}, bf16[64,64,128]{2,1,0:T(8,128)(2,1)}) custom-call(s32[384]{0:T(512)S(1)} %pad_add_fusion.index_ref, s32[2]{0:T(128)S(1)} %pad_add_fusion.2.counts_ref, bf16[384,32,128]{2,1,0:T(8,128)(2,1)S(1)} %shard_map.123.middle_ref, bf16[12,80,128]{2,1,0:T(8,128)(2,1)S(1)} %get-tuple-element.39.refs_0_, ...), custom_call_target="tpu_custom_call" | custom-call | flops 201326592 | bytes 4194304 | tf_op jit(solution)/shard_map/pallas_call | solution.py:466
  85.3 7.7 %shard_map.125 = (f32[1,3,64,64]{3,2,1,0:T(8,128)}, f32[64,64]{1,0:T(8,128)}) custom-call(s32[2]{0:T(128)S(1)} %pad_add_fusion.3.at_ref, f32[6,64,64]{2,1,0:T(8,128)S(1)} %copy-done.7, f32[4,32,128]{2,1,0:T(8,128)S(1)} %add.93.refs_0_, f32[4,32,128]{2,1,0:T(8,128)S(1)} %collective-permute-done.10.refs_1_, f32[4,32,128]{2,1,0:T(8,128)S(1)} %collective-permute-done.11.refs_2_, ...), custom_call_target="tpu_custom_call" | custom-call | flops 4194304 | bytes 131072 | tf_op jit(solution)/shard_map/pallas_call | solution.py:335
  (40 shorter events, 0.5 us)
Async XLA Ops:
  0.7 22.5 %copy-start = (f32[255,64,64]{0,2,1:T(8,128)S(1)}, f32[255,64,64]{0,2,1:T(8,128)}, u32[]{:S(2)}) copy-start(f32[255,64,64]{0,2,1:T(8,128)} %param.10) | copy-start | bytes 12533764
  16.8 13.4 %collective-permute-start = (bf16[12,32,128]{2,1,0:T(8,128)(2,1)S(1)}, bf16[12,32,128]{2,1,0:T(8,128)(2,1)S(1)}, u32[]{:S(2)}, u32[]{:S(2)}) collective-permute-start(bf16[12,32,128]{2,1,0:T(8,128)(2,1)S(1)} %get-tuple-element.50), channel_id=1, source_target_pairs={{0,1},{1,0},{2,3},{3,2},{4,5},{5,4},{6,7},{7,6},{8,9},{9,8},{10,11... | collective-permute-start | bytes 294920 | tf_op jit(solution)/shard_map/ppermute | solution.py:483
  19.9 10.4 %collective-permute-start.1 = (bf16[12,32,128]{2,1,0:T(8,128)(2,1)S(1)}, bf16[12,32,128]{2,1,0:T(8,128)(2,1)S(1)}, u32[]{:S(2)}, u32[]{:S(2)}) collective-permute-start(bf16[12,32,128]{2,1,0:T(8,128)(2,1)S(1)} %get-tuple-element.49), channel_id=1, source_target_pairs={{0,2},{1,3},{2,0},{3,1},{4,6},{5,7},{6,4},{7,5},{8,10},{9,11},{10,... | collective-permute-start | bytes 294920 | tf_op jit(solution)/shard_map/ppermute | solution.py:483
  22.5 7.8 %collective-permute-start.2 = (bf16[12,32,128]{2,1,0:T(8,128)(2,1)S(1)}, bf16[12,32,128]{2,1,0:T(8,128)(2,1)S(1)}, u32[]{:S(2)}, u32[]{:S(2)}) collective-permute-start(bf16[12,32,128]{2,1,0:T(8,128)(2,1)S(1)} %get-tuple-element.48), channel_id=1, source_target_pairs={{0,3},{1,2},{2,1},{3,0},{4,7},{5,6},{6,5},{7,4},{8,11},{9,10},{10,... | collective-permute-start | bytes 294920 | tf_op jit(solution)/shard_map/ppermute | solution.py:483
  23.2 17.6 %copy-start.1 = (bf16[256,64,64]{0,2,1:T(8,128)(2,1)S(1)}, bf16[256,64,64]{0,2,1:T(8,128)(2,1)}, u32[]{:S(2)}) copy-start(bf16[256,64,64]{0,2,1:T(8,128)(2,1)} %param.12) | copy-start | bytes 6291460
  23.2 17.6 %copy-start.2 = (bf16[128,64,64]{0,2,1:T(8,128)(2,1)S(1)}, bf16[128,64,64]{0,2,1:T(8,128)(2,1)}, u32[]{:S(2)}) copy-start(bf16[128,64,64]{0,2,1:T(8,128)(2,1)} %param.15) | copy-start | bytes 3145732
  33.0 17.8 %collective-permute-start.3 = (bf16[51,32,128]{2,1,0:T(8,128)(2,1)S(1)}, bf16[51,32,128]{2,1,0:T(8,128)(2,1)S(1)}, u32[]{:S(2)}, u32[]{:S(2)}) collective-permute-start(bf16[51,32,128]{2,1,0:T(8,128)(2,1)S(1)} %get-tuple-element.58), channel_id=1, source_target_pairs={{0,8},{4,12},{8,0},{12,4},{16,24},{20,28},{24,16},{28,20},{1,9},{5... | collective-permute-start | bytes 1253384 | tf_op jit(solution)/shard_map/ppermute | solution.py:483
  34.6 19.3 %collective-permute-start.4 = (bf16[51,32,128]{2,1,0:T(8,128)(2,1)S(1)}, bf16[51,32,128]{2,1,0:T(8,128)(2,1)S(1)}, u32[]{:S(2)}, u32[]{:S(2)}) collective-permute-start(bf16[51,32,128]{2,1,0:T(8,128)(2,1)S(1)} %get-tuple-element.58), channel_id=1, source_target_pairs={{0,16},{4,20},{8,24},{12,28},{16,0},{20,4},{24,8},{28,12},{1,17},{... | collective-permute-start | bytes 1253384 | tf_op jit(solution)/shard_map/ppermute | solution.py:483
  36.1 17.8 %collective-permute-start.5 = (bf16[51,32,128]{2,1,0:T(8,128)(2,1)S(1)}, bf16[51,32,128]{2,1,0:T(8,128)(2,1)S(1)}, u32[]{:S(2)}, u32[]{:S(2)}) collective-permute-start(bf16[51,32,128]{2,1,0:T(8,128)(2,1)S(1)} %get-tuple-element.58), channel_id=1, source_target_pairs={{0,24},{4,28},{8,16},{12,20},{16,8},{20,12},{24,0},{28,4},{1,25},{... | collective-permute-start | bytes 1253384 | tf_op jit(solution)/shard_map/ppermute | solution.py:483
  36.5 11.1 %collective-permute-start.6 = (bf16[12,80,128]{2,1,0:T(8,128)(2,1)S(1)}, bf16[12,80,128]{2,1,0:T(8,128)(2,1)S(1)}, u32[]{:S(2)}, u32[]{:S(2)}) collective-permute-start(bf16[12,80,128]{2,1,0:T(8,128)(2,1)S(1)} %get-tuple-element.39.refs_0_), channel_id=1, source_target_pairs={{0,1},{1,0},{2,3},{3,2},{4,5},{5,4},{6,7},{7,6},{8,9},{9,8},{10,11... | collective-permute-start | bytes 737288 | tf_op jit(solution)/shard_map/ppermute | solution.py:483
  38.1 12.0 %collective-permute-start.7 = (bf16[12,80,128]{2,1,0:T(8,128)(2,1)S(1)}, bf16[12,80,128]{2,1,0:T(8,128)(2,1)S(1)}, u32[]{:S(2)}, u32[]{:S(2)}) collective-permute-start(bf16[12,80,128]{2,1,0:T(8,128)(2,1)S(1)} %get-tuple-element.39.refs_0_), channel_id=1, source_target_pairs={{0,2},{1,3},{2,0},{3,1},{4,6},{5,7},{6,4},{7,5},{8,10},{9,11},{10,... | collective-permute-start | bytes 737288 | tf_op jit(solution)/shard_map/ppermute | solution.py:483
  45.4 12.1 %copy-start.8 = (s32[256,2]{0,1:T(2,128)S(1)}, s32[256,2]{0,1:T(2,128)}, u32[]{:S(2)}) copy-start(s32[256,2]{0,1:T(2,128)} %param.13) | copy-start | bytes 6148
  45.4 12.2 %copy-start.9 = (s32[128,2]{0,1:T(2,128)S(1)}, s32[128,2]{0,1:T(2,128)}, u32[]{:S(2)}) copy-start(s32[128,2]{0,1:T(2,128)} %param.16) | copy-start | bytes 3076
  47.6 0.7 copy-start.3
  50.0 0.7 copy-start.5
  56.2 6.0 %collective-permute-start.8 = (bf16[204,32,128]{2,1,0:T(8,128)(2,1)}, bf16[204,32,128]{2,1,0:T(8,128)(2,1)}, u32[]{:S(2)}, u32[]{:S(2)}) collective-permute-start(bf16[204,32,128]{2,1,0:T(8,128)(2,1)} %constant_dynamic-update-slice_fusion.4.same_ref), channel_id=1, source_target_pairs={{0,4},{4,0},{8,12},{12,8},{16,20},{20,16},{24,28},{28,24},{1,5},{5... | collective-permute-start | bytes 5013512 | tf_op jit(solution)/shard_map/ppermute | solution.py:483
  57.7 16.9 %collective-permute-start.9 = (bf16[12,80,128]{2,1,0:T(8,128)(2,1)S(1)}, bf16[12,80,128]{2,1,0:T(8,128)(2,1)S(1)}, u32[]{:S(2)}, u32[]{:S(2)}) collective-permute-start(bf16[12,80,128]{2,1,0:T(8,128)(2,1)S(1)} %get-tuple-element.39.refs_0_), channel_id=1, source_target_pairs={{0,3},{1,2},{2,1},{3,0},{4,7},{5,6},{6,5},{7,4},{8,11},{9,10},{10,... | collective-permute-start | bytes 737288 | tf_op jit(solution)/shard_map/ppermute | solution.py:483
  63.1 22.1 %collective-permute-start.10 = (f32[4,32,128]{2,1,0:T(8,128)S(1)}, f32[4,32,128]{2,1,0:T(8,128)S(1)}, u32[]{:S(2)}, u32[]{:S(2)}) collective-permute-start(f32[4,32,128]{2,1,0:T(8,128)S(1)} %add.93.refs_0_), channel_id=1, source_target_pairs={{0,1},{1,0},{2,3},{3,2},{4,5},{5,4},{6,7},{7,6},{8,9},{9,8},{10,11... | collective-permute-start | bytes 196616 | tf_op jit(solution)/shard_map/ppermute | solution.py:483
  63.2 22.1 %collective-permute-start.11 = (f32[4,32,128]{2,1,0:T(8,128)S(1)}, f32[4,32,128]{2,1,0:T(8,128)S(1)}, u32[]{:S(2)}, u32[]{:S(2)}) collective-permute-start(f32[4,32,128]{2,1,0:T(8,128)S(1)} %add.93.refs_0_), channel_id=1, source_target_pairs={{0,2},{1,3},{2,0},{3,1},{4,6},{5,7},{6,4},{7,5},{8,10},{9,11},{10,... | collective-permute-start | bytes 196616 | tf_op jit(solution)/shard_map/ppermute | solution.py:483
  65.2 20.1 %collective-permute-start.12 = (f32[4,32,128]{2,1,0:T(8,128)S(1)}, f32[4,32,128]{2,1,0:T(8,128)S(1)}, u32[]{:S(2)}, u32[]{:S(2)}) collective-permute-start(f32[4,32,128]{2,1,0:T(8,128)S(1)} %add.93.refs_0_), channel_id=1, source_target_pairs={{0,3},{1,2},{2,1},{3,0},{4,7},{5,6},{6,5},{7,4},{8,11},{9,10},{10,... | collective-permute-start | bytes 196616 | tf_op jit(solution)/shard_map/ppermute | solution.py:483
  67.7 7.0 %copy-start.4 = (bf16[12,80,128]{2,1,0:T(8,128)(2,1)S(1)}, bf16[12,80,128]{2,1,0:T(8,128)(2,1)}, u32[]{:S(2)}) copy-start(bf16[12,80,128]{2,1,0:T(8,128)(2,1)} %copy-done.3) | copy-start | bytes 737284
  67.7 7.0 %copy-start.6 = (bf16[12,80,128]{2,1,0:T(8,128)(2,1)S(1)}, bf16[12,80,128]{2,1,0:T(8,128)(2,1)}, u32[]{:S(2)}) copy-start(bf16[12,80,128]{2,1,0:T(8,128)(2,1)} %copy-done.5) | copy-start | bytes 737284
  74.6 10.7 %copy-start.7 = (f32[6,64,64]{2,1,0:T(8,128)S(1)}, f32[6,64,64]{2,1,0:T(8,128)}, u32[]{:S(2)}) copy-start(f32[6,64,64]{2,1,0:T(8,128)} %top_ref.1) | copy-start | bytes 294916

commit v5 on v4

--- a/solution.py
+++ b/solution.py
@@ -66,7 +66,7 @@
     sub = lax.broadcasted_iota(jnp.int32, (8, a.shape[2]), 0)
 
     def cols(block):
-        return pl.ds(pl.multiple_of(8 * block, 8), 8)
+        return pl.ds(8 * block, 8)
 
     for panel in range(K // 8):
         base = 8 * panel
@@ -90,12 +90,10 @@
                 a[base + k, pl.ds(8 * j, 8), :] = new[k]
         if panel < K // 8 - 1:
 
-            @pl.loop(panel + 1, K // 8)
-            def _(i_block):
+            for i_block in range(panel + 1, K // 8):
                 left = [a[base + k, cols(i_block), :] for k in range(8)]
 
-                @pl.loop(i_block, K // 8)
-                def _(j_block):
+                for j_block in range(i_block, K // 8):
                     right = [a[base + k, cols(j_block), :] for k in range(8)]
                     for i in range(8):
                         acc = a[8 * i_block + i, cols(j_block), :]
@@ -170,17 +168,11 @@
     all_basis_ref,
     all_xfer_ref,
     fac_ref,
-    sent_ref,
     gram1_ref,
-    xt,
-    s,
-    a,
-    g0,
-    basis_ref,
-    xfer_ref,
-    basis_sem,
-    sem,
+    *refs,
 ):
+    sent_refs = refs[:cols]
+    xt, s, a, g0, basis_ref, xfer_ref, basis_sem, sem = refs[cols:]
     col = at_ref[1]
     first = col * own
     pairs = min(PAIRS, own // 2)
@@ -222,7 +214,7 @@
         fac_ref[g] = pack([s[4 * g + m] for m in range(4)]).astype(BF)
     for e in range(cols):
         for r in range(count // cols):
-            sent_ref[e, r] = s[r * cols + jnp.bitwise_xor(col, e)].astype(BF)
+            sent_refs[e][r] = s[r * cols + jnp.bitwise_xor(col, e)].astype(BF)
 
 
 def own_factors(at, basis, xfer_lanes, cols):
@@ -231,9 +223,8 @@
     rows = (count + 7) // 8 * 8
     shapes = (
         jax.ShapeDtypeStruct((count // 4, 5 * Q, 2 * K), BF),
-        jax.ShapeDtypeStruct((cols, count // cols, H, 2 * K), BF),
         jax.ShapeDtypeStruct((own // 2, K, K), F32),
-    )
+    ) + (jax.ShapeDtypeStruct((count // cols, H, 2 * K), BF),) * cols
     return pl.pallas_call(
         functools.partial(factor_kernel, own, cols),
         out_shape=shapes,
@@ -266,17 +257,28 @@
     width = own * cols // 2
     while len(grams) > 1:
         here = len(grams)
-        first = offset + col * here
-        grams = lift_pairs(grams, [unhalf(xt[first + c]) for c in range(here)])
+        xfers = [unhalf(xt[offset + col * here + c]) for c in range(here)]
         offset += width
         width //= 2
+        if here < 4:
+            grams = lift_pairs(grams, xfers)
+            continue
+        here //= 2
+        upper = [unhalf(xt[offset + col * here + c]) for c in range(here)]
+        offset += width
+        width //= 2
+        xfers = [mul(upper[c // 2], x, NN) for c, x in enumerate(xfers)]
+        low = lift_pairs(grams, xfers)
+        grams = [x + y for x, y in zip(low[0::2], low[1::2])]
     shift = 0
+    whole = None
     while width >= 1:
-        grams = lift_all(grams, [unhalf(xt[offset + jnp.right_shift(col, shift)])])
+        xfer = unhalf(xt[offset + jnp.right_shift(col, shift)])
+        whole = xfer if whole is None else mul(xfer, whole, NN)
         offset += width
         width //= 2
         shift += 1
-    rest = halve(grams[0])
+    rest = halve(lift_all(grams, [whole])[0])
     for n in range(TERMS):
         term = rest.astype(BF)
         out_ref[n] = term
@@ -384,38 +386,91 @@
     )(*blocks)
 
 
-def middle_kernel(index_ref, cells_ref, same_ref, other_ref, out_ref):
-    entries = same_ref.shape[0]
-
-    @pl.loop(0, cells_ref.shape[0] // SLOTS)
-    def _(step):
-        at = [step * SLOTS + u for u in range(SLOTS)]
-        cols = []
-        for b in at:
-            n = index_ref[b]
-            there = n >= entries
-            n = jnp.where(there, n - entries, n)
-            cols.append(unhalf(jnp.where(there, other_ref[n], same_ref[n])))
-        cells = [unhalf(cells_ref[b]) for b in at]
-        y = [lax.dot_general(x, c, NT, preferred_element_type=F32) for x, c in zip(cells, cols)]
-        y = [halve(z.astype(BF)) for z in y]
-        for b, z in zip(at, y):
-            out_ref[b] = z
-
-
-def middle_products(index, cells, same_core, other_core):
+def join_kernel(inputs, *refs):
+    start = 0
+    for x in refs[:inputs]:
+        refs[inputs][pl.ds(start, x.shape[0])] = x[...]
+        start += x.shape[0]
+    for n, x in enumerate(refs[:inputs] if len(refs) > inputs + 1 else ()):
+        total = x[x.shape[0] - TERMS].astype(F32)
+        for t in range(1, TERMS):
+            total = total + x[x.shape[0] - TERMS + t].astype(F32)
+        refs[inputs + 1][n] = total
+
+
+def joined(pieces, sums=False):
+    entries = sum(x.shape[0] for x in pieces)
+    shapes = [jax.ShapeDtypeStruct((entries, H, 2 * K), BF)]
+    if sums:
+        shapes.append(jax.ShapeDtypeStruct((len(pieces), H, 2 * K), F32))
     return pl.pallas_call(
-        middle_kernel,
+        functools.partial(join_kernel, len(pieces)),
+        out_shape=tuple(shapes),
+        in_specs=[VMEM] * len(pieces),
+        out_specs=(VMEM,) * len(shapes),
+        compiler_params=PARAMS,
+        cost_estimate=cost(0, 2**18),
+    )(*pieces)
+
+
+def bits(size):
+    assert size & (size - 1) == 0
+    return size.bit_length() - 1
+
+
+def row_entry(sizes, at_ref, level, row):
+    own, cols = sizes[:2]
+    size = own >> level
+    row = row - at_ref[0] * (size * cols)
+    owner = jnp.bitwise_xor(jnp.right_shift(row, bits(size)), at_ref[1])
+    return owner * (own + own // 2) + level * own + jnp.bitwise_and(row, size - 1)
+
+
+def column_entry(sizes, at_ref, level, column):
+    own, cols = sizes[:2]
+    size = own >> level
+    count = own + own // 2
+    owner = jnp.right_shift(column, bits(size))
+    away = jnp.bitwise_xor(jnp.right_shift(owner, bits(cols)), at_ref[0])
+    part = jnp.bitwise_xor(jnp.bitwise_and(owner, cols - 1), at_ref[1])
+    entry = jnp.right_shift(away, 1) * (count + TERMS) + part * (count // cols)
+    within = jnp.right_shift(jnp.bitwise_and(column, size - 1), bits(cols))
+    return entry + level * (own // cols) + within, jnp.bitwise_and(away, 1) == 1
+
+
+def middle_kernel(groups, sizes, at_ref, *refs):
+    pairs, (cells_ref, same_ref, other_ref, out_ref) = refs[:-4], refs[-4:]
+    for g, (level, first) in enumerate(groups):
+
+        @pl.loop(0, LANES // SLOTS)
+        def _(step):
+            at = [step * SLOTS + u for u in range(SLOTS)]
+            cols = []
+            for b in at:
+                n, there = column_entry(sizes, at_ref, level, pairs[level][1, first + b])
+                cols.append(unhalf(jnp.where(there, other_ref[n], same_ref[n])))
+            cells = [unhalf(cells_ref[LANES * g + b]) for b in at]
+            y = [lax.dot_general(x, c, NT, preferred_element_type=F32) for x, c in zip(cells, cols)]
+            y = [halve(z.astype(BF)) for z in y]
+            for b, z in zip(at, y):
+                out_ref[LANES * g + b] = z
+
+
+def middle_products(sizes, at, pairs, cells, same_core, other_core):
+    groups = lane_groups([x.shape[1] for x in pairs])
+    return pl.pallas_call(
+        functools.partial(middle_kernel, groups, sizes),
         out_shape=jax.ShapeDtypeStruct(cells.shape, BF),
-        in_specs=[SMEM] + [VMEM] * 3,
+        in_specs=[SMEM] * (1 + len(pairs)) + [VMEM] * 3,
         out_specs=VMEM,
         compiler_params=PARAMS,
         cost_estimate=cost(cells.shape[0] * 2**19, 2**20),
-    )(index, cells, same_core, other_core)
-
-
-def outer_kernel(groups, outs, index_ref, counts_ref, middle_ref, *refs):
-    pieces, out_refs = refs[:-outs - 4], refs[-outs - 4 : -4]
+    )(at, *pairs, cells, same_core, other_core)
+
+
+def outer_kernel(groups, sizes, outs, at_ref, *refs):
+    pairs, counts, middle_ref = refs[:outs], refs[outs : 2 * outs], refs[2 * outs]
+    pieces, out_refs = refs[2 * outs + 1 : -outs - 4], refs[-outs - 4 : -4]
     pt, table, ready, sem = refs[-4:]
     packs = pieces[0].shape[0]
     together = math.gcd(packs, 6)
@@ -435,14 +490,14 @@
         @pl.loop(0, LANES // SLOTS)
         def _(step):
             at = [step * SLOTS + u for u in range(SLOTS)]
-            rows = [table[index_ref[LANES * g + b]] for b in at]
+            rows = [table[row_entry(sizes, at_ref, which, pairs[which][0, first + b])] for b in at]
             right = [unhalf(middle_ref[LANES * g + b]) for b in at]
             y = [lax.dot_general(r, x, NN, preferred_element_type=F32) for r, x in zip(rows, right)]
             y = [halve(z) for z in y]
             for b, z in zip(at, y):
                 pt[b] = z
 
-        keep = lax.broadcasted_iota(jnp.int32, (2 * K, LANES), 1) < counts_ref[which] - first
+        keep = lax.broadcasted_iota(jnp.int32, (2 * K, LANES), 1) < counts[which][0] - first
 
         @pl.loop(0, H // TURN)
         def _(step):
@@ -460,14 +515,15 @@
         copy.wait()
 
 
-def outer_products(pieces, index, counts, middle, sizes):
-    groups = lane_groups(sizes)
+def outer_products(sizes, at, pairs, counts, middle, pieces):
+    slots = [x.shape[1] for x in pairs]
+    groups = lane_groups(slots)
     entries = 4 * sum(x.shape[0] for x in pieces)
     return pl.pallas_call(
-        functools.partial(outer_kernel, groups, len(sizes)),
-        out_shape=tuple(jax.ShapeDtypeStruct((K, K, size), BF) for size in sizes),
-        in_specs=[SMEM, SMEM, VMEM] + [VMEM] * len(pieces),
-        out_specs=(ANY,) * len(sizes),
+        functools.partial(outer_kernel, groups, sizes, len(slots)),
+        out_shape=tuple(jax.ShapeDtypeStruct((K, K, size), BF) for size in slots),
+        in_specs=[SMEM] * (1 + 2 * len(slots)) + [VMEM] * (1 + len(pieces)),
+        out_specs=(ANY,) * len(slots),
         scratch_shapes=[
             pltpu.VMEM((LANES, H, 2 * K), F32),
             pltpu.VMEM((entries, K, K), BF),
@@ -476,7 +532,7 @@
         ],
         compiler_params=PARAMS,
         cost_estimate=cost(len(groups) * 2**26, 2**22),
-    )(index, counts, middle, *pieces)
+    )(at, *pairs, *counts, middle, *pieces)
 
 
 def swapped(x, axis, d):
@@ -487,58 +543,38 @@
     own = basis.shape[0]
     cols = lax.axis_size("col")
     leaves = lax.axis_size("leaf")
-    leaf, col = lax.axis_index("leaf"), lax.axis_index("col")
-    at = jnp.stack([leaf, col]).astype(jnp.int32)
+    at = jnp.stack([lax.axis_index("leaf"), lax.axis_index("col")]).astype(jnp.int32)
     xfer_lanes = jnp.transpose(transfer, (1, 2, 0))
     lanes0, lanes1 = jnp.transpose(blocks0, (1, 2, 0)), jnp.transpose(blocks1, (1, 2, 0))
-    count = own + own // 2
-    parts = count // cols
-
-    def indices(pairs, level):
-        size = own >> level
-        row = pairs[:, 0] - leaf * (size * cols)
-        row = (row // size ^ col) * count + level * own + row % size
-        owner = pairs[:, 1] // size
-        away = owner // cols ^ leaf
-        piece = (away & 1) * (leaves // 2) + (away >> 1)
-        column = piece * (count + TERMS) + (owner % cols ^ col) * parts
-        return row, column + level * (own // cols) + pairs[:, 1] % size // cols
-
-    row0, column0 = indices(pairs0, 0)
-    row1, column1 = indices(pairs1, 1)
-
-    factors, sent, gram1 = own_factors(at, basis, xfer_lanes, cols)
+    sizes = (own, cols)
+    pairs = (jnp.transpose(pairs0), jnp.transpose(pairs1))
+
+    factors, gram1, *sent = own_factors(at, basis, xfer_lanes, cols)
     received = [swapped(sent[d], "col", d) for d in range(1, cols)]
     terms = lifted_root(at, gram1, xfer_lanes, own, cols)
     received, terms, factors, lanes0, lanes1 = lax.optimization_barrier(
         (received, terms, factors, lanes0, lanes1)
     )
 
-    part = jnp.concatenate([sent[0]] + received + [terms], axis=0)
+    (part,) = joined([sent[0]] + received + [terms])
     chips = [swapped(part, "leaf", d) for d in range(2, leaves, 2)]
     row_pieces = [factors] + [swapped(factors, "col", d) for d in range(1, cols - 1)]
     cells = turned_blocks((lanes0, lanes1))
     chips, row_pieces, cells = lax.optimization_barrier((chips, row_pieces, cells))
 
     row_pieces = row_pieces + [swapped(factors, "col", cols - 1)]
-    same_core = jnp.concatenate([part] + chips, axis=0)
+    same_core, pair_part = joined([part] + chips, sums=True)
     other_core = swapped(same_core, "leaf", 1)
-
-    def sums(x):
-        return x.reshape(leaves // 2, count + TERMS, H, 2 * K)[:, count:].astype(F32).sum(axis=1)
-
-    pair_part = sums(same_core) + sums(other_core)
+    there = other_core.reshape(leaves // 2, part.shape[0], H, 2 * K)[:, -TERMS:].astype(F32)
+    other_part = there[:, 0]
+    for t in range(1, TERMS):
+        other_part = other_part + there[:, t]
+    pair_part = pair_part + other_part
     tops = [pair_part] + [swapped(pair_part, "col", d) for d in range(1, cols)]
     ancestors, root = top_factors(at, tops, top_transfer, leaves)
 
-    middle = middle_products(jnp.concatenate([column0, column1]), cells, same_core, other_core)
-    out0, out1 = outer_products(
-        row_pieces,
-        jnp.concatenate([row0, row1]),
-        jnp.concatenate([counts0, counts1]),
-        middle,
-        (blocks0.shape[0], blocks1.shape[0]),
-    )
+    middle = middle_products(sizes, at, pairs, cells, same_core, other_core)
+    out0, out1 = outer_products(sizes, at, pairs, (counts0, counts1), middle, row_pieces)
     return (jnp.transpose(out0, (2, 0, 1)), jnp.transpose(out1, (2, 0, 1)), root, ancestors)
 
 

time: 93.2 us -> 82.3 us (0.88)
  local copies, waits for them, and re-layouts: 7.1 us -> 0.03 us
  Pallas kernels: 52.9 us -> 48.8 us
  waiting for transfers between devices: 7.25 us -> 10.8 us
  other arithmetic: 2.09 us -> 0.11 us
  starting transfers between devices: 21.5 us -> 20.3 us
    unnamed x27 -> x12, local copies, waits for them, and re-layouts: 6.3 us -> 0.03 us
    ppermute x13, waiting for transfers between devices: 7.25 us -> 10.8 us  [swapped(): lax.ppermute(x, axis, [(i, i ^ d) for i in range(lax.axis_size(axis))])]
    reduce_sum x2 -> x0, other arithmetic: 1.83 us -> none  [sums(): x.reshape(leaves // 2, count + TERMS, H, 2 * K)[:, count:].astype(F32)]
    pallas_call x1, Pallas kernels: 16.1 us -> 14.6 us  [own_factors(): pl.pallas_call(functools.partial(factor_kernel, own, cols), out_shape=sha...]
    pallas_call x1, Pallas kernels: 7.72 us -> 6.22 us  [top_factors(): pl.pallas_call(functools.partial(top_kernel, leaves), out_shape=(jax.Shap...]
    ppermute x13, starting transfers between devices: 21.5 us -> 20.3 us  [swapped(): lax.ppermute(x, axis, [(i, i ^ d) for i in range(lax.axis_size(axis))])]
    pallas_call x1, Pallas kernels: 6.95 us -> 5.94 us  [lifted_root(): pl.pallas_call(functools.partial(chain_kernel, own, cols), out_shape=jax....]
    pallas_call x2 -> x4, Pallas kernels: 17.6 us -> 17.4 us  [the longest x1 10.5 us: outer_products(): pl.pallas_call(functools.partial(outer_kernel, groups, sizes, len(slots))...]
  transfers between devices with their start and end apart: 13 -> 13, of which waited for: 5 -> 6; matrix products, arithmetic and copies ran while one was open for 3% -> 0% of each run, Pallas kernels for 31% -> 34%
where the time goes in v5:
time: 82.3 us; the launch traced here: 82.1 us
  Pallas kernels  48.8 us (59%)
  starting transfers between devices  20.3 us (25%)
  waiting for transfers between devices  10.8 us (13%)
  between operations  2.1 us (3%)
    ppermute x13, starting transfers between devices, swapped(): lax.ppermute(x, axis, [(i, i ^ d) for i in range(lax.axis_size(axis))])  20.3 us
    pallas_call x1, Pallas kernels, own_factors(): pl.pallas_call(functools.partial(factor_kernel, own, cols), out_shape=sha...  14.6 us
    ppermute x13, waiting for transfers between devices, swapped(): lax.ppermute(x, axis, [(i, i ^ d) for i in range(lax.axis_size(axis))])  10.8 us
    pallas_call x1, Pallas kernels, outer_products(): pl.pallas_call(functools.partial(outer_kernel, groups, sizes, len(slots))...  10.5 us
    pallas_call x1, Pallas kernels, middle_products(): pl.pallas_call(functools.partial(middle_kernel, groups, sizes), out_shape...  6.8 us
    pallas_call x1, Pallas kernels, top_factors(): pl.pallas_call(functools.partial(top_kernel, leaves), out_shape=(jax.Shap...  6.22 us
    pallas_call x1, Pallas kernels, lifted_root(): pl.pallas_call(functools.partial(chain_kernel, own, cols), out_shape=jax....  5.94 us
    pallas_call x1, Pallas kernels, turned_blocks(): pl.pallas_call(functools.partial(turn_kernel, groups), out_shape=jax.Shap...  4.61 us
  transfers between devices with their start and end apart: 13, of which 6 were waited for; matrix products, arithmetic and copies ran while one was open for 0% of the time, Pallas kernels for 34%

profile of v5, /device:TPU:0, one launch (start us, length us, event | category | flops | bytes accessed | tf_op | source)
XLA Modules:
  0.0 82.1 jit_solution(14518337460423181699)
XLA Ops:
  0.6 0.1 pad_add_fusion.at_ref
  0.7 14.6 %shard_map.120 = (bf16[12,80,128]{2,1,0:T(8,128)(2,1)S(1)}, f32[16,64,64]{2,1,0:T(8,128)S(1)}, bf16[12,32,128]{2,1,0:T(8,128)(2,1)S(1)}, bf16[12,32,128]{2,1,0:T...) custom-call(s32[2]{0:T(128)S(1)} %pad_add_fusion.at_ref, ...), custom_call_target="tpu_custom_call" | custom-call | flops 536870912 | bytes 8388608 | tf_op jit(solution)/shard_map/pallas_call | solution.py:228
  15.3 3.1 %collective-permute-start = (bf16[12,32,128]{2,1,0:T(8,128)(2,1)S(1)}, bf16[12,32,128]{2,1,0:T(8,128)(2,1)S(1)}, u32[]{:S(2)}, u32[]{:S(2)}) collective-permute-start(bf16[12,32,128]{2,1,0:T(8,128)(2,1)S(1)} %get-tuple-element.31), channel_id=1, source_target_pairs={{0,1},{1,0},{2,3},{3,2},{4,5},{5,4},{6,7},{7,6},{8,9},{9,8},{10,11... | collective-permute-start | bytes 294920 | tf_op jit(solution)/shard_map/ppermute | solution.py:539
  18.4 2.6 %collective-permute-start.1 = (bf16[12,32,128]{2,1,0:T(8,128)(2,1)S(1)}, bf16[12,32,128]{2,1,0:T(8,128)(2,1)S(1)}, u32[]{:S(2)}, u32[]{:S(2)}) collective-permute-start(bf16[12,32,128]{2,1,0:T(8,128)(2,1)S(1)} %get-tuple-element.32), channel_id=1, source_target_pairs={{0,2},{1,3},{2,0},{3,1},{4,6},{5,7},{6,4},{7,5},{8,10},{9,11},{10,... | collective-permute-start | bytes 294920 | tf_op jit(solution)/shard_map/ppermute | solution.py:539
  21.0 5.9 %shard_map.121.refs_4_ = bf16[3,32,128]{2,1,0:T(8,128)(2,1)S(1)} custom-call(s32[2]{0:T(128)S(1)} %pad_add_fusion.at_ref, f32[16,64,64]{2,1,0:T(8,128)S(1)} %get-tuple-element.34.gram1_ref, f32[64,64,255]{2,1,0:T(8,128)S(1)} %bitcast.15), custom_call_target="tpu_custom_call" | custom-call | flops 536870912 | bytes 4194304 | tf_op jit(solution)/shard_map/pallas_call | solution.py:289
  26.9 0.1 collective-permute-done.refs_1_
  27.0 1.8 %collective-permute-done.1.refs_2_ = bf16[12,32,128]{2,1,0:T(8,128)(2,1)S(1)} collective-permute-done((bf16[12,32,128]{2,1,0:T(8,128)(2,1)S(1)}, bf16[12,32,128]{2,1,0:T(8,128)(2,1)S(1)}, u32[]{:S(2)}, u32[]{:S(2)}) %collective-permute-start.1) | collective-permute-done | bytes 98336 | tf_op jit(solution)/shard_map/ppermute | solution.py:539
  28.8 0.0 collective-permute-done.2.refs_3_
  28.9 1.6 %collective-permute-start.3 = (bf16[51,32,128]{2,1,0:T(8,128)(2,1)S(1)}, bf16[51,32,128]{2,1,0:T(8,128)(2,1)S(1)}, u32[]{:S(2)}, u32[]{:S(2)}) collective-permute-start(bf16[51,32,128]{2,1,0:T(8,128)(2,1)S(1)} %shard_map.122.refs_0_), channel_id=1, source_target_pairs={{0,8},{4,12},{8,0},{12,4},{16,24},{20,28},{24,16},{28,20},{1,9},{5... | collective-permute-start | bytes 1253384 | tf_op jit(solution)/shard_map/ppermute | solution.py:539
  30.4 1.5 %collective-permute-start.4 = (bf16[51,32,128]{2,1,0:T(8,128)(2,1)S(1)}, bf16[51,32,128]{2,1,0:T(8,128)(2,1)S(1)}, u32[]{:S(2)}, u32[]{:S(2)}) collective-permute-start(bf16[51,32,128]{2,1,0:T(8,128)(2,1)S(1)} %shard_map.122.refs_0_), channel_id=1, source_target_pairs={{0,16},{4,20},{8,24},{12,28},{16,0},{20,4},{24,8},{28,12},{1,17},{... | collective-permute-start | bytes 1253384 | tf_op jit(solution)/shard_map/ppermute | solution.py:539
  31.9 0.5 collective-permute-start.5
  32.4 1.6 %collective-permute-start.6 = (bf16[12,80,128]{2,1,0:T(8,128)(2,1)S(1)}, bf16[12,80,128]{2,1,0:T(8,128)(2,1)S(1)}, u32[]{:S(2)}, u32[]{:S(2)}) collective-permute-start(bf16[12,80,128]{2,1,0:T(8,128)(2,1)S(1)} %get-tuple-element.48.refs_5_), channel_id=1, source_target_pairs={{0,1},{1,0},{2,3},{3,2},{4,5},{5,4},{6,7},{7,6},{8,9},{9,8},{10,11... | collective-permute-start | bytes 737288 | tf_op jit(solution)/shard_map/ppermute | solution.py:539
  34.0 1.4 %collective-permute-start.7 = (bf16[12,80,128]{2,1,0:T(8,128)(2,1)S(1)}, bf16[12,80,128]{2,1,0:T(8,128)(2,1)S(1)}, u32[]{:S(2)}, u32[]{:S(2)}) collective-permute-start(bf16[12,80,128]{2,1,0:T(8,128)(2,1)S(1)} %get-tuple-element.48.refs_5_), channel_id=1, source_target_pairs={{0,2},{1,3},{2,0},{3,1},{4,6},{5,7},{6,4},{7,5},{8,10},{9,11},{10,... | collective-permute-start | bytes 737288 | tf_op jit(solution)/shard_map/ppermute | solution.py:539
  35.4 4.6 %shard_map.123.refs_2_ = bf16[384,32,128]{2,1,0:T(8,128)(2,1)S(1)} custom-call(bf16[64,64,256]{2,1,0:T(8,128)(2,1)S(1)} %bitcast.16, bf16[64,64,128]{2,1,0:T(8,128)(2,1)S(1)} %bitcast.18), custom_call_target="tpu_custom_call" | custom-call | flops 1048576 | bytes 1048576 | tf_op jit(solution)/shard_map/pallas_call | solution.py:378
  40.1 0.0 copy-start.4
  40.1 0.0 copy-start.5
  40.1 3.0 %collective-permute-done.6.refs_6_ = bf16[12,80,128]{2,1,0:T(8,128)(2,1)S(1)} collective-permute-done((bf16[12,80,128]{2,1,0:T(8,128)(2,1)S(1)}, bf16[12,80,128]{2,1,0:T(8,128)(2,1)S(1)}, u32[]{:S(2)}, u32[]{:S(2)}) %collective-permute-start.6) | collective-permute-done | bytes 245792 | tf_op jit(solution)/shard_map/ppermute | solution.py:539
  43.1 2.6 %collective-permute-done.7.refs_7_ = bf16[12,80,128]{2,1,0:T(8,128)(2,1)S(1)} collective-permute-done((bf16[12,80,128]{2,1,0:T(8,128)(2,1)S(1)}, bf16[12,80,128]{2,1,0:T(8,128)(2,1)S(1)}, u32[]{:S(2)}, u32[]{:S(2)}) %collective-permute-start.7) | collective-permute-done | bytes 245792 | tf_op jit(solution)/shard_map/ppermute | solution.py:539
  45.6 0.0 collective-permute-done.3.refs_1_
  45.7 2.9 %collective-permute-done.4.refs_2_ = bf16[51,32,128]{2,1,0:T(8,128)(2,1)S(1)} collective-permute-done((bf16[51,32,128]{2,1,0:T(8,128)(2,1)S(1)}, bf16[51,32,128]{2,1,0:T(8,128)(2,1)S(1)}, u32[]{:S(2)}, u32[]{:S(2)}) %collective-permute-start.4) | collective-permute-done | bytes 417824 | tf_op jit(solution)/shard_map/ppermute | solution.py:539
  48.6 0.0 collective-permute-done.5.refs_3_
  48.6 0.1 shard_map.124
  48.7 0.1 collective-permute-start.8
  48.8 3.1 %collective-permute-start.9 = (bf16[12,80,128]{2,1,0:T(8,128)(2,1)S(1)}, bf16[12,80,128]{2,1,0:T(8,128)(2,1)S(1)}, u32[]{:S(2)}, u32[]{:S(2)}) collective-permute-start(bf16[12,80,128]{2,1,0:T(8,128)(2,1)S(1)} %get-tuple-element.48.refs_5_), channel_id=1, source_target_pairs={{0,3},{1,2},{2,1},{3,0},{4,7},{5,6},{6,5},{7,4},{8,11},{9,10},{10,... | collective-permute-start | bytes 737288 | tf_op jit(solution)/shard_map/ppermute | solution.py:539
  51.9 0.4 collective-permute-done.8.refs_4_
  52.4 2.4 %collective-permute-start.10 = (f32[4,32,128]{2,1,0:T(8,128)S(1)}, f32[4,32,128]{2,1,0:T(8,128)S(1)}, u32[]{:S(2)}, u32[]{:S(2)}) collective-permute-start(f32[4,32,128]{2,1,0:T(8,128)S(1)} %fusion.1.refs_0_), channel_id=1, source_target_pairs={{0,1},{1,0},{2,3},{3,2},{4,5},{5,4},{6,7},{7,6},{8,9},{9,8},{10,11... | collective-permute-start | bytes 196616 | tf_op jit(solution)/shard_map/ppermute | solution.py:539
  54.8 1.3 %collective-permute-start.11 = (f32[4,32,128]{2,1,0:T(8,128)S(1)}, f32[4,32,128]{2,1,0:T(8,128)S(1)}, u32[]{:S(2)}, u32[]{:S(2)}) collective-permute-start(f32[4,32,128]{2,1,0:T(8,128)S(1)} %fusion.1.refs_0_), channel_id=1, source_target_pairs={{0,2},{1,3},{2,0},{3,1},{4,6},{5,7},{6,4},{7,5},{8,10},{9,11},{10,... | collective-permute-start | bytes 196616 | tf_op jit(solution)/shard_map/ppermute | solution.py:539
  56.1 1.1 %collective-permute-start.12 = (f32[4,32,128]{2,1,0:T(8,128)S(1)}, f32[4,32,128]{2,1,0:T(8,128)S(1)}, u32[]{:S(2)}, u32[]{:S(2)}) collective-permute-start(f32[4,32,128]{2,1,0:T(8,128)S(1)} %fusion.1.refs_0_), channel_id=1, source_target_pairs={{0,3},{1,2},{2,1},{3,0},{4,7},{5,6},{6,5},{7,4},{8,11},{9,10},{10,... | collective-permute-start | bytes 196616 | tf_op jit(solution)/shard_map/ppermute | solution.py:539
  58.5 6.8 %shard_map.125.refs_4_ = bf16[384,32,128]{2,1,0:T(8,128)(2,1)S(1)} custom-call(s32[2]{0:T(128)S(1)} %pad_add_fusion.at_ref, s32[2,256]{1,0:T(2,128)S(1)} %bitcast.19, s32[2,128]{1,0:T(2,128)S(1)} %bitcast.21, bf16[384,32,128]{2,1,0:T(8,128)(2,1)S(1)} %shard_map.123.refs_2_, bf16[204,32,128]{2,1,0:T(8,128)(2,1)S(1)} %get-tuple-element.47.refs_3_, ...), custom_call_target="tpu_custom_call" | custom-call | flops 201326592 | bytes 1048576 | tf_op jit(solution)/shard_map/pallas_call | solution.py:461
  65.4 10.5 %shard_map.126 = (bf16[64,64,256]{2,1,0:T(8,128)(2,1)}, bf16[64,64,128]{2,1,0:T(8,128)(2,1)}) custom-call(s32[2]{0:T(128)S(1)} %pad_add_fusion.at_ref, s32[2,256]{1,0:T(2,128)S(1)} %bitcast.20, s32[2,128]{1,0:T(2,128)S(1)} %bitcast.22, s32[1]{0:T(128)S(6)} %copy.16.refs_2_, s32[1]{0:T(128)S(6)} %copy.17.refs_3_, ...), custom_call_target="tpu_custom_call" | custom-call | flops 201326592 | bytes 4194304 | tf_op jit(solution)/shard_map/pallas_call | solution.py:522
  75.9 0.0 collective-permute-done.10.refs_1_
  75.9 6.2 %shard_map.127 = (f32[1,3,64,64]{3,2,1,0:T(8,128)}, f32[64,64]{1,0:T(8,128)}) custom-call(s32[2]{0:T(128)S(1)} %pad_add_fusion.at_ref, f32[6,64,64]{2,1,0:T(8,128)S(1)} %copy-done.3, f32[4,32,128]{2,1,0:T(8,128)S(1)} %fusion.1.refs_0_, f32[4,32,128]{2,1,0:T(8,128)S(1)} %collective-permute-done.10.refs_1_, f32[4,32,128]{2,1,0:T(8,128)S(1)} %collective-permute-done.11.refs_2_, ...), custom_call_target="tpu_custom_call" | custom-call | flops 4194304 | bytes 131072 | tf_op jit(solution)/shard_map/pallas_call | solution.py:337
  (17 shorter events, 0.1 us)
Async XLA Ops:
  0.7 20.3 %copy-start = (f32[255,64,64]{0,2,1:T(8,128)S(1)}, f32[255,64,64]{0,2,1:T(8,128)}, u32[]{:S(2)}) copy-start(f32[255,64,64]{0,2,1:T(8,128)} %param.10) | copy-start | bytes 12533764
  15.3 11.7 %collective-permute-start = (bf16[12,32,128]{2,1,0:T(8,128)(2,1)S(1)}, bf16[12,32,128]{2,1,0:T(8,128)(2,1)S(1)}, u32[]{:S(2)}, u32[]{:S(2)}) collective-permute-start(bf16[12,32,128]{2,1,0:T(8,128)(2,1)S(1)} %get-tuple-element.31), channel_id=1, source_target_pairs={{0,1},{1,0},{2,3},{3,2},{4,5},{5,4},{6,7},{7,6},{8,9},{9,8},{10,11... | collective-permute-start | bytes 294920 | tf_op jit(solution)/shard_map/ppermute | solution.py:539
  18.4 10.4 %collective-permute-start.1 = (bf16[12,32,128]{2,1,0:T(8,128)(2,1)S(1)}, bf16[12,32,128]{2,1,0:T(8,128)(2,1)S(1)}, u32[]{:S(2)}, u32[]{:S(2)}) collective-permute-start(bf16[12,32,128]{2,1,0:T(8,128)(2,1)S(1)} %get-tuple-element.32), channel_id=1, source_target_pairs={{0,2},{1,3},{2,0},{3,1},{4,6},{5,7},{6,4},{7,5},{8,10},{9,11},{10,... | collective-permute-start | bytes 294920 | tf_op jit(solution)/shard_map/ppermute | solution.py:539
  21.0 7.8 %collective-permute-start.2 = (bf16[12,32,128]{2,1,0:T(8,128)(2,1)S(1)}, bf16[12,32,128]{2,1,0:T(8,128)(2,1)S(1)}, u32[]{:S(2)}, u32[]{:S(2)}) collective-permute-start(bf16[12,32,128]{2,1,0:T(8,128)(2,1)S(1)} %get-tuple-element.33), channel_id=1, source_target_pairs={{0,3},{1,2},{2,1},{3,0},{4,7},{5,6},{6,5},{7,4},{8,11},{9,10},{10,... | collective-permute-start | bytes 294920 | tf_op jit(solution)/shard_map/ppermute | solution.py:539
  21.0 14.4 %copy-start.1 = (bf16[256,64,64]{0,2,1:T(8,128)(2,1)S(1)}, bf16[256,64,64]{0,2,1:T(8,128)(2,1)}, u32[]{:S(2)}) copy-start(bf16[256,64,64]{0,2,1:T(8,128)(2,1)} %param.12) | copy-start | bytes 6291460
  21.0 14.5 %copy-start.2 = (bf16[128,64,64]{0,2,1:T(8,128)(2,1)S(1)}, bf16[128,64,64]{0,2,1:T(8,128)(2,1)}, u32[]{:S(2)}) copy-start(bf16[128,64,64]{0,2,1:T(8,128)(2,1)} %param.15) | copy-start | bytes 3145732
  28.9 16.8 %collective-permute-start.3 = (bf16[51,32,128]{2,1,0:T(8,128)(2,1)S(1)}, bf16[51,32,128]{2,1,0:T(8,128)(2,1)S(1)}, u32[]{:S(2)}, u32[]{:S(2)}) collective-permute-start(bf16[51,32,128]{2,1,0:T(8,128)(2,1)S(1)} %shard_map.122.refs_0_), channel_id=1, source_target_pairs={{0,8},{4,12},{8,0},{12,4},{16,24},{20,28},{24,16},{28,20},{1,9},{5... | collective-permute-start | bytes 1253384 | tf_op jit(solution)/shard_map/ppermute | solution.py:539
  30.4 18.2 %collective-permute-start.4 = (bf16[51,32,128]{2,1,0:T(8,128)(2,1)S(1)}, bf16[51,32,128]{2,1,0:T(8,128)(2,1)S(1)}, u32[]{:S(2)}, u32[]{:S(2)}) collective-permute-start(bf16[51,32,128]{2,1,0:T(8,128)(2,1)S(1)} %shard_map.122.refs_0_), channel_id=1, source_target_pairs={{0,16},{4,20},{8,24},{12,28},{16,0},{20,4},{24,8},{28,12},{1,17},{... | collective-permute-start | bytes 1253384 | tf_op jit(solution)/shard_map/ppermute | solution.py:539
  31.9 16.7 %collective-permute-start.5 = (bf16[51,32,128]{2,1,0:T(8,128)(2,1)S(1)}, bf16[51,32,128]{2,1,0:T(8,128)(2,1)S(1)}, u32[]{:S(2)}, u32[]{:S(2)}) collective-permute-start(bf16[51,32,128]{2,1,0:T(8,128)(2,1)S(1)} %shard_map.122.refs_0_), channel_id=1, source_target_pairs={{0,24},{4,28},{8,16},{12,20},{16,8},{20,12},{24,0},{28,4},{1,25},{... | collective-permute-start | bytes 1253384 | tf_op jit(solution)/shard_map/ppermute | solution.py:539
  32.4 10.7 %collective-permute-start.6 = (bf16[12,80,128]{2,1,0:T(8,128)(2,1)S(1)}, bf16[12,80,128]{2,1,0:T(8,128)(2,1)S(1)}, u32[]{:S(2)}, u32[]{:S(2)}) collective-permute-start(bf16[12,80,128]{2,1,0:T(8,128)(2,1)S(1)} %get-tuple-element.48.refs_5_), channel_id=1, source_target_pairs={{0,1},{1,0},{2,3},{3,2},{4,5},{5,4},{6,7},{7,6},{8,9},{9,8},{10,11... | collective-permute-start | bytes 737288 | tf_op jit(solution)/shard_map/ppermute | solution.py:539
  34.0 11.6 %collective-permute-start.7 = (bf16[12,80,128]{2,1,0:T(8,128)(2,1)S(1)}, bf16[12,80,128]{2,1,0:T(8,128)(2,1)S(1)}, u32[]{:S(2)}, u32[]{:S(2)}) collective-permute-start(bf16[12,80,128]{2,1,0:T(8,128)(2,1)S(1)} %get-tuple-element.48.refs_5_), channel_id=1, source_target_pairs={{0,2},{1,3},{2,0},{3,1},{4,6},{5,7},{6,4},{7,5},{8,10},{9,11},{10,... | collective-permute-start | bytes 737288 | tf_op jit(solution)/shard_map/ppermute | solution.py:539
  40.1 18.5 %copy-start.4 = (s32[256,2]{0,1:T(2,128)S(1)}, s32[256,2]{0,1:T(2,128)}, u32[]{:S(2)}) copy-start(s32[256,2]{0,1:T(2,128)} %param.13) | copy-start | bytes 6148
  40.1 18.5 %copy-start.5 = (s32[128,2]{0,1:T(2,128)S(1)}, s32[128,2]{0,1:T(2,128)}, u32[]{:S(2)}) copy-start(s32[128,2]{0,1:T(2,128)} %param.16) | copy-start | bytes 3076
  48.7 3.6 %collective-permute-start.8 = (bf16[204,32,128]{2,1,0:T(8,128)(2,1)S(1)}, bf16[204,32,128]{2,1,0:T(8,128)(2,1)S(1)}, u32[]{:S(2)}, u32[]{:S(2)}) collective-permute-start(bf16[204,32,128]{2,1,0:T(8,128)(2,1)S(1)} %get-tuple-element.47.refs_3_), channel_id=1, source_target_pairs={{0,4},{4,0},{8,12},{12,8},{16,20},{20,16},{24,28},{28,24},{1,5},{5... | collective-permute-start | bytes 5013512 | tf_op jit(solution)/shard_map/ppermute | solution.py:539
  48.8 16.6 %collective-permute-start.9 = (bf16[12,80,128]{2,1,0:T(8,128)(2,1)S(1)}, bf16[12,80,128]{2,1,0:T(8,128)(2,1)S(1)}, u32[]{:S(2)}, u32[]{:S(2)}) collective-permute-start(bf16[12,80,128]{2,1,0:T(8,128)(2,1)S(1)} %get-tuple-element.48.refs_5_), channel_id=1, source_target_pairs={{0,3},{1,2},{2,1},{3,0},{4,7},{5,6},{6,5},{7,4},{8,11},{9,10},{10,... | collective-permute-start | bytes 737288 | tf_op jit(solution)/shard_map/ppermute | solution.py:539
  52.4 23.5 %collective-permute-start.10 = (f32[4,32,128]{2,1,0:T(8,128)S(1)}, f32[4,32,128]{2,1,0:T(8,128)S(1)}, u32[]{:S(2)}, u32[]{:S(2)}) collective-permute-start(f32[4,32,128]{2,1,0:T(8,128)S(1)} %fusion.1.refs_0_), channel_id=1, source_target_pairs={{0,1},{1,0},{2,3},{3,2},{4,5},{5,4},{6,7},{7,6},{8,9},{9,8},{10,11... | collective-permute-start | bytes 196616 | tf_op jit(solution)/shard_map/ppermute | solution.py:539
  54.8 21.1 %collective-permute-start.11 = (f32[4,32,128]{2,1,0:T(8,128)S(1)}, f32[4,32,128]{2,1,0:T(8,128)S(1)}, u32[]{:S(2)}, u32[]{:S(2)}) collective-permute-start(f32[4,32,128]{2,1,0:T(8,128)S(1)} %fusion.1.refs_0_), channel_id=1, source_target_pairs={{0,2},{1,3},{2,0},{3,1},{4,6},{5,7},{6,4},{7,5},{8,10},{9,11},{10,... | collective-permute-start | bytes 196616 | tf_op jit(solution)/shard_map/ppermute | solution.py:539
  56.1 19.8 %collective-permute-start.12 = (f32[4,32,128]{2,1,0:T(8,128)S(1)}, f32[4,32,128]{2,1,0:T(8,128)S(1)}, u32[]{:S(2)}, u32[]{:S(2)}) collective-permute-start(f32[4,32,128]{2,1,0:T(8,128)S(1)} %fusion.1.refs_0_), channel_id=1, source_target_pairs={{0,3},{1,2},{2,1},{3,0},{4,7},{5,6},{6,5},{7,4},{8,11},{9,10},{10,... | collective-permute-start | bytes 196616 | tf_op jit(solution)/shard_map/ppermute | solution.py:539
  65.3 10.6 %copy-start.3 = (f32[6,64,64]{2,1,0:T(8,128)S(1)}, f32[6,64,64]{2,1,0:T(8,128)}, u32[]{:S(2)}) copy-start(f32[6,64,64]{2,1,0:T(8,128)} %top_ref.1) | copy-start | bytes 294916

commit v6 on v5

--- a/solution.py
+++ b/solution.py
@@ -23,7 +23,7 @@
 TERMS = 3
 TURN = 8
 SLOTS = 64
-PAIRS = 4
+PAIRS = 8
 PARAMS = pltpu.CompilerParams(vmem_limit_bytes=24 * 2**20)
 
 
@@ -35,8 +35,22 @@
     return jnp.concatenate([x[:H], x[H:]], axis=1)
 
 
+def bf16_terms(x):
+    high = x.astype(BF)
+    rest = x - high.astype(F32)
+    mid = rest.astype(BF)
+    return high, mid, (rest - mid.astype(F32)).astype(BF)
+
+
 def mul(x, y, dims):
-    return lax.dot_general(x, y, dims, precision=EXACT, preferred_element_type=F32)
+    if x.shape[1] != K:
+        return lax.dot_general(x, y, dims, precision=EXACT, preferred_element_type=F32)
+    h, m, l = bf16_terms(x)
+    p, q, r = bf16_terms(y)
+    axis = dims[0][1][0]
+    dot = functools.partial(lax.dot_general, dimension_numbers=dims, preferred_element_type=F32)
+    main = dot(jnp.concatenate([h, h, m, m], axis=1), jnp.concatenate([p, q, p, q], axis=axis))
+    return main + dot(jnp.concatenate([h, l], axis=1), jnp.concatenate([r, p], axis=axis))
 
 
 def lift_all(grams, xfers_t):
@@ -124,6 +138,14 @@
             s[:, q, :] = y
 
 
+def packed(matrices):
+    return matrices % 4 == 0
+
+
+def slabs(matrices):
+    return matrices // 4 * 5 if packed(matrices) else 2 * matrices
+
+
 def lane(low, high):
     at = lax.broadcasted_iota(jnp.int32, (Q, 2 * K), 1)
     return (at >= low) & (at < high)
@@ -145,8 +167,7 @@
     )
 
 
-def unpack(x):
-    unit = [x[Q * n : Q * (n + 1)] for n in range(5)]
+def unpack(unit):
     full = []
     for m in range(3):
         full.append((unit[m], jnp.where(lane(H, K), pltpu.roll(unit[m], K, 1), 0.0)))
@@ -213,8 +234,12 @@
     for g in range(count // 4):
         fac_ref[g] = pack([s[4 * g + m] for m in range(4)]).astype(BF)
     for e in range(cols):
-        for r in range(count // cols):
-            sent_refs[e][r] = s[r * cols + jnp.bitwise_xor(col, e)].astype(BF)
+        mine = [s[r * cols + jnp.bitwise_xor(col, e)] for r in range(count // cols)]
+        start = 0
+        for x in [pack(mine[n : n + 4]) for n in range(0, len(mine), 4)] if packed(len(mine)) else mine:
+            for n in range(x.shape[0] // Q):
+                sent_refs[e][start + n] = x[Q * n : Q * (n + 1)].astype(BF)
+            start += x.shape[0] // Q
 
 
 def own_factors(at, basis, xfer_lanes, cols):
@@ -224,7 +249,7 @@
     shapes = (
         jax.ShapeDtypeStruct((count // 4, 5 * Q, 2 * K), BF),
         jax.ShapeDtypeStruct((own // 2, K, K), F32),
-    ) + (jax.ShapeDtypeStruct((count // cols, H, 2 * K), BF),) * cols
+    ) + (jax.ShapeDtypeStruct((slabs(count // cols), Q, 2 * K), BF),) * cols
     return pl.pallas_call(
         functools.partial(factor_kernel, own, cols),
         out_shape=shapes,
@@ -281,21 +306,22 @@
     rest = halve(lift_all(grams, [whole])[0])
     for n in range(TERMS):
         term = rest.astype(BF)
-        out_ref[n] = term
+        out_ref[2 * n] = term[:Q]
+        out_ref[2 * n + 1] = term[Q:]
         rest = rest - term.astype(F32)
 
 
 def lifted_root(at, gram1, xfer_lanes, own, cols):
     return pl.pallas_call(
         functools.partial(chain_kernel, own, cols),
-        out_shape=jax.ShapeDtypeStruct((TERMS, H, 2 * K), BF),
+        out_shape=jax.ShapeDtypeStruct((2 * TERMS, Q, 2 * K), BF),
         grid=(1,),
         in_specs=[
             SMEM,
             pl.BlockSpec(gram1.shape, lambda i: (0, 0, 0)),
             pl.BlockSpec((K, K, LANES), lambda i: (0, 0, 1)),
         ],
-        out_specs=pl.BlockSpec((TERMS, H, 2 * K), lambda i: (0, 0, 0)),
+        out_specs=pl.BlockSpec((2 * TERMS, Q, 2 * K), lambda i: (0, 0, 0)),
         scratch_shapes=[pltpu.VMEM((LANES, H, 2 * K), F32)],
         compiler_params=PARAMS,
         cost_estimate=cost(own * 2**24, 2**22),
@@ -307,7 +333,7 @@
     parts, (anc_ref, root_ref, level_ref, s, a) = refs[:-5], refs[-5:]
     pair = jnp.right_shift(at_ref[0], 1)
     for m in range(pairs):
-        terms = [part[m] for part in parts]
+        terms = [part[m].reshape(H, 2 * K) for part in parts]
         while len(terms) > 1:
             terms = [x + y for x, y in zip(terms[0::2], terms[1::2])]
         level_ref[jnp.bitwise_xor(pair, m)] = terms[0]
@@ -392,17 +418,18 @@
         refs[inputs][pl.ds(start, x.shape[0])] = x[...]
         start += x.shape[0]
     for n, x in enumerate(refs[:inputs] if len(refs) > inputs + 1 else ()):
-        total = x[x.shape[0] - TERMS].astype(F32)
+        last = x.shape[0] - 2 * TERMS
+        total = x[last : last + 2].astype(F32)
         for t in range(1, TERMS):
-            total = total + x[x.shape[0] - TERMS + t].astype(F32)
+            total = total + x[last + 2 * t : last + 2 * t + 2].astype(F32)
         refs[inputs + 1][n] = total
 
 
 def joined(pieces, sums=False):
     entries = sum(x.shape[0] for x in pieces)
-    shapes = [jax.ShapeDtypeStruct((entries, H, 2 * K), BF)]
+    shapes = [jax.ShapeDtypeStruct((entries, Q, 2 * K), BF)]
     if sums:
-        shapes.append(jax.ShapeDtypeStruct((len(pieces), H, 2 * K), F32))
+        shapes.append(jax.ShapeDtypeStruct((len(pieces), 2, Q, 2 * K), F32))
     return pl.pallas_call(
         functools.partial(join_kernel, len(pieces)),
         out_shape=tuple(shapes),
@@ -427,28 +454,51 @@
 
 
 def column_entry(sizes, at_ref, level, column):
-    own, cols = sizes[:2]
+    own, cols, leaves = sizes
     size = own >> level
     count = own + own // 2
     owner = jnp.right_shift(column, bits(size))
     away = jnp.bitwise_xor(jnp.right_shift(owner, bits(cols)), at_ref[0])
     part = jnp.bitwise_xor(jnp.bitwise_and(owner, cols - 1), at_ref[1])
-    entry = jnp.right_shift(away, 1) * (count + TERMS) + part * (count // cols)
+    piece = jnp.bitwise_and(away, 1) * (leaves // 2) + jnp.right_shift(away, 1)
+    entry = piece * count + part * (count // cols)
     within = jnp.right_shift(jnp.bitwise_and(column, size - 1), bits(cols))
-    return entry + level * (own // cols) + within, jnp.bitwise_and(away, 1) == 1
+    return entry + level * (own // cols) + within
+
+
+def fill_column_table(table, start, ref, sizes):
+    own, cols, leaves = sizes
+    count = own + own // 2
+    parts = count // cols
+    step = slabs(parts)
+    length = ref.shape[0] // (leaves // 2)
+
+    @pl.loop(0, leaves // 2)
+    def _(p):
+        found = []
+        for e in range(cols):
+            first = p * length + e * step
+            if packed(parts):
+                for g in range(parts // 4):
+                    found += unpack([ref[first + 5 * g + n].astype(F32) for n in range(5)])
+            else:
+                for r in range(parts):
+                    two = [ref[first + 2 * r + n] for n in range(2)]
+                    found.append(unhalf(jnp.concatenate(two, axis=0)))
+        for n, x in enumerate(found):
+            table[start + p * count + n] = x.astype(BF)
 
 
 def middle_kernel(groups, sizes, at_ref, *refs):
-    pairs, (cells_ref, same_ref, other_ref, out_ref) = refs[:-4], refs[-4:]
+    pairs, (cells_ref, same_ref, other_ref, out_ref, table) = refs[:-5], refs[-5:]
+    fill_column_table(table, 0, same_ref, sizes)
+    fill_column_table(table, table.shape[0] // 2, other_ref, sizes)
     for g, (level, first) in enumerate(groups):
 
         @pl.loop(0, LANES // SLOTS)
         def _(step):
             at = [step * SLOTS + u for u in range(SLOTS)]
-            cols = []
-            for b in at:
-                n, there = column_entry(sizes, at_ref, level, pairs[level][1, first + b])
-                cols.append(unhalf(jnp.where(there, other_ref[n], same_ref[n])))
+            cols = [table[column_entry(sizes, at_ref, level, pairs[level][1, first + b])] for b in at]
             cells = [unhalf(cells_ref[LANES * g + b]) for b in at]
             y = [lax.dot_general(x, c, NT, preferred_element_type=F32) for x, c in zip(cells, cols)]
             y = [halve(z.astype(BF)) for z in y]
@@ -463,7 +513,8 @@
         out_shape=jax.ShapeDtypeStruct(cells.shape, BF),
         in_specs=[SMEM] * (1 + len(pairs)) + [VMEM] * 3,
         out_specs=VMEM,
-        compiler_params=PARAMS,
+        scratch_shapes=[pltpu.VMEM((sizes[2] * (sizes[0] + sizes[0] // 2), K, K), BF)],
+        compiler_params=pltpu.CompilerParams(vmem_limit_bytes=36 * 2**20),
         cost_estimate=cost(cells.shape[0] * 2**19, 2**20),
     )(at, *pairs, cells, same_core, other_core)
 
@@ -479,7 +530,7 @@
         @pl.loop(0, packs // together)
         def _(step):
             at = [step * together + g for g in range(together)]
-            full = [unpack(piece[g].astype(F32)) for g in at]
+            full = [unpack([piece[g, Q * n : Q * (n + 1)].astype(F32) for n in range(5)]) for g in at]
             for g, four in zip(at, full):
                 for m in range(4):
                     table[4 * (e * packs + g) + m] = four[m].astype(BF)
@@ -546,7 +597,7 @@
     at = jnp.stack([lax.axis_index("leaf"), lax.axis_index("col")]).astype(jnp.int32)
     xfer_lanes = jnp.transpose(transfer, (1, 2, 0))
     lanes0, lanes1 = jnp.transpose(blocks0, (1, 2, 0)), jnp.transpose(blocks1, (1, 2, 0))
-    sizes = (own, cols)
+    sizes = (own, cols, leaves)
     pairs = (jnp.transpose(pairs0), jnp.transpose(pairs1))
 
     factors, gram1, *sent = own_factors(at, basis, xfer_lanes, cols)
@@ -558,17 +609,18 @@
 
     (part,) = joined([sent[0]] + received + [terms])
     chips = [swapped(part, "leaf", d) for d in range(2, leaves, 2)]
-    row_pieces = [factors] + [swapped(factors, "col", d) for d in range(1, cols - 1)]
+    early = {d: swapped(factors, "col", d) for d in range(cols // 2, cols - 1)}
     cells = turned_blocks((lanes0, lanes1))
-    chips, row_pieces, cells = lax.optimization_barrier((chips, row_pieces, cells))
-
-    row_pieces = row_pieces + [swapped(factors, "col", cols - 1)]
+    chips, early, cells = lax.optimization_barrier((chips, early, cells))
+
+    rows = [early[d] if d in early else swapped(factors, "col", d) for d in range(1, cols)]
+    row_pieces = [factors] + rows
     same_core, pair_part = joined([part] + chips, sums=True)
     other_core = swapped(same_core, "leaf", 1)
-    there = other_core.reshape(leaves // 2, part.shape[0], H, 2 * K)[:, -TERMS:].astype(F32)
-    other_part = there[:, 0]
+    there = other_core.reshape(leaves // 2, part.shape[0], Q, 2 * K)[:, -2 * TERMS :].astype(F32)
+    other_part = there[:, 0:2]
     for t in range(1, TERMS):
-        other_part = other_part + there[:, t]
+        other_part = other_part + there[:, 2 * t : 2 * t + 2]
     pair_part = pair_part + other_part
     tops = [pair_part] + [swapped(pair_part, "col", d) for d in range(1, cols)]
     ancestors, root = top_factors(at, tops, top_transfer, leaves)

time: 82.3 us -> 77.1 us (0.937)
  waiting for transfers between devices: 10.8 us -> 6.63 us
  starting transfers between devices: 20.3 us -> 17.7 us
  Pallas kernels: 48.8 us -> 50.4 us
    ppermute x13, waiting for transfers between devices: 10.8 us -> 6.63 us  [swapped(): lax.ppermute(x, axis, [(i, i ^ d) for i in range(lax.axis_size(axis))])]
    pallas_call x1, Pallas kernels: 6.8 us -> 10.1 us  [middle_products(): pl.pallas_call(functools.partial(middle_kernel, groups, sizes), out_shape...]
    ppermute x13, starting transfers between devices: 20.3 us -> 17.7 us  [swapped(): lax.ppermute(x, axis, [(i, i ^ d) for i in range(lax.axis_size(axis))])]
  transfers between devices with their start and end apart: 13 -> 13, of which waited for: 6 -> 2; matrix products, arithmetic and copies ran while one was open for 0% -> 0% of each run, Pallas kernels for 34% -> 40%
where the time goes in v6:
time: 77.1 us; the launch traced here: 76.9 us
  Pallas kernels  50.4 us (65%)
  starting transfers between devices  17.7 us (23%)
  waiting for transfers between devices  6.63 us (9%)
  between operations  2.11 us (3%)
    ppermute x13, starting transfers between devices, swapped(): lax.ppermute(x, axis, [(i, i ^ d) for i in range(lax.axis_size(axis))])  17.7 us
    pallas_call x1, Pallas kernels, own_factors(): pl.pallas_call(functools.partial(factor_kernel, own, cols), out_shape=sha...  13.8 us
    pallas_call x1, Pallas kernels, outer_products(): pl.pallas_call(functools.partial(outer_kernel, groups, sizes, len(slots))...  10.5 us
    pallas_call x1, Pallas kernels, middle_products(): pl.pallas_call(functools.partial(middle_kernel, groups, sizes), out_shape...  10.1 us
    ppermute x13, waiting for transfers between devices, swapped(): lax.ppermute(x, axis, [(i, i ^ d) for i in range(lax.axis_size(axis))])  6.63 us
    pallas_call x1, Pallas kernels, top_factors(): pl.pallas_call(functools.partial(top_kernel, leaves), out_shape=(jax.Shap...  6.03 us
    pallas_call x1, Pallas kernels, lifted_root(): pl.pallas_call(functools.partial(chain_kernel, own, cols), out_shape=jax....  5.2 us
    pallas_call x1, Pallas kernels, turned_blocks(): pl.pallas_call(functools.partial(turn_kernel, groups), out_shape=jax.Shap...  4.61 us
  transfers between devices with their start and end apart: 13, of which 2 were waited for; matrix products, arithmetic and copies ran while one was open for 0% of the time, Pallas kernels for 40%

profile of v6, /device:TPU:0, one launch (start us, length us, event | category | flops | bytes accessed | tf_op | source)
XLA Modules:
  0.0 76.9 jit_solution(12439951259106531005)
XLA Ops:
  0.6 0.1 pad_add_fusion.at_ref
  0.7 13.8 %shard_map.120 = (bf16[12,80,128]{2,1,0:T(8,128)(2,1)S(1)}, f32[16,64,64]{2,1,0:T(8,128)S(1)}, bf16[15,16,128]{2,1,0:T(8,128)(2,1)S(1)}, bf16[15,16,128]{2,1,0:T...) custom-call(s32[2]{0:T(128)S(1)} %pad_add_fusion.at_ref, ...), custom_call_target="tpu_custom_call" | custom-call | flops 536870912 | bytes 8388608 | tf_op jit(solution)/shard_map/pallas_call | solution.py:253
  14.5 3.1 %collective-permute-start = (bf16[15,16,128]{2,1,0:T(8,128)(2,1)S(1)}, bf16[15,16,128]{2,1,0:T(8,128)(2,1)S(1)}, u32[]{:S(2)}, u32[]{:S(2)}) collective-permute-start(bf16[15,16,128]{2,1,0:T(8,128)(2,1)S(1)} %get-tuple-element.29), channel_id=1, source_target_pairs={{0,1},{1,0},{2,3},{3,2},{4,5},{5,4},{6,7},{7,6},{8,9},{9,8},{10,11... | collective-permute-start | bytes 184328 | tf_op jit(solution)/shard_map/ppermute | solution.py:590
  17.6 2.6 %collective-permute-start.1 = (bf16[15,16,128]{2,1,0:T(8,128)(2,1)S(1)}, bf16[15,16,128]{2,1,0:T(8,128)(2,1)S(1)}, u32[]{:S(2)}, u32[]{:S(2)}) collective-permute-start(bf16[15,16,128]{2,1,0:T(8,128)(2,1)S(1)} %get-tuple-element.30), channel_id=1, source_target_pairs={{0,2},{1,3},{2,0},{3,1},{4,6},{5,7},{6,4},{7,5},{8,10},{9,11},{10,... | collective-permute-start | bytes 184328 | tf_op jit(solution)/shard_map/ppermute | solution.py:590
  20.2 0.0 collective-permute-start.2
  20.2 5.2 %shard_map.121.refs_4_ = bf16[6,16,128]{2,1,0:T(8,128)(2,1)S(1)} custom-call(s32[2]{0:T(128)S(1)} %pad_add_fusion.at_ref, f32[16,64,64]{2,1,0:T(8,128)S(1)} %get-tuple-element.32.gram1_ref, f32[64,64,255]{2,1,0:T(8,128)S(1)} %bitcast.11), custom_call_target="tpu_custom_call" | custom-call | flops 536870912 | bytes 4194304 | tf_op jit(solution)/shard_map/pallas_call | solution.py:315
  25.4 0.0 collective-permute-done.refs_1_
  25.4 0.0 collective-permute-done.1.refs_2_
  25.4 0.8 %collective-permute-done.2.refs_3_ = bf16[15,16,128]{2,1,0:T(8,128)(2,1)S(1)} collective-permute-done((bf16[15,16,128]{2,1,0:T(8,128)(2,1)S(1)}, bf16[15,16,128]{2,1,0:T(8,128)(2,1)S(1)}, u32[]{:S(2)}, u32[]{:S(2)}) %collective-permute-start.2) | collective-permute-done | bytes 61472 | tf_op jit(solution)/shard_map/ppermute | solution.py:590
  26.2 0.0 copy-start.4
  26.2 0.0 copy-start.5
  26.2 1.6 %collective-permute-start.3 = (bf16[66,16,128]{2,1,0:T(8,128)(2,1)S(1)}, bf16[66,16,128]{2,1,0:T(8,128)(2,1)S(1)}, u32[]{:S(2)}, u32[]{:S(2)}) collective-permute-start(bf16[66,16,128]{2,1,0:T(8,128)(2,1)S(1)} %shard_map.122.refs_0_), channel_id=1, source_target_pairs={{0,8},{4,12},{8,0},{12,4},{16,24},{20,28},{24,16},{28,20},{1,9},{5... | collective-permute-start | bytes 811016 | tf_op jit(solution)/shard_map/ppermute | solution.py:590
  27.8 1.5 %collective-permute-start.4 = (bf16[66,16,128]{2,1,0:T(8,128)(2,1)S(1)}, bf16[66,16,128]{2,1,0:T(8,128)(2,1)S(1)}, u32[]{:S(2)}, u32[]{:S(2)}) collective-permute-start(bf16[66,16,128]{2,1,0:T(8,128)(2,1)S(1)} %shard_map.122.refs_0_), channel_id=1, source_target_pairs={{0,16},{4,20},{8,24},{12,28},{16,0},{20,4},{24,8},{28,12},{1,17},{... | collective-permute-start | bytes 811016 | tf_op jit(solution)/shard_map/ppermute | solution.py:590
  29.3 0.5 collective-permute-start.5
  29.8 1.3 %collective-permute-start.6 = (bf16[12,80,128]{2,1,0:T(8,128)(2,1)S(1)}, bf16[12,80,128]{2,1,0:T(8,128)(2,1)S(1)}, u32[]{:S(2)}, u32[]{:S(2)}) collective-permute-start(bf16[12,80,128]{2,1,0:T(8,128)(2,1)S(1)} %get-tuple-element.38.refs_5_), channel_id=1, source_target_pairs={{0,2},{1,3},{2,0},{3,1},{4,6},{5,7},{6,4},{7,5},{8,10},{9,11},{10,... | collective-permute-start | bytes 737288 | tf_op jit(solution)/shard_map/ppermute | solution.py:590
  31.1 4.6 %shard_map.123.refs_2_ = bf16[384,32,128]{2,1,0:T(8,128)(2,1)S(1)} custom-call(bf16[64,64,256]{2,1,0:T(8,128)(2,1)S(1)} %bitcast.12, bf16[64,64,128]{2,1,0:T(8,128)(2,1)S(1)} %bitcast.14), custom_call_target="tpu_custom_call" | custom-call | flops 1048576 | bytes 1048576 | tf_op jit(solution)/shard_map/pallas_call | solution.py:404
  35.7 5.8 %collective-permute-done.6.refs_7_ = bf16[12,80,128]{2,1,0:T(8,128)(2,1)S(1)} collective-permute-done((bf16[12,80,128]{2,1,0:T(8,128)(2,1)S(1)}, bf16[12,80,128]{2,1,0:T(8,128)(2,1)S(1)}, u32[]{:S(2)}, u32[]{:S(2)}) %collective-permute-start.6) | collective-permute-done | bytes 245792 | tf_op jit(solution)/shard_map/ppermute | solution.py:590
  41.5 0.0 collective-permute-done.5.refs_3_
  41.5 0.1 shard_map.124
  41.6 0.1 collective-permute-start.7
  41.7 0.1 collective-permute-start.8
  41.7 2.6 %collective-permute-start.9 = (bf16[12,80,128]{2,1,0:T(8,128)(2,1)S(1)}, bf16[12,80,128]{2,1,0:T(8,128)(2,1)S(1)}, u32[]{:S(2)}, u32[]{:S(2)}) collective-permute-start(bf16[12,80,128]{2,1,0:T(8,128)(2,1)S(1)} %get-tuple-element.38.refs_5_), channel_id=1, source_target_pairs={{0,3},{1,2},{2,1},{3,0},{4,7},{5,6},{6,5},{7,4},{8,11},{9,10},{10,... | collective-permute-start | bytes 737288 | tf_op jit(solution)/shard_map/ppermute | solution.py:590
  44.3 0.0 collective-permute-done.7.refs_4_
  44.4 1.1 %collective-permute-start.10 = (f32[4,2,16,128]{3,2,1,0:T(8,128)S(1)}, f32[4,2,16,128]{3,2,1,0:T(8,128)S(1)}, u32[]{:S(2)}, u32[]{:S(2)}) collective-permute-start(f32[4,2,16,128]{3,2,1,0:T(8,128)S(1)} %fusion.refs_0_), channel_id=1, source_target_pairs={{0,1},{1,0},{2,3},{3,2},{4,5},{5,4},{6,7},{7,6},{8,9},{9,8},{10,11... | collective-permute-start | bytes 196616 | tf_op jit(solution)/shard_map/ppermute | solution.py:590
  45.5 2.1 %collective-permute-start.11 = (f32[4,2,16,128]{3,2,1,0:T(8,128)S(1)}, f32[4,2,16,128]{3,2,1,0:T(8,128)S(1)}, u32[]{:S(2)}, u32[]{:S(2)}) collective-permute-start(f32[4,2,16,128]{3,2,1,0:T(8,128)S(1)} %fusion.refs_0_), channel_id=1, source_target_pairs={{0,2},{1,3},{2,0},{3,1},{4,6},{5,7},{6,4},{7,5},{8,10},{9,11},{10,... | collective-permute-start | bytes 196616 | tf_op jit(solution)/shard_map/ppermute | solution.py:590
  47.6 1.3 %collective-permute-start.12 = (f32[4,2,16,128]{3,2,1,0:T(8,128)S(1)}, f32[4,2,16,128]{3,2,1,0:T(8,128)S(1)}, u32[]{:S(2)}, u32[]{:S(2)}) collective-permute-start(f32[4,2,16,128]{3,2,1,0:T(8,128)S(1)} %fusion.refs_0_), channel_id=1, source_target_pairs={{0,3},{1,2},{2,1},{3,0},{4,7},{5,6},{6,5},{7,4},{8,11},{9,10},{10,... | collective-permute-start | bytes 196616 | tf_op jit(solution)/shard_map/ppermute | solution.py:590
  50.2 10.1 %shard_map.125.refs_4_ = bf16[384,32,128]{2,1,0:T(8,128)(2,1)S(1)} custom-call(s32[2]{0:T(128)S(1)} %pad_add_fusion.at_ref, s32[2,256]{1,0:T(2,128)S(1)} %bitcast.15, s32[2,128]{1,0:T(2,128)S(1)} %bitcast.17, bf16[384,32,128]{2,1,0:T(8,128)(2,1)S(1)} %shard_map.123.refs_2_, bf16[264,16,128]{2,1,0:T(8,128)(2,1)S(1)} %get-tuple-element.45.refs_3_, ...), custom_call_target="tpu_custom_call" | custom-call | flops 201326592 | bytes 1048576 | tf_op jit(solution)/shard_map/pallas_call | solution.py:511
  60.3 0.0 collective-permute-done.8.refs_6_
  60.3 10.5 %shard_map.126 = (bf16[64,64,256]{2,1,0:T(8,128)(2,1)}, bf16[64,64,128]{2,1,0:T(8,128)(2,1)}) custom-call(s32[2]{0:T(128)S(1)} %pad_add_fusion.at_ref, s32[2,256]{1,0:T(2,128)S(1)} %bitcast.16, s32[2,128]{1,0:T(2,128)S(1)} %bitcast.18, s32[1]{0:T(128)S(6)} %copy.13.refs_2_, s32[1]{0:T(128)S(6)} %copy.14.refs_3_, ...), custom_call_target="tpu_custom_call" | custom-call | flops 201326592 | bytes 4194304 | tf_op jit(solution)/shard_map/pallas_call | solution.py:573
  70.9 0.0 collective-permute-done.11.refs_2_
  70.9 0.0 collective-permute-done.12.refs_3_
  70.9 6.0 %shard_map.127 = (f32[1,3,64,64]{3,2,1,0:T(8,128)}, f32[64,64]{1,0:T(8,128)}) custom-call(s32[2]{0:T(128)S(1)} %pad_add_fusion.at_ref, f32[6,64,64]{2,1,0:T(8,128)S(1)} %copy-done.3, f32[4,2,16,128]{3,2,1,0:T(8,128)S(1)} %fusion.refs_0_, f32[4,2,16,128]{3,2,1,0:T(8,128)S(1)} %collective-permute-done.10.refs_1_, ...), custom_call_target="tpu_custom_call" | custom-call | flops 4194304 | bytes 131072 | tf_op jit(solution)/shard_map/pallas_call | solution.py:363
  (17 shorter events, 0.1 us)
Async XLA Ops:
  0.7 19.4 %copy-start = (f32[255,64,64]{0,2,1:T(8,128)S(1)}, f32[255,64,64]{0,2,1:T(8,128)}, u32[]{:S(2)}) copy-start(f32[255,64,64]{0,2,1:T(8,128)} %param.10) | copy-start | bytes 12533764
  14.5 10.9 %collective-permute-start = (bf16[15,16,128]{2,1,0:T(8,128)(2,1)S(1)}, bf16[15,16,128]{2,1,0:T(8,128)(2,1)S(1)}, u32[]{:S(2)}, u32[]{:S(2)}) collective-permute-start(bf16[15,16,128]{2,1,0:T(8,128)(2,1)S(1)} %get-tuple-element.29), channel_id=1, source_target_pairs={{0,1},{1,0},{2,3},{3,2},{4,5},{5,4},{6,7},{7,6},{8,9},{9,8},{10,11... | collective-permute-start | bytes 184328 | tf_op jit(solution)/shard_map/ppermute | solution.py:590
  17.6 7.8 %collective-permute-start.1 = (bf16[15,16,128]{2,1,0:T(8,128)(2,1)S(1)}, bf16[15,16,128]{2,1,0:T(8,128)(2,1)S(1)}, u32[]{:S(2)}, u32[]{:S(2)}) collective-permute-start(bf16[15,16,128]{2,1,0:T(8,128)(2,1)S(1)} %get-tuple-element.30), channel_id=1, source_target_pairs={{0,2},{1,3},{2,0},{3,1},{4,6},{5,7},{6,4},{7,5},{8,10},{9,11},{10,... | collective-permute-start | bytes 184328 | tf_op jit(solution)/shard_map/ppermute | solution.py:590
  20.2 6.0 %collective-permute-start.2 = (bf16[15,16,128]{2,1,0:T(8,128)(2,1)S(1)}, bf16[15,16,128]{2,1,0:T(8,128)(2,1)S(1)}, u32[]{:S(2)}, u32[]{:S(2)}) collective-permute-start(bf16[15,16,128]{2,1,0:T(8,128)(2,1)S(1)} %get-tuple-element.31), channel_id=1, source_target_pairs={{0,3},{1,2},{2,1},{3,0},{4,7},{5,6},{6,5},{7,4},{8,11},{9,10},{10,... | collective-permute-start | bytes 184328 | tf_op jit(solution)/shard_map/ppermute | solution.py:590
  20.2 10.9 %copy-start.1 = (bf16[256,64,64]{0,2,1:T(8,128)(2,1)S(1)}, bf16[256,64,64]{0,2,1:T(8,128)(2,1)}, u32[]{:S(2)}) copy-start(bf16[256,64,64]{0,2,1:T(8,128)(2,1)} %param.12) | copy-start | bytes 6291460
  20.2 10.9 %copy-start.2 = (bf16[128,64,64]{0,2,1:T(8,128)(2,1)S(1)}, bf16[128,64,64]{0,2,1:T(8,128)(2,1)}, u32[]{:S(2)}) copy-start(bf16[128,64,64]{0,2,1:T(8,128)(2,1)} %param.15) | copy-start | bytes 3145732
  26.2 24.0 %copy-start.4 = (s32[256,2]{0,1:T(2,128)S(1)}, s32[256,2]{0,1:T(2,128)}, u32[]{:S(2)}) copy-start(s32[256,2]{0,1:T(2,128)} %param.13) | copy-start | bytes 6148
  26.2 24.0 %copy-start.5 = (s32[128,2]{0,1:T(2,128)S(1)}, s32[128,2]{0,1:T(2,128)}, u32[]{:S(2)}) copy-start(s32[128,2]{0,1:T(2,128)} %param.16) | copy-start | bytes 3076
  26.2 15.3 %collective-permute-start.3 = (bf16[66,16,128]{2,1,0:T(8,128)(2,1)S(1)}, bf16[66,16,128]{2,1,0:T(8,128)(2,1)S(1)}, u32[]{:S(2)}, u32[]{:S(2)}) collective-permute-start(bf16[66,16,128]{2,1,0:T(8,128)(2,1)S(1)} %shard_map.122.refs_0_), channel_id=1, source_target_pairs={{0,8},{4,12},{8,0},{12,4},{16,24},{20,28},{24,16},{28,20},{1,9},{5... | collective-permute-start | bytes 811016 | tf_op jit(solution)/shard_map/ppermute | solution.py:590
  27.8 13.7 %collective-permute-start.4 = (bf16[66,16,128]{2,1,0:T(8,128)(2,1)S(1)}, bf16[66,16,128]{2,1,0:T(8,128)(2,1)S(1)}, u32[]{:S(2)}, u32[]{:S(2)}) collective-permute-start(bf16[66,16,128]{2,1,0:T(8,128)(2,1)S(1)} %shard_map.122.refs_0_), channel_id=1, source_target_pairs={{0,16},{4,20},{8,24},{12,28},{16,0},{20,4},{24,8},{28,12},{1,17},{... | collective-permute-start | bytes 811016 | tf_op jit(solution)/shard_map/ppermute | solution.py:590
  29.3 12.2 %collective-permute-start.5 = (bf16[66,16,128]{2,1,0:T(8,128)(2,1)S(1)}, bf16[66,16,128]{2,1,0:T(8,128)(2,1)S(1)}, u32[]{:S(2)}, u32[]{:S(2)}) collective-permute-start(bf16[66,16,128]{2,1,0:T(8,128)(2,1)S(1)} %shard_map.122.refs_0_), channel_id=1, source_target_pairs={{0,24},{4,28},{8,16},{12,20},{16,8},{20,12},{24,0},{28,4},{1,25},{... | collective-permute-start | bytes 811016 | tf_op jit(solution)/shard_map/ppermute | solution.py:590
  29.8 11.7 %collective-permute-start.6 = (bf16[12,80,128]{2,1,0:T(8,128)(2,1)S(1)}, bf16[12,80,128]{2,1,0:T(8,128)(2,1)S(1)}, u32[]{:S(2)}, u32[]{:S(2)}) collective-permute-start(bf16[12,80,128]{2,1,0:T(8,128)(2,1)S(1)} %get-tuple-element.38.refs_5_), channel_id=1, source_target_pairs={{0,2},{1,3},{2,0},{3,1},{4,6},{5,7},{6,4},{7,5},{8,10},{9,11},{10,... | collective-permute-start | bytes 737288 | tf_op jit(solution)/shard_map/ppermute | solution.py:590
  41.6 2.8 %collective-permute-start.7 = (bf16[264,16,128]{2,1,0:T(8,128)(2,1)S(1)}, bf16[264,16,128]{2,1,0:T(8,128)(2,1)S(1)}, u32[]{:S(2)}, u32[]{:S(2)}) collective-permute-start(bf16[264,16,128]{2,1,0:T(8,128)(2,1)S(1)} %get-tuple-element.45.refs_3_), channel_id=1, source_target_pairs={{0,4},{4,0},{8,12},{12,8},{16,20},{20,16},{24,28},{28,24},{1,5},{5... | collective-permute-start | bytes 3244040 | tf_op jit(solution)/shard_map/ppermute | solution.py:590
  41.7 18.7 %collective-permute-start.8 = (bf16[12,80,128]{2,1,0:T(8,128)(2,1)S(1)}, bf16[12,80,128]{2,1,0:T(8,128)(2,1)S(1)}, u32[]{:S(2)}, u32[]{:S(2)}) collective-permute-start(bf16[12,80,128]{2,1,0:T(8,128)(2,1)S(1)} %get-tuple-element.38.refs_5_), channel_id=1, source_target_pairs={{0,1},{1,0},{2,3},{3,2},{4,5},{5,4},{6,7},{7,6},{8,9},{9,8},{10,11... | collective-permute-start | bytes 737288 | tf_op jit(solution)/shard_map/ppermute | solution.py:590
  41.7 18.6 %collective-permute-start.9 = (bf16[12,80,128]{2,1,0:T(8,128)(2,1)S(1)}, bf16[12,80,128]{2,1,0:T(8,128)(2,1)S(1)}, u32[]{:S(2)}, u32[]{:S(2)}) collective-permute-start(bf16[12,80,128]{2,1,0:T(8,128)(2,1)S(1)} %get-tuple-element.38.refs_5_), channel_id=1, source_target_pairs={{0,3},{1,2},{2,1},{3,0},{4,7},{5,6},{6,5},{7,4},{8,11},{9,10},{10,... | collective-permute-start | bytes 737288 | tf_op jit(solution)/shard_map/ppermute | solution.py:590
  44.4 26.4 %collective-permute-start.10 = (f32[4,2,16,128]{3,2,1,0:T(8,128)S(1)}, f32[4,2,16,128]{3,2,1,0:T(8,128)S(1)}, u32[]{:S(2)}, u32[]{:S(2)}) collective-permute-start(f32[4,2,16,128]{3,2,1,0:T(8,128)S(1)} %fusion.refs_0_), channel_id=1, source_target_pairs={{0,1},{1,0},{2,3},{3,2},{4,5},{5,4},{6,7},{7,6},{8,9},{9,8},{10,11... | collective-permute-start | bytes 196616 | tf_op jit(solution)/shard_map/ppermute | solution.py:590
  45.5 25.4 %collective-permute-start.11 = (f32[4,2,16,128]{3,2,1,0:T(8,128)S(1)}, f32[4,2,16,128]{3,2,1,0:T(8,128)S(1)}, u32[]{:S(2)}, u32[]{:S(2)}) collective-permute-start(f32[4,2,16,128]{3,2,1,0:T(8,128)S(1)} %fusion.refs_0_), channel_id=1, source_target_pairs={{0,2},{1,3},{2,0},{3,1},{4,6},{5,7},{6,4},{7,5},{8,10},{9,11},{10,... | collective-permute-start | bytes 196616 | tf_op jit(solution)/shard_map/ppermute | solution.py:590
  47.6 23.3 %collective-permute-start.12 = (f32[4,2,16,128]{3,2,1,0:T(8,128)S(1)}, f32[4,2,16,128]{3,2,1,0:T(8,128)S(1)}, u32[]{:S(2)}, u32[]{:S(2)}) collective-permute-start(f32[4,2,16,128]{3,2,1,0:T(8,128)S(1)} %fusion.refs_0_), channel_id=1, source_target_pairs={{0,3},{1,2},{2,1},{3,0},{4,7},{5,6},{6,5},{7,4},{8,11},{9,10},{10,... | collective-permute-start | bytes 196616 | tf_op jit(solution)/shard_map/ppermute | solution.py:590
  60.3 10.6 %copy-start.3 = (f32[6,64,64]{2,1,0:T(8,128)S(1)}, f32[6,64,64]{2,1,0:T(8,128)}, u32[]{:S(2)}) copy-start(f32[6,64,64]{2,1,0:T(8,128)} %top_ref.1) | copy-start | bytes 294916

commit v7 on v6

--- a/solution.py
+++ b/solution.py
@@ -21,8 +21,8 @@
 ANY = pl.BlockSpec(memory_space=pl.ANY)
 HBM = pl.BlockSpec(memory_space=pltpu.HBM)
 TERMS = 3
-TURN = 8
-SLOTS = 64
+TURN = 16
+SLOTS = 128
 PAIRS = 8
 PARAMS = pltpu.CompilerParams(vmem_limit_bytes=24 * 2**20)
 
@@ -413,31 +413,38 @@
 
 
 def join_kernel(inputs, *refs):
+    pieces, out = refs[: inputs[0]], refs[sum(inputs) :]
     start = 0
-    for x in refs[:inputs]:
-        refs[inputs][pl.ds(start, x.shape[0])] = x[...]
+    for x in pieces:
+        out[0][pl.ds(start, x.shape[0])] = x[...]
         start += x.shape[0]
-    for n, x in enumerate(refs[:inputs] if len(refs) > inputs + 1 else ()):
+    if len(out) == 1:
+        return
+    for n, x in enumerate(pieces):
         last = x.shape[0] - 2 * TERMS
         total = x[last : last + 2].astype(F32)
         for t in range(1, TERMS):
             total = total + x[last + 2 * t : last + 2 * t + 2].astype(F32)
-        refs[inputs + 1][n] = total
-
-
-def joined(pieces, sums=False):
-    entries = sum(x.shape[0] for x in pieces)
-    shapes = [jax.ShapeDtypeStruct((entries, Q, 2 * K), BF)]
-    if sums:
+        out[1][n] = total
+    start = 0
+    for x in refs[inputs[0] : sum(inputs)]:
+        out[2][pl.ds(start, x.shape[0])] = x[...]
+        start += x.shape[0]
+
+
+def joined(pieces, packs=()):
+    shapes = [jax.ShapeDtypeStruct((sum(x.shape[0] for x in pieces), Q, 2 * K), BF)]
+    if packs:
         shapes.append(jax.ShapeDtypeStruct((len(pieces), 2, Q, 2 * K), F32))
+        shapes.append(jax.ShapeDtypeStruct((sum(x.shape[0] for x in packs), 5 * Q, 2 * K), BF))
     return pl.pallas_call(
-        functools.partial(join_kernel, len(pieces)),
+        functools.partial(join_kernel, (len(pieces), len(packs))),
         out_shape=tuple(shapes),
-        in_specs=[VMEM] * len(pieces),
+        in_specs=[VMEM] * (len(pieces) + len(packs)),
         out_specs=(VMEM,) * len(shapes),
         compiler_params=PARAMS,
         cost_estimate=cost(0, 2**18),
-    )(*pieces)
+    )(*pieces, *packs)
 
 
 def bits(size):
@@ -519,21 +526,23 @@
     )(at, *pairs, cells, same_core, other_core)
 
 
-def outer_kernel(groups, sizes, outs, at_ref, *refs):
+def outer_kernel(groups, sizes, outs, orders, at_ref, *refs):
     pairs, counts, middle_ref = refs[:outs], refs[outs : 2 * outs], refs[2 * outs]
     pieces, out_refs = refs[2 * outs + 1 : -outs - 4], refs[-outs - 4 : -4]
     pt, table, ready, sem = refs[-4:]
-    packs = pieces[0].shape[0]
+    packs = (sizes[0] + sizes[0] // 2) // 4
     together = math.gcd(packs, 6)
-    for e, piece in enumerate(pieces):
-
-        @pl.loop(0, packs // together)
-        def _(step):
-            at = [step * together + g for g in range(together)]
-            full = [unpack([piece[g, Q * n : Q * (n + 1)].astype(F32) for n in range(5)]) for g in at]
-            for g, four in zip(at, full):
-                for m in range(4):
-                    table[4 * (e * packs + g) + m] = four[m].astype(BF)
+    for piece, order in zip(pieces, orders):
+        for n, e in enumerate(order):
+
+            @pl.loop(0, packs // together)
+            def _(step):
+                at = [step * together + g for g in range(together)]
+                units = [[piece[n * packs + g, Q * u : Q * (u + 1)] for u in range(5)] for g in at]
+                full = [unpack([x.astype(F32) for x in five]) for five in units]
+                for g, four in zip(at, full):
+                    for m in range(4):
+                        table[4 * (e * packs + g) + m] = four[m].astype(BF)
 
     copies = []
     for g, (which, first) in enumerate(groups):
@@ -566,12 +575,12 @@
         copy.wait()
 
 
-def outer_products(sizes, at, pairs, counts, middle, pieces):
+def outer_products(sizes, at, pairs, counts, middle, pieces, orders):
     slots = [x.shape[1] for x in pairs]
     groups = lane_groups(slots)
     entries = 4 * sum(x.shape[0] for x in pieces)
     return pl.pallas_call(
-        functools.partial(outer_kernel, groups, sizes, len(slots)),
+        functools.partial(outer_kernel, groups, sizes, len(slots), orders),
         out_shape=tuple(jax.ShapeDtypeStruct((K, K, size), BF) for size in slots),
         in_specs=[SMEM] * (1 + 2 * len(slots)) + [VMEM] * (1 + len(pieces)),
         out_specs=(ANY,) * len(slots),
@@ -609,24 +618,36 @@
 
     (part,) = joined([sent[0]] + received + [terms])
     chips = [swapped(part, "leaf", d) for d in range(2, leaves, 2)]
-    early = {d: swapped(factors, "col", d) for d in range(cols // 2, cols - 1)}
+    bit = cols // 2
+    early = swapped(factors, "col", bit)
     cells = turned_blocks((lanes0, lanes1))
     chips, early, cells = lax.optimization_barrier((chips, early, cells))
 
-    rows = [early[d] if d in early else swapped(factors, "col", d) for d in range(1, cols)]
-    row_pieces = [factors] + rows
-    same_core, pair_part = joined([part] + chips, sums=True)
+    same_core, pair_part, rows = joined([part] + chips, [factors, early])
     other_core = swapped(same_core, "leaf", 1)
+    orders = [0, bit]
+    while True:
+        bit //= 2
+        forwarded = swapped(rows, "col", bit)
+        orders = [orders, [e ^ bit for e in orders]]
+        if bit == 1:
+            break
+        rows = jnp.concatenate([rows, forwarded], axis=0)
+        orders = orders[0] + orders[1]
     there = other_core.reshape(leaves // 2, part.shape[0], Q, 2 * K)[:, -2 * TERMS :].astype(F32)
     other_part = there[:, 0:2]
     for t in range(1, TERMS):
         other_part = other_part + there[:, 2 * t : 2 * t + 2]
     pair_part = pair_part + other_part
-    tops = [pair_part] + [swapped(pair_part, "col", d) for d in range(1, cols)]
+    for d in range(1, bits(cols)):
+        pair_part = pair_part + swapped(pair_part, "col", cols >> d)
+    middle = middle_products(sizes, at, pairs, cells, same_core, other_core)
+    pair_part, middle = lax.optimization_barrier((pair_part, middle))
+    tops = [pair_part, swapped(pair_part, "col", 1)]
+    out0, out1 = outer_products(
+        sizes, at, pairs, (counts0, counts1), middle, [rows, forwarded], orders
+    )
     ancestors, root = top_factors(at, tops, top_transfer, leaves)
-
-    middle = middle_products(sizes, at, pairs, cells, same_core, other_core)
-    out0, out1 = outer_products(sizes, at, pairs, (counts0, counts1), middle, row_pieces)
     return (jnp.transpose(out0, (2, 0, 1)), jnp.transpose(out1, (2, 0, 1)), root, ancestors)
 
 

time: 77.1 us -> 74.6 us (0.968)
  waiting for transfers between devices: 6.63 us -> 10.2 us
  Pallas kernels: 50.4 us -> 47.3 us
  starting transfers between devices: 17.7 us -> 14.8 us
    ppermute x13 -> x11, waiting for transfers between devices: 6.63 us -> 10.2 us  [swapped(): lax.ppermute(x, axis, [(i, i ^ d) for i in range(lax.axis_size(axis))])]
    ppermute x13 -> x11, starting transfers between devices: 17.7 us -> 14.8 us  [swapped(): lax.ppermute(x, axis, [(i, i ^ d) for i in range(lax.axis_size(axis))])]
    pallas_call x1, Pallas kernels: 10.1 us -> 8.78 us  [middle_products(): pl.pallas_call(functools.partial(middle_kernel, groups, sizes), out_shape...]
    pallas_call x3, Pallas kernels: 10.6 us -> 9.68 us  [the longest x1 9.55 us: outer_products(): pl.pallas_call(functools.partial(outer_kernel, groups, sizes, len(slots),...]
  transfers between devices with their start and end apart: 13 -> 11, of which waited for: 2 -> 4; matrix products, arithmetic and copies ran while one was open for 0% -> 0% of each run, Pallas kernels for 40% -> 37%
where the time goes in v7:
time: 74.6 us; the launch traced here: 74.5 us
  Pallas kernels  47.3 us (63%)
  starting transfers between devices  14.8 us (20%)
  waiting for transfers between devices  10.2 us (14%)
  between operations  2.08 us (3%)
    ppermute x11, starting transfers between devices, swapped(): lax.ppermute(x, axis, [(i, i ^ d) for i in range(lax.axis_size(axis))])  14.8 us
    pallas_call x1, Pallas kernels, own_factors(): pl.pallas_call(functools.partial(factor_kernel, own, cols), out_shape=sha...  13.5 us
    ppermute x11, waiting for transfers between devices, swapped(): lax.ppermute(x, axis, [(i, i ^ d) for i in range(lax.axis_size(axis))])  10.2 us
    pallas_call x1, Pallas kernels, outer_products(): pl.pallas_call(functools.partial(outer_kernel, groups, sizes, len(slots),...  9.55 us
    pallas_call x1, Pallas kernels, middle_products(): pl.pallas_call(functools.partial(middle_kernel, groups, sizes), out_shape...  8.78 us
    pallas_call x1, Pallas kernels, top_factors(): pl.pallas_call(functools.partial(top_kernel, leaves), out_shape=(jax.Shap...  5.8 us
    pallas_call x1, Pallas kernels, lifted_root(): pl.pallas_call(functools.partial(chain_kernel, own, cols), out_shape=jax....  5.16 us
    pallas_call x1, Pallas kernels, turned_blocks(): pl.pallas_call(functools.partial(turn_kernel, groups), out_shape=jax.Shap...  4.37 us
  transfers between devices with their start and end apart: 11, of which 4 were waited for; matrix products, arithmetic and copies ran while one was open for 0% of the time, Pallas kernels for 37%

profile of v7, /device:TPU:0, one launch (start us, length us, event | category | flops | bytes accessed | tf_op | source)
XLA Modules:
  0.0 74.5 jit_solution(8571390116952161849)
XLA Ops:
  0.6 0.1 pad_add_fusion.at_ref
  0.7 13.5 %shard_map.120 = (bf16[12,80,128]{2,1,0:T(8,128)(2,1)S(1)}, f32[16,64,64]{2,1,0:T(8,128)S(1)}, bf16[15,16,128]{2,1,0:T(8,128)(2,1)S(1)}, bf16[15,16,128]{2,1,0:T...) custom-call(s32[2]{0:T(128)S(1)} %pad_add_fusion.at_ref, ...), custom_call_target="tpu_custom_call" | custom-call | flops 536870912 | bytes 8388608 | tf_op jit(solution)/shard_map/pallas_call | solution.py:253
  14.2 3.1 %collective-permute-start = (bf16[15,16,128]{2,1,0:T(8,128)(2,1)S(1)}, bf16[15,16,128]{2,1,0:T(8,128)(2,1)S(1)}, u32[]{:S(2)}, u32[]{:S(2)}) collective-permute-start(bf16[15,16,128]{2,1,0:T(8,128)(2,1)S(1)} %get-tuple-element.32), channel_id=1, source_target_pairs={{0,1},{1,0},{2,3},{3,2},{4,5},{5,4},{6,7},{7,6},{8,9},{9,8},{10,11... | collective-permute-start | bytes 184328 | tf_op jit(solution)/shard_map/ppermute | solution.py:599
  17.3 2.6 %collective-permute-start.1 = (bf16[15,16,128]{2,1,0:T(8,128)(2,1)S(1)}, bf16[15,16,128]{2,1,0:T(8,128)(2,1)S(1)}, u32[]{:S(2)}, u32[]{:S(2)}) collective-permute-start(bf16[15,16,128]{2,1,0:T(8,128)(2,1)S(1)} %get-tuple-element.33), channel_id=1, source_target_pairs={{0,2},{1,3},{2,0},{3,1},{4,6},{5,7},{6,4},{7,5},{8,10},{9,11},{10,... | collective-permute-start | bytes 184328 | tf_op jit(solution)/shard_map/ppermute | solution.py:599
  19.9 0.0 collective-permute-start.2
  19.9 5.2 %shard_map.121.refs_4_ = bf16[6,16,128]{2,1,0:T(8,128)(2,1)S(1)} custom-call(s32[2]{0:T(128)S(1)} %pad_add_fusion.at_ref, f32[16,64,64]{2,1,0:T(8,128)S(1)} %get-tuple-element.35.gram1_ref, f32[64,64,255]{2,1,0:T(8,128)S(1)} %bitcast.11), custom_call_target="tpu_custom_call" | custom-call | flops 536870912 | bytes 4194304 | tf_op jit(solution)/shard_map/pallas_call | solution.py:315
  25.0 0.0 collective-permute-done.refs_1_
  25.0 0.0 collective-permute-done.1.refs_2_
  25.1 0.8 %collective-permute-done.2.refs_3_ = bf16[15,16,128]{2,1,0:T(8,128)(2,1)S(1)} collective-permute-done((bf16[15,16,128]{2,1,0:T(8,128)(2,1)S(1)}, bf16[15,16,128]{2,1,0:T(8,128)(2,1)S(1)}, u32[]{:S(2)}, u32[]{:S(2)}) %collective-permute-start.2) | collective-permute-done | bytes 61472 | tf_op jit(solution)/shard_map/ppermute | solution.py:599
  25.9 1.6 %collective-permute-start.3 = (bf16[66,16,128]{2,1,0:T(8,128)(2,1)S(1)}, bf16[66,16,128]{2,1,0:T(8,128)(2,1)S(1)}, u32[]{:S(2)}, u32[]{:S(2)}) collective-permute-start(bf16[66,16,128]{2,1,0:T(8,128)(2,1)S(1)} %shard_map.122.refs_0_), channel_id=1, source_target_pairs={{0,8},{4,12},{8,0},{12,4},{16,24},{20,28},{24,16},{28,20},{1,9},{5... | collective-permute-start | bytes 811016 | tf_op jit(solution)/shard_map/ppermute | solution.py:599
  27.5 1.5 %collective-permute-start.4 = (bf16[66,16,128]{2,1,0:T(8,128)(2,1)S(1)}, bf16[66,16,128]{2,1,0:T(8,128)(2,1)S(1)}, u32[]{:S(2)}, u32[]{:S(2)}) collective-permute-start(bf16[66,16,128]{2,1,0:T(8,128)(2,1)S(1)} %shard_map.122.refs_0_), channel_id=1, source_target_pairs={{0,16},{4,20},{8,24},{12,28},{16,0},{20,4},{24,8},{28,12},{1,17},{... | collective-permute-start | bytes 811016 | tf_op jit(solution)/shard_map/ppermute | solution.py:599
  29.0 0.5 collective-permute-start.5
  29.5 1.3 %collective-permute-start.6 = (bf16[12,80,128]{2,1,0:T(8,128)(2,1)S(1)}, bf16[12,80,128]{2,1,0:T(8,128)(2,1)S(1)}, u32[]{:S(2)}, u32[]{:S(2)}) collective-permute-start(bf16[12,80,128]{2,1,0:T(8,128)(2,1)S(1)} %get-tuple-element.41.refs_4_), channel_id=1, source_target_pairs={{0,2},{1,3},{2,0},{3,1},{4,6},{5,7},{6,4},{7,5},{8,10},{9,11},{10,... | collective-permute-start | bytes 737288 | tf_op jit(solution)/shard_map/ppermute | solution.py:599
  30.7 4.4 %shard_map.123.refs_2_ = bf16[384,32,128]{2,1,0:T(8,128)(2,1)S(1)} custom-call(bf16[64,64,256]{2,1,0:T(8,128)(2,1)S(1)} %bitcast.12, bf16[64,64,128]{2,1,0:T(8,128)(2,1)S(1)} %bitcast.14), custom_call_target="tpu_custom_call" | custom-call | flops 1048576 | bytes 1048576 | tf_op jit(solution)/shard_map/pallas_call | solution.py:404
  35.1 0.0 copy-start.4
  35.1 0.0 copy-start.5
  35.1 6.0 %collective-permute-done.6.refs_5_ = bf16[12,80,128]{2,1,0:T(8,128)(2,1)S(1)} collective-permute-done((bf16[12,80,128]{2,1,0:T(8,128)(2,1)S(1)}, bf16[12,80,128]{2,1,0:T(8,128)(2,1)S(1)}, u32[]{:S(2)}, u32[]{:S(2)}) %collective-permute-start.6) | collective-permute-done | bytes 245792 | tf_op jit(solution)/shard_map/ppermute | solution.py:599
  41.1 0.0 collective-permute-done.3.refs_1_
  41.1 0.0 collective-permute-done.4.refs_2_
  41.1 0.0 collective-permute-done.5.refs_3_
  41.1 0.1 shard_map.124
  41.2 0.1 collective-permute-start.7
  41.3 0.1 collective-permute-start.9
  41.4 2.6 %collective-permute-done.7.refs_4_ = bf16[264,16,128]{2,1,0:T(8,128)(2,1)S(1)} collective-permute-done((bf16[264,16,128]{2,1,0:T(8,128)(2,1)S(1)}, bf16[264,16,128]{2,1,0:T(8,128)(2,1)S(1)}, u32[]{:S(2)}, u32[]{:S(2)}) %collective-permute-start.7) | collective-permute-done | bytes 1081376 | tf_op jit(solution)/shard_map/ppermute | solution.py:599
  44.1 0.5 collective-permute-start.8
  44.6 8.8 %shard_map.125.refs_4_ = bf16[384,32,128]{2,1,0:T(8,128)(2,1)S(1)} custom-call(s32[2]{0:T(128)S(1)} %pad_add_fusion.at_ref, s32[2,256]{1,0:T(2,128)S(1)} %bitcast.15, s32[2,128]{1,0:T(2,128)S(1)} %bitcast.17, bf16[384,32,128]{2,1,0:T(8,128)(2,1)S(1)} %shard_map.123.refs_2_, bf16[264,16,128]{2,1,0:T(8,128)(2,1)S(1)} %get-tuple-element.49.refs_3_, ...), custom_call_target="tpu_custom_call" | custom-call | flops 201326592 | bytes 1048576 | tf_op jit(solution)/shard_map/pallas_call | solution.py:518
  53.4 0.8 %collective-permute-done.8 = f32[4,2,16,128]{3,2,1,0:T(8,128)S(1)} collective-permute-done((f32[4,2,16,128]{3,2,1,0:T(8,128)S(1)}, f32[4,2,16,128]{3,2,1,0:T(8,128)S(1)}, u32[]{:S(2)}, u32[]{:S(2)}) %collective-permute-start.8) | collective-permute-done | bytes 65568 | tf_op jit(solution)/shard_map/ppermute | solution.py:599
  54.2 0.0 copy-start.3
  54.2 3.6 %collective-permute-start.10 = (f32[4,2,16,128]{3,2,1,0:T(8,128)S(1)}, f32[4,2,16,128]{3,2,1,0:T(8,128)S(1)}, u32[]{:S(2)}, u32[]{:S(2)}) collective-permute-start(f32[4,2,16,128]{3,2,1,0:T(8,128)S(1)} %add.15.refs_0_), channel_id=1, source_target_pairs={{0,1},{1,0},{2,3},{3,2},{4,5},{5,4},{6,7},{7,6},{8,9},{9,8},{10,11... | collective-permute-start | bytes 196616 | tf_op jit(solution)/shard_map/ppermute | solution.py:599
  59.1 9.5 %shard_map.126 = (bf16[64,64,256]{2,1,0:T(8,128)(2,1)}, bf16[64,64,128]{2,1,0:T(8,128)(2,1)}) custom-call(s32[2]{0:T(128)S(1)} %pad_add_fusion.at_ref, s32[2,256]{1,0:T(2,128)S(1)} %bitcast.16, s32[2,128]{1,0:T(2,128)S(1)} %bitcast.18, s32[1]{0:T(128)S(6)} %copy.13.refs_2_, s32[1]{0:T(128)S(6)} %copy.14.refs_3_, ...), custom_call_target="tpu_custom_call" | custom-call | flops 201326592 | bytes 4194304 | tf_op jit(solution)/shard_map/pallas_call | solution.py:582
  68.6 0.0 collective-permute-done.10.refs_1_
  68.7 5.8 %shard_map.127 = (f32[1,3,64,64]{3,2,1,0:T(8,128)}, f32[64,64]{1,0:T(8,128)}) custom-call(s32[2]{0:T(128)S(1)} %pad_add_fusion.at_ref, f32[6,64,64]{2,1,0:T(8,128)S(1)} %copy-done.3, f32[4,2,16,128]{3,2,1,0:T(8,128)S(1)} %add.15.refs_0_, f32[4,2,16,128]{3,2,1,0:T(8,128)S(1)} %collective-permute-done.10.refs_1_), custom_call_target="tpu_custom_call" | custom-call | flops 4194304 | bytes 131072 | tf_op jit(solution)/shard_map/pallas_call | solution.py:363
  (14 shorter events, 0.1 us)
Async XLA Ops:
  0.7 19.2 %copy-start = (f32[255,64,64]{0,2,1:T(8,128)S(1)}, f32[255,64,64]{0,2,1:T(8,128)}, u32[]{:S(2)}) copy-start(f32[255,64,64]{0,2,1:T(8,128)} %param.10) | copy-start | bytes 12533764
  14.2 10.8 %collective-permute-start = (bf16[15,16,128]{2,1,0:T(8,128)(2,1)S(1)}, bf16[15,16,128]{2,1,0:T(8,128)(2,1)S(1)}, u32[]{:S(2)}, u32[]{:S(2)}) collective-permute-start(bf16[15,16,128]{2,1,0:T(8,128)(2,1)S(1)} %get-tuple-element.32), channel_id=1, source_target_pairs={{0,1},{1,0},{2,3},{3,2},{4,5},{5,4},{6,7},{7,6},{8,9},{9,8},{10,11... | collective-permute-start | bytes 184328 | tf_op jit(solution)/shard_map/ppermute | solution.py:599
  17.3 7.8 %collective-permute-start.1 = (bf16[15,16,128]{2,1,0:T(8,128)(2,1)S(1)}, bf16[15,16,128]{2,1,0:T(8,128)(2,1)S(1)}, u32[]{:S(2)}, u32[]{:S(2)}) collective-permute-start(bf16[15,16,128]{2,1,0:T(8,128)(2,1)S(1)} %get-tuple-element.33), channel_id=1, source_target_pairs={{0,2},{1,3},{2,0},{3,1},{4,6},{5,7},{6,4},{7,5},{8,10},{9,11},{10,... | collective-permute-start | bytes 184328 | tf_op jit(solution)/shard_map/ppermute | solution.py:599
  19.9 6.0 %collective-permute-start.2 = (bf16[15,16,128]{2,1,0:T(8,128)(2,1)S(1)}, bf16[15,16,128]{2,1,0:T(8,128)(2,1)S(1)}, u32[]{:S(2)}, u32[]{:S(2)}) collective-permute-start(bf16[15,16,128]{2,1,0:T(8,128)(2,1)S(1)} %get-tuple-element.34), channel_id=1, source_target_pairs={{0,3},{1,2},{2,1},{3,0},{4,7},{5,6},{6,5},{7,4},{8,11},{9,10},{10,... | collective-permute-start | bytes 184328 | tf_op jit(solution)/shard_map/ppermute | solution.py:599
  19.9 10.9 %copy-start.1 = (bf16[256,64,64]{0,2,1:T(8,128)(2,1)S(1)}, bf16[256,64,64]{0,2,1:T(8,128)(2,1)}, u32[]{:S(2)}) copy-start(bf16[256,64,64]{0,2,1:T(8,128)(2,1)} %param.12) | copy-start | bytes 6291460
  19.9 10.9 %copy-start.2 = (bf16[128,64,64]{0,2,1:T(8,128)(2,1)S(1)}, bf16[128,64,64]{0,2,1:T(8,128)(2,1)}, u32[]{:S(2)}) copy-start(bf16[128,64,64]{0,2,1:T(8,128)(2,1)} %param.15) | copy-start | bytes 3145732
  25.9 15.2 %collective-permute-start.3 = (bf16[66,16,128]{2,1,0:T(8,128)(2,1)S(1)}, bf16[66,16,128]{2,1,0:T(8,128)(2,1)S(1)}, u32[]{:S(2)}, u32[]{:S(2)}) collective-permute-start(bf16[66,16,128]{2,1,0:T(8,128)(2,1)S(1)} %shard_map.122.refs_0_), channel_id=1, source_target_pairs={{0,8},{4,12},{8,0},{12,4},{16,24},{20,28},{24,16},{28,20},{1,9},{5... | collective-permute-start | bytes 811016 | tf_op jit(solution)/shard_map/ppermute | solution.py:599
  27.5 13.7 %collective-permute-start.4 = (bf16[66,16,128]{2,1,0:T(8,128)(2,1)S(1)}, bf16[66,16,128]{2,1,0:T(8,128)(2,1)S(1)}, u32[]{:S(2)}, u32[]{:S(2)}) collective-permute-start(bf16[66,16,128]{2,1,0:T(8,128)(2,1)S(1)} %shard_map.122.refs_0_), channel_id=1, source_target_pairs={{0,16},{4,20},{8,24},{12,28},{16,0},{20,4},{24,8},{28,12},{1,17},{... | collective-permute-start | bytes 811016 | tf_op jit(solution)/shard_map/ppermute | solution.py:599
  29.0 12.1 %collective-permute-start.5 = (bf16[66,16,128]{2,1,0:T(8,128)(2,1)S(1)}, bf16[66,16,128]{2,1,0:T(8,128)(2,1)S(1)}, u32[]{:S(2)}, u32[]{:S(2)}) collective-permute-start(bf16[66,16,128]{2,1,0:T(8,128)(2,1)S(1)} %shard_map.122.refs_0_), channel_id=1, source_target_pairs={{0,24},{4,28},{8,16},{12,20},{16,8},{20,12},{24,0},{28,4},{1,25},{... | collective-permute-start | bytes 811016 | tf_op jit(solution)/shard_map/ppermute | solution.py:599
  29.5 11.7 %collective-permute-start.6 = (bf16[12,80,128]{2,1,0:T(8,128)(2,1)S(1)}, bf16[12,80,128]{2,1,0:T(8,128)(2,1)S(1)}, u32[]{:S(2)}, u32[]{:S(2)}) collective-permute-start(bf16[12,80,128]{2,1,0:T(8,128)(2,1)S(1)} %get-tuple-element.41.refs_4_), channel_id=1, source_target_pairs={{0,2},{1,3},{2,0},{3,1},{4,6},{5,7},{6,4},{7,5},{8,10},{9,11},{10,... | collective-permute-start | bytes 737288 | tf_op jit(solution)/shard_map/ppermute | solution.py:599
  35.1 9.5 %copy-start.4 = (s32[256,2]{0,1:T(2,128)S(1)}, s32[256,2]{0,1:T(2,128)}, u32[]{:S(2)}) copy-start(s32[256,2]{0,1:T(2,128)} %param.13) | copy-start | bytes 6148
  35.1 9.5 %copy-start.5 = (s32[128,2]{0,1:T(2,128)S(1)}, s32[128,2]{0,1:T(2,128)}, u32[]{:S(2)}) copy-start(s32[128,2]{0,1:T(2,128)} %param.16) | copy-start | bytes 3076
  41.2 2.8 %collective-permute-start.7 = (bf16[264,16,128]{2,1,0:T(8,128)(2,1)S(1)}, bf16[264,16,128]{2,1,0:T(8,128)(2,1)S(1)}, u32[]{:S(2)}, u32[]{:S(2)}) collective-permute-start(bf16[264,16,128]{2,1,0:T(8,128)(2,1)S(1)} %get-tuple-element.49.refs_3_), channel_id=1, source_target_pairs={{0,4},{4,0},{8,12},{12,8},{16,20},{20,16},{24,28},{28,24},{1,5},{5... | collective-permute-start | bytes 3244040 | tf_op jit(solution)/shard_map/ppermute | solution.py:599
  41.3 17.8 %collective-permute-start.9 = (bf16[24,80,128]{2,1,0:T(8,128)(2,1)S(1)}, bf16[24,80,128]{2,1,0:T(8,128)(2,1)S(1)}, u32[]{:S(2)}, u32[]{:S(2)}) collective-permute-start(bf16[24,80,128]{2,1,0:T(8,128)(2,1)S(1)} %get-tuple-element.52.refs_5_), channel_id=1, source_target_pairs={{0,1},{1,0},{2,3},{3,2},{4,5},{5,4},{6,7},{7,6},{8,9},{9,8},{10,11... | collective-permute-start | bytes 1474568 | tf_op jit(solution)/shard_map/ppermute | solution.py:599
  44.1 10.1 %collective-permute-start.8 = (f32[4,2,16,128]{3,2,1,0:T(8,128)S(1)}, f32[4,2,16,128]{3,2,1,0:T(8,128)S(1)}, u32[]{:S(2)}, u32[]{:S(2)}) collective-permute-start(f32[4,2,16,128]{3,2,1,0:T(8,128)S(1)} %fusion), channel_id=1, source_target_pairs={{0,2},{1,3},{2,0},{3,1},{4,6},{5,7},{6,4},{7,5},{8,10},{9,11},{10,... | collective-permute-start | bytes 196616 | tf_op jit(solution)/shard_map/ppermute | solution.py:599
  54.2 14.5 %copy-start.3 = (f32[6,64,64]{2,1,0:T(8,128)S(1)}, f32[6,64,64]{2,1,0:T(8,128)}, u32[]{:S(2)}) copy-start(f32[6,64,64]{2,1,0:T(8,128)} %top_ref.1) | copy-start | bytes 294916
  54.2 14.5 %collective-permute-start.10 = (f32[4,2,16,128]{3,2,1,0:T(8,128)S(1)}, f32[4,2,16,128]{3,2,1,0:T(8,128)S(1)}, u32[]{:S(2)}, u32[]{:S(2)}) collective-permute-start(f32[4,2,16,128]{3,2,1,0:T(8,128)S(1)} %add.15.refs_0_), channel_id=1, source_target_pairs={{0,1},{1,0},{2,3},{3,2},{4,5},{5,4},{6,7},{7,6},{8,9},{9,8},{10,11... | collective-permute-start | bytes 196616 | tf_op jit(solution)/shard_map/ppermute | solution.py:599

commit v8 on v7

--- a/solution.py
+++ b/solution.py
@@ -167,17 +167,22 @@
     )
 
 
+def rolled(x, by):
+    return jnp.concatenate([x[:, 2 * K - by :], x[:, : 2 * K - by]], axis=1)
+
+
 def unpack(unit):
+    zero = jnp.zeros_like(unit[0])
     full = []
     for m in range(3):
-        full.append((unit[m], jnp.where(lane(H, K), pltpu.roll(unit[m], K, 1), 0.0)))
-    first = jnp.where(lane(0, H), pltpu.roll(unit[0], K, 1), pltpu.roll(unit[1], 2 * K - H, 1))
-    full.append((first, jnp.where(lane(H, K), pltpu.roll(unit[2], 2 * K - H, 1), 0.0)))
+        full.append((unit[m], jnp.where(lane(H, K), rolled(unit[m], K), zero)))
+    first = jnp.where(lane(0, H), rolled(unit[0], K), rolled(unit[1], 2 * K - H))
+    full.append((first, jnp.where(lane(H, K), rolled(unit[2], 2 * K - H), zero)))
     out = []
     for m, (block0, block2) in enumerate(full):
-        low = unit[3 + m // 2] if m % 2 == 0 else pltpu.roll(unit[3 + m // 2], K, 1)
-        block1 = jnp.where(lane(Q, K), low, 0.0)
-        block3 = jnp.where(lane(K - Q, K), pltpu.roll(low, K - Q, 1), 0.0)
+        low = unit[3 + m // 2] if m % 2 == 0 else rolled(unit[3 + m // 2], K)
+        block1 = jnp.where(lane(Q, K), low, zero)
+        block3 = jnp.where(lane(K - Q, K), rolled(low, K - Q), zero)
         out.append(jnp.concatenate([block0, block1, block2, block3], axis=0)[:, :K])
     return out
 
@@ -396,14 +401,19 @@
             for q, y in zip(at, turned):
                 bt[:, q, :] = y
 
-        cells_ref[pl.ds(LANES * g, LANES)] = bt[...].astype(BF)
+        @pl.loop(0, LANES // TURN)
+        def _(step):
+            at = [step * TURN + u for u in range(TURN)]
+            cells = [unhalf(bt[b].astype(BF)) for b in at]
+            for b, x in zip(at, cells):
+                cells_ref[LANES * g + b] = x
 
 
 def turned_blocks(blocks):
     groups = lane_groups([x.shape[2] for x in blocks])
     return pl.pallas_call(
         functools.partial(turn_kernel, groups),
-        out_shape=jax.ShapeDtypeStruct((LANES * len(groups), H, 2 * K), BF),
+        out_shape=jax.ShapeDtypeStruct((LANES * len(groups), K, K), BF),
         in_specs=[VMEM] * len(blocks),
         out_specs=VMEM,
         scratch_shapes=[pltpu.VMEM((LANES, H, 2 * K), F32)],
@@ -487,13 +497,13 @@
             first = p * length + e * step
             if packed(parts):
                 for g in range(parts // 4):
-                    found += unpack([ref[first + 5 * g + n].astype(F32) for n in range(5)])
+                    found += unpack([ref[first + 5 * g + n] for n in range(5)])
             else:
                 for r in range(parts):
                     two = [ref[first + 2 * r + n] for n in range(2)]
                     found.append(unhalf(jnp.concatenate(two, axis=0)))
         for n, x in enumerate(found):
-            table[start + p * count + n] = x.astype(BF)
+            table[start + p * count + n] = x
 
 
 def middle_kernel(groups, sizes, at_ref, *refs):
@@ -506,18 +516,17 @@
         def _(step):
             at = [step * SLOTS + u for u in range(SLOTS)]
             cols = [table[column_entry(sizes, at_ref, level, pairs[level][1, first + b])] for b in at]
-            cells = [unhalf(cells_ref[LANES * g + b]) for b in at]
+            cells = [cells_ref[LANES * g + b] for b in at]
             y = [lax.dot_general(x, c, NT, preferred_element_type=F32) for x, c in zip(cells, cols)]
-            y = [halve(z.astype(BF)) for z in y]
             for b, z in zip(at, y):
-                out_ref[LANES * g + b] = z
+                out_ref[LANES * g + b] = z.astype(BF)
 
 
 def middle_products(sizes, at, pairs, cells, same_core, other_core):
     groups = lane_groups([x.shape[1] for x in pairs])
     return pl.pallas_call(
         functools.partial(middle_kernel, groups, sizes),
-        out_shape=jax.ShapeDtypeStruct(cells.shape, BF),
+        out_shape=jax.ShapeDtypeStruct((cells.shape[0], K, K), BF),
         in_specs=[SMEM] * (1 + len(pairs)) + [VMEM] * 3,
         out_specs=VMEM,
         scratch_shapes=[pltpu.VMEM((sizes[2] * (sizes[0] + sizes[0] // 2), K, K), BF)],
@@ -539,10 +548,10 @@
             def _(step):
                 at = [step * together + g for g in range(together)]
                 units = [[piece[n * packs + g, Q * u : Q * (u + 1)] for u in range(5)] for g in at]
-                full = [unpack([x.astype(F32) for x in five]) for five in units]
+                full = [unpack(five) for five in units]
                 for g, four in zip(at, full):
                     for m in range(4):
-                        table[4 * (e * packs + g) + m] = four[m].astype(BF)
+                        table[4 * (e * packs + g) + m] = four[m]
 
     copies = []
     for g, (which, first) in enumerate(groups):
@@ -551,7 +560,7 @@
         def _(step):
             at = [step * SLOTS + u for u in range(SLOTS)]
             rows = [table[row_entry(sizes, at_ref, which, pairs[which][0, first + b])] for b in at]
-            right = [unhalf(middle_ref[LANES * g + b]) for b in at]
+            right = [middle_ref[LANES * g + b] for b in at]
             y = [lax.dot_general(r, x, NN, preferred_element_type=F32) for r, x in zip(rows, right)]
             y = [halve(z) for z in y]
             for b, z in zip(at, y):

time: 74.6 us -> 74.1 us (level)
    pallas_call x1, Pallas kernels: 8.78 us -> 6.36 us  [middle_products(): pl.pallas_call(functools.partial(middle_kernel, groups, sizes), out_shape...]
    pallas_call x1, Pallas kernels: 4.37 us -> 6.65 us  [turned_blocks(): pl.pallas_call(functools.partial(turn_kernel, groups), out_shape=jax.Shap...]
where the time goes in v8:
time: 74.1 us; the launch traced here: 74 us
  Pallas kernels  46.6 us (63%)
  starting transfers between devices  14.8 us (20%)
  waiting for transfers between devices  10.3 us (14%)
  between operations  2.09 us (3%)
    ppermute x11, starting transfers between devices, swapped(): lax.ppermute(x, axis, [(i, i ^ d) for i in range(lax.axis_size(axis))])  14.8 us
    pallas_call x1, Pallas kernels, own_factors(): pl.pallas_call(functools.partial(factor_kernel, own, cols), out_shape=sha...  13.5 us
    ppermute x11, waiting for transfers between devices, swapped(): lax.ppermute(x, axis, [(i, i ^ d) for i in range(lax.axis_size(axis))])  10.3 us
    pallas_call x1, Pallas kernels, outer_products(): pl.pallas_call(functools.partial(outer_kernel, groups, sizes, len(slots),...  9.04 us
    pallas_call x1, Pallas kernels, turned_blocks(): pl.pallas_call(functools.partial(turn_kernel, groups), out_shape=jax.Shap...  6.65 us
    pallas_call x1, Pallas kernels, middle_products(): pl.pallas_call(functools.partial(middle_kernel, groups, sizes), out_shape...  6.36 us
    pallas_call x1, Pallas kernels, top_factors(): pl.pallas_call(functools.partial(top_kernel, leaves), out_shape=(jax.Shap...  5.8 us
    pallas_call x1, Pallas kernels, lifted_root(): pl.pallas_call(functools.partial(chain_kernel, own, cols), out_shape=jax....  5.16 us
  transfers between devices with their start and end apart: 11, of which 4 were waited for; matrix products, arithmetic and copies ran while one was open for 0% of the time, Pallas kernels for 37%

profile of v8, /device:TPU:0, one launch (start us, length us, event | category | flops | bytes accessed | tf_op | source)
XLA Modules:
  0.0 74.0 jit_solution(12298473659395683594)
XLA Ops:
  0.6 0.1 pad_add_fusion.at_ref
  0.7 13.5 %shard_map.120 = (bf16[12,80,128]{2,1,0:T(8,128)(2,1)S(1)}, f32[16,64,64]{2,1,0:T(8,128)S(1)}, bf16[15,16,128]{2,1,0:T(8,128)(2,1)S(1)}, bf16[15,16,128]{2,1,0:T...) custom-call(s32[2]{0:T(128)S(1)} %pad_add_fusion.at_ref, ...), custom_call_target="tpu_custom_call" | custom-call | flops 536870912 | bytes 8388608 | tf_op jit(solution)/shard_map/pallas_call | solution.py:258
  14.2 3.1 %collective-permute-start = (bf16[15,16,128]{2,1,0:T(8,128)(2,1)S(1)}, bf16[15,16,128]{2,1,0:T(8,128)(2,1)S(1)}, u32[]{:S(2)}, u32[]{:S(2)}) collective-permute-start(bf16[15,16,128]{2,1,0:T(8,128)(2,1)S(1)} %get-tuple-element.32), channel_id=1, source_target_pairs={{0,1},{1,0},{2,3},{3,2},{4,5},{5,4},{6,7},{7,6},{8,9},{9,8},{10,11... | collective-permute-start | bytes 184328 | tf_op jit(solution)/shard_map/ppermute | solution.py:608
  17.3 2.6 %collective-permute-start.1 = (bf16[15,16,128]{2,1,0:T(8,128)(2,1)S(1)}, bf16[15,16,128]{2,1,0:T(8,128)(2,1)S(1)}, u32[]{:S(2)}, u32[]{:S(2)}) collective-permute-start(bf16[15,16,128]{2,1,0:T(8,128)(2,1)S(1)} %get-tuple-element.33), channel_id=1, source_target_pairs={{0,2},{1,3},{2,0},{3,1},{4,6},{5,7},{6,4},{7,5},{8,10},{9,11},{10,... | collective-permute-start | bytes 184328 | tf_op jit(solution)/shard_map/ppermute | solution.py:608
  19.9 0.0 collective-permute-start.2
  19.9 5.2 %shard_map.121.refs_4_ = bf16[6,16,128]{2,1,0:T(8,128)(2,1)S(1)} custom-call(s32[2]{0:T(128)S(1)} %pad_add_fusion.at_ref, f32[16,64,64]{2,1,0:T(8,128)S(1)} %get-tuple-element.35.gram1_ref, f32[64,64,255]{2,1,0:T(8,128)S(1)} %bitcast.11), custom_call_target="tpu_custom_call" | custom-call | flops 536870912 | bytes 4194304 | tf_op jit(solution)/shard_map/pallas_call | solution.py:320
  25.0 0.0 collective-permute-done.refs_1_
  25.0 0.0 collective-permute-done.1.refs_2_
  25.1 0.8 %collective-permute-done.2.refs_3_ = bf16[15,16,128]{2,1,0:T(8,128)(2,1)S(1)} collective-permute-done((bf16[15,16,128]{2,1,0:T(8,128)(2,1)S(1)}, bf16[15,16,128]{2,1,0:T(8,128)(2,1)S(1)}, u32[]{:S(2)}, u32[]{:S(2)}) %collective-permute-start.2) | collective-permute-done | bytes 61472 | tf_op jit(solution)/shard_map/ppermute | solution.py:608
  25.9 1.6 %collective-permute-start.3 = (bf16[66,16,128]{2,1,0:T(8,128)(2,1)S(1)}, bf16[66,16,128]{2,1,0:T(8,128)(2,1)S(1)}, u32[]{:S(2)}, u32[]{:S(2)}) collective-permute-start(bf16[66,16,128]{2,1,0:T(8,128)(2,1)S(1)} %shard_map.122.refs_0_), channel_id=1, source_target_pairs={{0,8},{4,12},{8,0},{12,4},{16,24},{20,28},{24,16},{28,20},{1,9},{5... | collective-permute-start | bytes 811016 | tf_op jit(solution)/shard_map/ppermute | solution.py:608
  27.5 1.5 %collective-permute-start.4 = (bf16[66,16,128]{2,1,0:T(8,128)(2,1)S(1)}, bf16[66,16,128]{2,1,0:T(8,128)(2,1)S(1)}, u32[]{:S(2)}, u32[]{:S(2)}) collective-permute-start(bf16[66,16,128]{2,1,0:T(8,128)(2,1)S(1)} %shard_map.122.refs_0_), channel_id=1, source_target_pairs={{0,16},{4,20},{8,24},{12,28},{16,0},{20,4},{24,8},{28,12},{1,17},{... | collective-permute-start | bytes 811016 | tf_op jit(solution)/shard_map/ppermute | solution.py:608
  29.0 0.5 collective-permute-start.5
  29.5 1.3 %collective-permute-start.6 = (bf16[12,80,128]{2,1,0:T(8,128)(2,1)S(1)}, bf16[12,80,128]{2,1,0:T(8,128)(2,1)S(1)}, u32[]{:S(2)}, u32[]{:S(2)}) collective-permute-start(bf16[12,80,128]{2,1,0:T(8,128)(2,1)S(1)} %get-tuple-element.41.refs_4_), channel_id=1, source_target_pairs={{0,2},{1,3},{2,0},{3,1},{4,6},{5,7},{6,4},{7,5},{8,10},{9,11},{10,... | collective-permute-start | bytes 737288 | tf_op jit(solution)/shard_map/ppermute | solution.py:608
  30.7 6.6 %shard_map.123.refs_2_ = bf16[384,64,64]{2,1,0:T(8,128)(2,1)S(1)} custom-call(bf16[64,64,256]{2,1,0:T(8,128)(2,1)S(1)} %bitcast.12, bf16[64,64,128]{2,1,0:T(8,128)(2,1)S(1)} %bitcast.14), custom_call_target="tpu_custom_call" | custom-call | flops 1048576 | bytes 1048576 | tf_op jit(solution)/shard_map/pallas_call | solution.py:414
  37.4 0.0 copy-start.4
  37.4 0.0 copy-start.5
  37.4 3.7 %collective-permute-done.6.refs_5_ = bf16[12,80,128]{2,1,0:T(8,128)(2,1)S(1)} collective-permute-done((bf16[12,80,128]{2,1,0:T(8,128)(2,1)S(1)}, bf16[12,80,128]{2,1,0:T(8,128)(2,1)S(1)}, u32[]{:S(2)}, u32[]{:S(2)}) %collective-permute-start.6) | collective-permute-done | bytes 245792 | tf_op jit(solution)/shard_map/ppermute | solution.py:608
  41.1 0.0 collective-permute-done.3.refs_1_
  41.1 0.0 collective-permute-done.4.refs_2_
  41.1 0.0 collective-permute-done.5.refs_3_
  41.1 0.1 shard_map.124
  41.2 0.1 collective-permute-start.7
  41.3 0.1 collective-permute-start.9
  41.4 2.6 %collective-permute-done.7.refs_4_ = bf16[264,16,128]{2,1,0:T(8,128)(2,1)S(1)} collective-permute-done((bf16[264,16,128]{2,1,0:T(8,128)(2,1)S(1)}, bf16[264,16,128]{2,1,0:T(8,128)(2,1)S(1)}, u32[]{:S(2)}, u32[]{:S(2)}) %collective-permute-start.7) | collective-permute-done | bytes 1081376 | tf_op jit(solution)/shard_map/ppermute | solution.py:608
  44.1 0.5 collective-permute-start.8
  44.6 6.4 %shard_map.125.refs_4_ = bf16[384,64,64]{2,1,0:T(8,128)(2,1)S(1)} custom-call(s32[2]{0:T(128)S(1)} %pad_add_fusion.at_ref, s32[2,256]{1,0:T(2,128)S(1)} %bitcast.15, s32[2,128]{1,0:T(2,128)S(1)} %bitcast.17, bf16[384,64,64]{2,1,0:T(8,128)(2,1)S(1)} %shard_map.123.refs_2_, bf16[264,16,128]{2,1,0:T(8,128)(2,1)S(1)} %get-tuple-element.49.refs_3_, ...), custom_call_target="tpu_custom_call" | custom-call | flops 201326592 | bytes 1048576 | tf_op jit(solution)/shard_map/pallas_call | solution.py:527
  51.0 3.2 %collective-permute-done.8 = f32[4,2,16,128]{3,2,1,0:T(8,128)S(1)} collective-permute-done((f32[4,2,16,128]{3,2,1,0:T(8,128)S(1)}, f32[4,2,16,128]{3,2,1,0:T(8,128)S(1)}, u32[]{:S(2)}, u32[]{:S(2)}) %collective-permute-start.8) | collective-permute-done | bytes 65568 | tf_op jit(solution)/shard_map/ppermute | solution.py:608
  54.2 3.6 %collective-permute-start.10 = (f32[4,2,16,128]{3,2,1,0:T(8,128)S(1)}, f32[4,2,16,128]{3,2,1,0:T(8,128)S(1)}, u32[]{:S(2)}, u32[]{:S(2)}) collective-permute-start(f32[4,2,16,128]{3,2,1,0:T(8,128)S(1)} %add.15.refs_0_), channel_id=1, source_target_pairs={{0,1},{1,0},{2,3},{3,2},{4,5},{5,4},{6,7},{7,6},{8,9},{9,8},{10,11... | collective-permute-start | bytes 196616 | tf_op jit(solution)/shard_map/ppermute | solution.py:608
  59.1 0.0 copy-start.3
  59.1 0.0 collective-permute-done.9.refs_6_
  59.1 9.0 %shard_map.126 = (bf16[64,64,256]{2,1,0:T(8,128)(2,1)}, bf16[64,64,128]{2,1,0:T(8,128)(2,1)}) custom-call(s32[2]{0:T(128)S(1)} %pad_add_fusion.at_ref, s32[2,256]{1,0:T(2,128)S(1)} %bitcast.16, s32[2,128]{1,0:T(2,128)S(1)} %bitcast.18, s32[1]{0:T(128)S(6)} %copy.13.refs_2_, s32[1]{0:T(128)S(6)} %copy.14.refs_3_, ...), custom_call_target="tpu_custom_call" | custom-call | flops 201326592 | bytes 4194304 | tf_op jit(solution)/shard_map/pallas_call | solution.py:591
  68.2 5.8 %shard_map.127 = (f32[1,3,64,64]{3,2,1,0:T(8,128)}, f32[64,64]{1,0:T(8,128)}) custom-call(s32[2]{0:T(128)S(1)} %pad_add_fusion.at_ref, f32[6,64,64]{2,1,0:T(8,128)S(1)} %copy-done.3, f32[4,2,16,128]{3,2,1,0:T(8,128)S(1)} %add.15.refs_0_, f32[4,2,16,128]{3,2,1,0:T(8,128)S(1)} %collective-permute-done.10.refs_1_), custom_call_target="tpu_custom_call" | custom-call | flops 4194304 | bytes 131072 | tf_op jit(solution)/shard_map/pallas_call | solution.py:368
  (14 shorter events, 0.1 us)
Async XLA Ops:
  0.7 19.2 %copy-start = (f32[255,64,64]{0,2,1:T(8,128)S(1)}, f32[255,64,64]{0,2,1:T(8,128)}, u32[]{:S(2)}) copy-start(f32[255,64,64]{0,2,1:T(8,128)} %param.10) | copy-start | bytes 12533764
  14.2 10.8 %collective-permute-start = (bf16[15,16,128]{2,1,0:T(8,128)(2,1)S(1)}, bf16[15,16,128]{2,1,0:T(8,128)(2,1)S(1)}, u32[]{:S(2)}, u32[]{:S(2)}) collective-permute-start(bf16[15,16,128]{2,1,0:T(8,128)(2,1)S(1)} %get-tuple-element.32), channel_id=1, source_target_pairs={{0,1},{1,0},{2,3},{3,2},{4,5},{5,4},{6,7},{7,6},{8,9},{9,8},{10,11... | collective-permute-start | bytes 184328 | tf_op jit(solution)/shard_map/ppermute | solution.py:608
  17.3 7.8 %collective-permute-start.1 = (bf16[15,16,128]{2,1,0:T(8,128)(2,1)S(1)}, bf16[15,16,128]{2,1,0:T(8,128)(2,1)S(1)}, u32[]{:S(2)}, u32[]{:S(2)}) collective-permute-start(bf16[15,16,128]{2,1,0:T(8,128)(2,1)S(1)} %get-tuple-element.33), channel_id=1, source_target_pairs={{0,2},{1,3},{2,0},{3,1},{4,6},{5,7},{6,4},{7,5},{8,10},{9,11},{10,... | collective-permute-start | bytes 184328 | tf_op jit(solution)/shard_map/ppermute | solution.py:608
  19.9 6.0 %collective-permute-start.2 = (bf16[15,16,128]{2,1,0:T(8,128)(2,1)S(1)}, bf16[15,16,128]{2,1,0:T(8,128)(2,1)S(1)}, u32[]{:S(2)}, u32[]{:S(2)}) collective-permute-start(bf16[15,16,128]{2,1,0:T(8,128)(2,1)S(1)} %get-tuple-element.34), channel_id=1, source_target_pairs={{0,3},{1,2},{2,1},{3,0},{4,7},{5,6},{6,5},{7,4},{8,11},{9,10},{10,... | collective-permute-start | bytes 184328 | tf_op jit(solution)/shard_map/ppermute | solution.py:608
  19.9 10.9 %copy-start.1 = (bf16[256,64,64]{0,2,1:T(8,128)(2,1)S(1)}, bf16[256,64,64]{0,2,1:T(8,128)(2,1)}, u32[]{:S(2)}) copy-start(bf16[256,64,64]{0,2,1:T(8,128)(2,1)} %param.12) | copy-start | bytes 6291460
  19.9 10.9 %copy-start.2 = (bf16[128,64,64]{0,2,1:T(8,128)(2,1)S(1)}, bf16[128,64,64]{0,2,1:T(8,128)(2,1)}, u32[]{:S(2)}) copy-start(bf16[128,64,64]{0,2,1:T(8,128)(2,1)} %param.15) | copy-start | bytes 3145732
  25.9 15.2 %collective-permute-start.3 = (bf16[66,16,128]{2,1,0:T(8,128)(2,1)S(1)}, bf16[66,16,128]{2,1,0:T(8,128)(2,1)S(1)}, u32[]{:S(2)}, u32[]{:S(2)}) collective-permute-start(bf16[66,16,128]{2,1,0:T(8,128)(2,1)S(1)} %shard_map.122.refs_0_), channel_id=1, source_target_pairs={{0,8},{4,12},{8,0},{12,4},{16,24},{20,28},{24,16},{28,20},{1,9},{5... | collective-permute-start | bytes 811016 | tf_op jit(solution)/shard_map/ppermute | solution.py:608
  27.5 13.7 %collective-permute-start.4 = (bf16[66,16,128]{2,1,0:T(8,128)(2,1)S(1)}, bf16[66,16,128]{2,1,0:T(8,128)(2,1)S(1)}, u32[]{:S(2)}, u32[]{:S(2)}) collective-permute-start(bf16[66,16,128]{2,1,0:T(8,128)(2,1)S(1)} %shard_map.122.refs_0_), channel_id=1, source_target_pairs={{0,16},{4,20},{8,24},{12,28},{16,0},{20,4},{24,8},{28,12},{1,17},{... | collective-permute-start | bytes 811016 | tf_op jit(solution)/shard_map/ppermute | solution.py:608
  29.0 12.1 %collective-permute-start.5 = (bf16[66,16,128]{2,1,0:T(8,128)(2,1)S(1)}, bf16[66,16,128]{2,1,0:T(8,128)(2,1)S(1)}, u32[]{:S(2)}, u32[]{:S(2)}) collective-permute-start(bf16[66,16,128]{2,1,0:T(8,128)(2,1)S(1)} %shard_map.122.refs_0_), channel_id=1, source_target_pairs={{0,24},{4,28},{8,16},{12,20},{16,8},{20,12},{24,0},{28,4},{1,25},{... | collective-permute-start | bytes 811016 | tf_op jit(solution)/shard_map/ppermute | solution.py:608
  29.5 11.7 %collective-permute-start.6 = (bf16[12,80,128]{2,1,0:T(8,128)(2,1)S(1)}, bf16[12,80,128]{2,1,0:T(8,128)(2,1)S(1)}, u32[]{:S(2)}, u32[]{:S(2)}) collective-permute-start(bf16[12,80,128]{2,1,0:T(8,128)(2,1)S(1)} %get-tuple-element.41.refs_4_), channel_id=1, source_target_pairs={{0,2},{1,3},{2,0},{3,1},{4,6},{5,7},{6,4},{7,5},{8,10},{9,11},{10,... | collective-permute-start | bytes 737288 | tf_op jit(solution)/shard_map/ppermute | solution.py:608
  37.4 7.2 %copy-start.4 = (s32[256,2]{0,1:T(2,128)S(1)}, s32[256,2]{0,1:T(2,128)}, u32[]{:S(2)}) copy-start(s32[256,2]{0,1:T(2,128)} %param.13) | copy-start | bytes 6148
  37.4 7.2 %copy-start.5 = (s32[128,2]{0,1:T(2,128)S(1)}, s32[128,2]{0,1:T(2,128)}, u32[]{:S(2)}) copy-start(s32[128,2]{0,1:T(2,128)} %param.16) | copy-start | bytes 3076
  41.2 2.8 %collective-permute-start.7 = (bf16[264,16,128]{2,1,0:T(8,128)(2,1)S(1)}, bf16[264,16,128]{2,1,0:T(8,128)(2,1)S(1)}, u32[]{:S(2)}, u32[]{:S(2)}) collective-permute-start(bf16[264,16,128]{2,1,0:T(8,128)(2,1)S(1)} %get-tuple-element.49.refs_3_), channel_id=1, source_target_pairs={{0,4},{4,0},{8,12},{12,8},{16,20},{20,16},{24,28},{28,24},{1,5},{5... | collective-permute-start | bytes 3244040 | tf_op jit(solution)/shard_map/ppermute | solution.py:608
  41.3 17.8 %collective-permute-start.9 = (bf16[24,80,128]{2,1,0:T(8,128)(2,1)S(1)}, bf16[24,80,128]{2,1,0:T(8,128)(2,1)S(1)}, u32[]{:S(2)}, u32[]{:S(2)}) collective-permute-start(bf16[24,80,128]{2,1,0:T(8,128)(2,1)S(1)} %get-tuple-element.52.refs_5_), channel_id=1, source_target_pairs={{0,1},{1,0},{2,3},{3,2},{4,5},{5,4},{6,7},{7,6},{8,9},{9,8},{10,11... | collective-permute-start | bytes 1474568 | tf_op jit(solution)/shard_map/ppermute | solution.py:608
  44.1 10.1 %collective-permute-start.8 = (f32[4,2,16,128]{3,2,1,0:T(8,128)S(1)}, f32[4,2,16,128]{3,2,1,0:T(8,128)S(1)}, u32[]{:S(2)}, u32[]{:S(2)}) collective-permute-start(f32[4,2,16,128]{3,2,1,0:T(8,128)S(1)} %fusion), channel_id=1, source_target_pairs={{0,2},{1,3},{2,0},{3,1},{4,6},{5,7},{6,4},{7,5},{8,10},{9,11},{10,... | collective-permute-start | bytes 196616 | tf_op jit(solution)/shard_map/ppermute | solution.py:608
  54.2 14.0 %collective-permute-start.10 = (f32[4,2,16,128]{3,2,1,0:T(8,128)S(1)}, f32[4,2,16,128]{3,2,1,0:T(8,128)S(1)}, u32[]{:S(2)}, u32[]{:S(2)}) collective-permute-start(f32[4,2,16,128]{3,2,1,0:T(8,128)S(1)} %add.15.refs_0_), channel_id=1, source_target_pairs={{0,1},{1,0},{2,3},{3,2},{4,5},{5,4},{6,7},{7,6},{8,9},{9,8},{10,11... | collective-permute-start | bytes 196616 | tf_op jit(solution)/shard_map/ppermute | solution.py:608
  59.1 9.1 %copy-start.3 = (f32[6,64,64]{2,1,0:T(8,128)S(1)}, f32[6,64,64]{2,1,0:T(8,128)}, u32[]{:S(2)}) copy-start(f32[6,64,64]{2,1,0:T(8,128)} %top_ref.1) | copy-start | bytes 294916

commit v9 on v8

--- a/solution.py
+++ b/solution.py
@@ -648,15 +648,13 @@
     for t in range(1, TERMS):
         other_part = other_part + there[:, 2 * t : 2 * t + 2]
     pair_part = pair_part + other_part
-    for d in range(1, bits(cols)):
-        pair_part = pair_part + swapped(pair_part, "col", cols >> d)
+    tops = [pair_part] + [swapped(pair_part, "col", d) for d in range(1, cols)]
     middle = middle_products(sizes, at, pairs, cells, same_core, other_core)
-    pair_part, middle = lax.optimization_barrier((pair_part, middle))
-    tops = [pair_part, swapped(pair_part, "col", 1)]
+    ancestors, root = top_factors(at, tops, top_transfer, leaves)
+    middle, ancestors, root = lax.optimization_barrier((middle, ancestors, root))
     out0, out1 = outer_products(
         sizes, at, pairs, (counts0, counts1), middle, [rows, forwarded], orders
     )
-    ancestors, root = top_factors(at, tops, top_transfer, leaves)
     return (jnp.transpose(out0, (2, 0, 1)), jnp.transpose(out1, (2, 0, 1)), root, ancestors)
 
 

time: 74.1 us -> 75.1 us (1.013)
    ppermute x11 -> x12, waiting for transfers between devices: 10.3 us -> 10.9 us  [swapped(): lax.ppermute(x, axis, [(i, i ^ d) for i in range(lax.axis_size(axis))])]
    ppermute x11 -> x12, starting transfers between devices: 14.8 us -> 15.1 us  [swapped(): lax.ppermute(x, axis, [(i, i ^ d) for i in range(lax.axis_size(axis))])]
  transfers between devices with their start and end apart: 11 -> 12, of which waited for: 4 -> 5; matrix products, arithmetic and copies ran while one was open for 0% -> 0% of each run, Pallas kernels for 37% -> 32%
where the time goes in v9:
time: 75.1 us; the launch traced here: 74.9 us
  Pallas kernels  46.6 us (62%)
  starting transfers between devices  15.1 us (20%)
  waiting for transfers between devices  10.9 us (15%)
  between operations  2.24 us (3%)
    ppermute x12, starting transfers between devices, swapped(): lax.ppermute(x, axis, [(i, i ^ d) for i in range(lax.axis_size(axis))])  15.1 us
    pallas_call x1, Pallas kernels, own_factors(): pl.pallas_call(functools.partial(factor_kernel, own, cols), out_shape=sha...  13.5 us
    ppermute x12, waiting for transfers between devices, swapped(): lax.ppermute(x, axis, [(i, i ^ d) for i in range(lax.axis_size(axis))])  10.9 us
    pallas_call x1, Pallas kernels, outer_products(): pl.pallas_call(functools.partial(outer_kernel, groups, sizes, len(slots),...  9.03 us
    pallas_call x1, Pallas kernels, turned_blocks(): pl.pallas_call(functools.partial(turn_kernel, groups), out_shape=jax.Shap...  6.65 us
    pallas_call x1, Pallas kernels, middle_products(): pl.pallas_call(functools.partial(middle_kernel, groups, sizes), out_shape...  6.36 us
    pallas_call x1, Pallas kernels, top_factors(): pl.pallas_call(functools.partial(top_kernel, leaves), out_shape=(jax.Shap...  5.8 us
    pallas_call x1, Pallas kernels, lifted_root(): pl.pallas_call(functools.partial(chain_kernel, own, cols), out_shape=jax....  5.16 us
  transfers between devices with their start and end apart: 12, of which 5 were waited for; matrix products, arithmetic and copies ran while one was open for 0% of the time, Pallas kernels for 32%

profile of v9, /device:TPU:0, one launch (start us, length us, event | category | flops | bytes accessed | tf_op | source)
XLA Modules:
  0.0 74.9 jit_solution(6170563703491566950)
XLA Ops:
  0.6 0.1 pad_add_fusion.at_ref
  0.7 13.5 %shard_map.120 = (bf16[12,80,128]{2,1,0:T(8,128)(2,1)S(1)}, f32[16,64,64]{2,1,0:T(8,128)S(1)}, bf16[15,16,128]{2,1,0:T(8,128)(2,1)S(1)}, bf16[15,16,128]{2,1,0:T...) custom-call(s32[2]{0:T(128)S(1)} %pad_add_fusion.at_ref, ...), custom_call_target="tpu_custom_call" | custom-call | flops 536870912 | bytes 8388608 | tf_op jit(solution)/shard_map/pallas_call | solution.py:258
  14.2 3.1 %collective-permute-start = (bf16[15,16,128]{2,1,0:T(8,128)(2,1)S(1)}, bf16[15,16,128]{2,1,0:T(8,128)(2,1)S(1)}, u32[]{:S(2)}, u32[]{:S(2)}) collective-permute-start(bf16[15,16,128]{2,1,0:T(8,128)(2,1)S(1)} %get-tuple-element.33), channel_id=1, source_target_pairs={{0,1},{1,0},{2,3},{3,2},{4,5},{5,4},{6,7},{7,6},{8,9},{9,8},{10,11... | collective-permute-start | bytes 184328 | tf_op jit(solution)/shard_map/ppermute | solution.py:608
  17.3 2.6 %collective-permute-start.1 = (bf16[15,16,128]{2,1,0:T(8,128)(2,1)S(1)}, bf16[15,16,128]{2,1,0:T(8,128)(2,1)S(1)}, u32[]{:S(2)}, u32[]{:S(2)}) collective-permute-start(bf16[15,16,128]{2,1,0:T(8,128)(2,1)S(1)} %get-tuple-element.34), channel_id=1, source_target_pairs={{0,2},{1,3},{2,0},{3,1},{4,6},{5,7},{6,4},{7,5},{8,10},{9,11},{10,... | collective-permute-start | bytes 184328 | tf_op jit(solution)/shard_map/ppermute | solution.py:608
  19.9 5.2 %shard_map.121.refs_4_ = bf16[6,16,128]{2,1,0:T(8,128)(2,1)S(1)} custom-call(s32[2]{0:T(128)S(1)} %pad_add_fusion.at_ref, f32[16,64,64]{2,1,0:T(8,128)S(1)} %get-tuple-element.36.gram1_ref, f32[64,64,255]{2,1,0:T(8,128)S(1)} %bitcast.11), custom_call_target="tpu_custom_call" | custom-call | flops 536870912 | bytes 4194304 | tf_op jit(solution)/shard_map/pallas_call | solution.py:320
  25.0 0.0 collective-permute-done.refs_1_
  25.0 0.0 collective-permute-done.1.refs_2_
  25.1 0.8 %collective-permute-done.2.refs_3_ = bf16[15,16,128]{2,1,0:T(8,128)(2,1)S(1)} collective-permute-done((bf16[15,16,128]{2,1,0:T(8,128)(2,1)S(1)}, bf16[15,16,128]{2,1,0:T(8,128)(2,1)S(1)}, u32[]{:S(2)}, u32[]{:S(2)}) %collective-permute-start.2) | collective-permute-done | bytes 61472 | tf_op jit(solution)/shard_map/ppermute | solution.py:608
  25.9 1.6 %collective-permute-start.3 = (bf16[66,16,128]{2,1,0:T(8,128)(2,1)S(1)}, bf16[66,16,128]{2,1,0:T(8,128)(2,1)S(1)}, u32[]{:S(2)}, u32[]{:S(2)}) collective-permute-start(bf16[66,16,128]{2,1,0:T(8,128)(2,1)S(1)} %shard_map.122.refs_0_), channel_id=1, source_target_pairs={{0,8},{4,12},{8,0},{12,4},{16,24},{20,28},{24,16},{28,20},{1,9},{5... | collective-permute-start | bytes 811016 | tf_op jit(solution)/shard_map/ppermute | solution.py:608
  27.5 1.5 %collective-permute-start.4 = (bf16[66,16,128]{2,1,0:T(8,128)(2,1)S(1)}, bf16[66,16,128]{2,1,0:T(8,128)(2,1)S(1)}, u32[]{:S(2)}, u32[]{:S(2)}) collective-permute-start(bf16[66,16,128]{2,1,0:T(8,128)(2,1)S(1)} %shard_map.122.refs_0_), channel_id=1, source_target_pairs={{0,16},{4,20},{8,24},{12,28},{16,0},{20,4},{24,8},{28,12},{1,17},{... | collective-permute-start | bytes 811016 | tf_op jit(solution)/shard_map/ppermute | solution.py:608
  29.0 0.5 collective-permute-start.5
  29.5 1.3 %collective-permute-start.6 = (bf16[12,80,128]{2,1,0:T(8,128)(2,1)S(1)}, bf16[12,80,128]{2,1,0:T(8,128)(2,1)S(1)}, u32[]{:S(2)}, u32[]{:S(2)}) collective-permute-start(bf16[12,80,128]{2,1,0:T(8,128)(2,1)S(1)} %get-tuple-element.42.refs_4_), channel_id=1, source_target_pairs={{0,2},{1,3},{2,0},{3,1},{4,6},{5,7},{6,4},{7,5},{8,10},{9,11},{10,... | collective-permute-start | bytes 737288 | tf_op jit(solution)/shard_map/ppermute | solution.py:608
  30.7 6.6 %shard_map.123.refs_2_ = bf16[384,64,64]{2,1,0:T(8,128)(2,1)S(1)} custom-call(bf16[64,64,256]{2,1,0:T(8,128)(2,1)S(1)} %bitcast.12, bf16[64,64,128]{2,1,0:T(8,128)(2,1)S(1)} %bitcast.14), custom_call_target="tpu_custom_call" | custom-call | flops 1048576 | bytes 1048576 | tf_op jit(solution)/shard_map/pallas_call | solution.py:414
  37.4 0.0 copy-start.4
  37.4 0.0 copy-start.5
  37.4 3.7 %collective-permute-done.6.refs_5_ = bf16[12,80,128]{2,1,0:T(8,128)(2,1)S(1)} collective-permute-done((bf16[12,80,128]{2,1,0:T(8,128)(2,1)S(1)}, bf16[12,80,128]{2,1,0:T(8,128)(2,1)S(1)}, u32[]{:S(2)}, u32[]{:S(2)}) %collective-permute-start.6) | collective-permute-done | bytes 245792 | tf_op jit(solution)/shard_map/ppermute | solution.py:608
  41.1 0.0 collective-permute-done.3.refs_1_
  41.1 0.0 collective-permute-done.4.refs_2_
  41.1 0.1 shard_map.124
  41.2 0.1 collective-permute-start.7
  41.3 0.1 collective-permute-start.11
  41.4 2.6 %collective-permute-done.7.refs_4_ = bf16[264,16,128]{2,1,0:T(8,128)(2,1)S(1)} collective-permute-done((bf16[264,16,128]{2,1,0:T(8,128)(2,1)S(1)}, bf16[264,16,128]{2,1,0:T(8,128)(2,1)S(1)}, u32[]{:S(2)}, u32[]{:S(2)}) %collective-permute-start.7) | collective-permute-done | bytes 1081376 | tf_op jit(solution)/shard_map/ppermute | solution.py:608
  44.1 0.1 collective-permute-start.8
  44.1 3.1 %collective-permute-start.9 = (f32[4,2,16,128]{3,2,1,0:T(8,128)S(1)}, f32[4,2,16,128]{3,2,1,0:T(8,128)S(1)}, u32[]{:S(2)}, u32[]{:S(2)}) collective-permute-start(f32[4,2,16,128]{3,2,1,0:T(8,128)S(1)} %fusion.refs_0_), channel_id=1, source_target_pairs={{0,2},{1,3},{2,0},{3,1},{4,6},{5,7},{6,4},{7,5},{8,10},{9,11},{10,... | collective-permute-start | bytes 196616 | tf_op jit(solution)/shard_map/ppermute | solution.py:608
  47.2 1.3 %collective-permute-start.10 = (f32[4,2,16,128]{3,2,1,0:T(8,128)S(1)}, f32[4,2,16,128]{3,2,1,0:T(8,128)S(1)}, u32[]{:S(2)}, u32[]{:S(2)}) collective-permute-start(f32[4,2,16,128]{3,2,1,0:T(8,128)S(1)} %fusion.refs_0_), channel_id=1, source_target_pairs={{0,3},{1,2},{2,1},{3,0},{4,7},{5,6},{6,5},{7,4},{8,11},{9,10},{10,... | collective-permute-start | bytes 196616 | tf_op jit(solution)/shard_map/ppermute | solution.py:608
  49.8 0.0 copy-start.3
  49.8 6.4 %shard_map.125.refs_4_ = bf16[384,64,64]{2,1,0:T(8,128)(2,1)S(1)} custom-call(s32[2]{0:T(128)S(1)} %pad_add_fusion.at_ref, s32[2,256]{1,0:T(2,128)S(1)} %bitcast.15, s32[2,128]{1,0:T(2,128)S(1)} %bitcast.17, bf16[384,64,64]{2,1,0:T(8,128)(2,1)S(1)} %shard_map.123.refs_2_, bf16[264,16,128]{2,1,0:T(8,128)(2,1)S(1)} %get-tuple-element.50.refs_3_, ...), custom_call_target="tpu_custom_call" | custom-call | flops 201326592 | bytes 1048576 | tf_op jit(solution)/shard_map/pallas_call | solution.py:527
  56.2 1.5 %collective-permute-done.8.refs_1_ = f32[4,2,16,128]{3,2,1,0:T(8,128)S(1)} collective-permute-done((f32[4,2,16,128]{3,2,1,0:T(8,128)S(1)}, f32[4,2,16,128]{3,2,1,0:T(8,128)S(1)}, u32[]{:S(2)}, u32[]{:S(2)}) %collective-permute-start.8) | collective-permute-done | bytes 65568 | tf_op jit(solution)/shard_map/ppermute | solution.py:608
  57.8 0.0 collective-permute-done.9.refs_2_
  57.8 2.2 %collective-permute-done.10.refs_3_ = f32[4,2,16,128]{3,2,1,0:T(8,128)S(1)} collective-permute-done((f32[4,2,16,128]{3,2,1,0:T(8,128)S(1)}, f32[4,2,16,128]{3,2,1,0:T(8,128)S(1)}, u32[]{:S(2)}, u32[]{:S(2)}) %collective-permute-start.10) | collective-permute-done | bytes 65568 | tf_op jit(solution)/shard_map/ppermute | solution.py:608
  59.9 5.8 %shard_map.126 = (f32[1,3,64,64]{3,2,1,0:T(8,128)}, f32[64,64]{1,0:T(8,128)}) custom-call(s32[2]{0:T(128)S(1)} %pad_add_fusion.at_ref, f32[6,64,64]{2,1,0:T(8,128)S(1)} %copy-done.3, f32[4,2,16,128]{3,2,1,0:T(8,128)S(1)} %fusion.refs_0_, f32[4,2,16,128]{3,2,1,0:T(8,128)S(1)} %collective-permute-done.8.refs_1_, ...), custom_call_target="tpu_custom_call" | custom-call | flops 4194304 | bytes 131072 | tf_op jit(solution)/shard_map/pallas_call | solution.py:368
  65.7 9.0 %shard_map.127 = (bf16[64,64,256]{2,1,0:T(8,128)(2,1)}, bf16[64,64,128]{2,1,0:T(8,128)(2,1)}) custom-call(s32[2]{0:T(128)S(1)} %pad_add_fusion.at_ref, s32[2,256]{1,0:T(2,128)S(1)} %bitcast.16, s32[2,128]{1,0:T(2,128)S(1)} %bitcast.18, s32[1]{0:T(128)S(6)} %copy.13.refs_2_, s32[1]{0:T(128)S(6)} %copy.14.refs_3_, ...), custom_call_target="tpu_custom_call" | custom-call | flops 201326592 | bytes 4194304 | tf_op jit(solution)/shard_map/pallas_call | solution.py:591
  (15 shorter events, 0.1 us)
Async XLA Ops:
  0.7 19.2 %copy-start = (f32[255,64,64]{0,2,1:T(8,128)S(1)}, f32[255,64,64]{0,2,1:T(8,128)}, u32[]{:S(2)}) copy-start(f32[255,64,64]{0,2,1:T(8,128)} %param.10) | copy-start | bytes 12533764
  14.2 10.8 %collective-permute-start = (bf16[15,16,128]{2,1,0:T(8,128)(2,1)S(1)}, bf16[15,16,128]{2,1,0:T(8,128)(2,1)S(1)}, u32[]{:S(2)}, u32[]{:S(2)}) collective-permute-start(bf16[15,16,128]{2,1,0:T(8,128)(2,1)S(1)} %get-tuple-element.33), channel_id=1, source_target_pairs={{0,1},{1,0},{2,3},{3,2},{4,5},{5,4},{6,7},{7,6},{8,9},{9,8},{10,11... | collective-permute-start | bytes 184328 | tf_op jit(solution)/shard_map/ppermute | solution.py:608
  17.3 7.8 %collective-permute-start.1 = (bf16[15,16,128]{2,1,0:T(8,128)(2,1)S(1)}, bf16[15,16,128]{2,1,0:T(8,128)(2,1)S(1)}, u32[]{:S(2)}, u32[]{:S(2)}) collective-permute-start(bf16[15,16,128]{2,1,0:T(8,128)(2,1)S(1)} %get-tuple-element.34), channel_id=1, source_target_pairs={{0,2},{1,3},{2,0},{3,1},{4,6},{5,7},{6,4},{7,5},{8,10},{9,11},{10,... | collective-permute-start | bytes 184328 | tf_op jit(solution)/shard_map/ppermute | solution.py:608
  19.9 6.0 %collective-permute-start.2 = (bf16[15,16,128]{2,1,0:T(8,128)(2,1)S(1)}, bf16[15,16,128]{2,1,0:T(8,128)(2,1)S(1)}, u32[]{:S(2)}, u32[]{:S(2)}) collective-permute-start(bf16[15,16,128]{2,1,0:T(8,128)(2,1)S(1)} %get-tuple-element.35), channel_id=1, source_target_pairs={{0,3},{1,2},{2,1},{3,0},{4,7},{5,6},{6,5},{7,4},{8,11},{9,10},{10,... | collective-permute-start | bytes 184328 | tf_op jit(solution)/shard_map/ppermute | solution.py:608
  19.9 10.9 %copy-start.1 = (bf16[256,64,64]{0,2,1:T(8,128)(2,1)S(1)}, bf16[256,64,64]{0,2,1:T(8,128)(2,1)}, u32[]{:S(2)}) copy-start(bf16[256,64,64]{0,2,1:T(8,128)(2,1)} %param.12) | copy-start | bytes 6291460
  19.9 10.9 %copy-start.2 = (bf16[128,64,64]{0,2,1:T(8,128)(2,1)S(1)}, bf16[128,64,64]{0,2,1:T(8,128)(2,1)}, u32[]{:S(2)}) copy-start(bf16[128,64,64]{0,2,1:T(8,128)(2,1)} %param.15) | copy-start | bytes 3145732
  25.9 15.2 %collective-permute-start.3 = (bf16[66,16,128]{2,1,0:T(8,128)(2,1)S(1)}, bf16[66,16,128]{2,1,0:T(8,128)(2,1)S(1)}, u32[]{:S(2)}, u32[]{:S(2)}) collective-permute-start(bf16[66,16,128]{2,1,0:T(8,128)(2,1)S(1)} %shard_map.122.refs_0_), channel_id=1, source_target_pairs={{0,8},{4,12},{8,0},{12,4},{16,24},{20,28},{24,16},{28,20},{1,9},{5... | collective-permute-start | bytes 811016 | tf_op jit(solution)/shard_map/ppermute | solution.py:608
  27.5 13.7 %collective-permute-start.4 = (bf16[66,16,128]{2,1,0:T(8,128)(2,1)S(1)}, bf16[66,16,128]{2,1,0:T(8,128)(2,1)S(1)}, u32[]{:S(2)}, u32[]{:S(2)}) collective-permute-start(bf16[66,16,128]{2,1,0:T(8,128)(2,1)S(1)} %shard_map.122.refs_0_), channel_id=1, source_target_pairs={{0,16},{4,20},{8,24},{12,28},{16,0},{20,4},{24,8},{28,12},{1,17},{... | collective-permute-start | bytes 811016 | tf_op jit(solution)/shard_map/ppermute | solution.py:608
  29.0 12.1 %collective-permute-start.5 = (bf16[66,16,128]{2,1,0:T(8,128)(2,1)S(1)}, bf16[66,16,128]{2,1,0:T(8,128)(2,1)S(1)}, u32[]{:S(2)}, u32[]{:S(2)}) collective-permute-start(bf16[66,16,128]{2,1,0:T(8,128)(2,1)S(1)} %shard_map.122.refs_0_), channel_id=1, source_target_pairs={{0,24},{4,28},{8,16},{12,20},{16,8},{20,12},{24,0},{28,4},{1,25},{... | collective-permute-start | bytes 811016 | tf_op jit(solution)/shard_map/ppermute | solution.py:608
  29.5 11.7 %collective-permute-start.6 = (bf16[12,80,128]{2,1,0:T(8,128)(2,1)S(1)}, bf16[12,80,128]{2,1,0:T(8,128)(2,1)S(1)}, u32[]{:S(2)}, u32[]{:S(2)}) collective-permute-start(bf16[12,80,128]{2,1,0:T(8,128)(2,1)S(1)} %get-tuple-element.42.refs_4_), channel_id=1, source_target_pairs={{0,2},{1,3},{2,0},{3,1},{4,6},{5,7},{6,4},{7,5},{8,10},{9,11},{10,... | collective-permute-start | bytes 737288 | tf_op jit(solution)/shard_map/ppermute | solution.py:608
  37.4 12.4 %copy-start.4 = (s32[256,2]{0,1:T(2,128)S(1)}, s32[256,2]{0,1:T(2,128)}, u32[]{:S(2)}) copy-start(s32[256,2]{0,1:T(2,128)} %param.13) | copy-start | bytes 6148
  37.4 12.4 %copy-start.5 = (s32[128,2]{0,1:T(2,128)S(1)}, s32[128,2]{0,1:T(2,128)}, u32[]{:S(2)}) copy-start(s32[128,2]{0,1:T(2,128)} %param.16) | copy-start | bytes 3076
  41.2 2.8 %collective-permute-start.7 = (bf16[264,16,128]{2,1,0:T(8,128)(2,1)S(1)}, bf16[264,16,128]{2,1,0:T(8,128)(2,1)S(1)}, u32[]{:S(2)}, u32[]{:S(2)}) collective-permute-start(bf16[264,16,128]{2,1,0:T(8,128)(2,1)S(1)} %get-tuple-element.50.refs_3_), channel_id=1, source_target_pairs={{0,4},{4,0},{8,12},{12,8},{16,20},{20,16},{24,28},{28,24},{1,5},{5... | collective-permute-start | bytes 3244040 | tf_op jit(solution)/shard_map/ppermute | solution.py:608
  41.3 24.4 %collective-permute-start.11 = (bf16[24,80,128]{2,1,0:T(8,128)(2,1)S(1)}, bf16[24,80,128]{2,1,0:T(8,128)(2,1)S(1)}, u32[]{:S(2)}, u32[]{:S(2)}) collective-permute-start(bf16[24,80,128]{2,1,0:T(8,128)(2,1)S(1)} %get-tuple-element.55.refs_5_), channel_id=1, source_target_pairs={{0,1},{1,0},{2,3},{3,2},{4,5},{5,4},{6,7},{7,6},{8,9},{9,8},{10,11... | collective-permute-start | bytes 1474568 | tf_op jit(solution)/shard_map/ppermute | solution.py:608
  44.1 13.7 %collective-permute-start.8 = (f32[4,2,16,128]{3,2,1,0:T(8,128)S(1)}, f32[4,2,16,128]{3,2,1,0:T(8,128)S(1)}, u32[]{:S(2)}, u32[]{:S(2)}) collective-permute-start(f32[4,2,16,128]{3,2,1,0:T(8,128)S(1)} %fusion.refs_0_), channel_id=1, source_target_pairs={{0,1},{1,0},{2,3},{3,2},{4,5},{5,4},{6,7},{7,6},{8,9},{9,8},{10,11... | collective-permute-start | bytes 196616 | tf_op jit(solution)/shard_map/ppermute | solution.py:608
  44.1 13.6 %collective-permute-start.9 = (f32[4,2,16,128]{3,2,1,0:T(8,128)S(1)}, f32[4,2,16,128]{3,2,1,0:T(8,128)S(1)}, u32[]{:S(2)}, u32[]{:S(2)}) collective-permute-start(f32[4,2,16,128]{3,2,1,0:T(8,128)S(1)} %fusion.refs_0_), channel_id=1, source_target_pairs={{0,2},{1,3},{2,0},{3,1},{4,6},{5,7},{6,4},{7,5},{8,10},{9,11},{10,... | collective-permute-start | bytes 196616 | tf_op jit(solution)/shard_map/ppermute | solution.py:608
  47.2 12.7 %collective-permute-start.10 = (f32[4,2,16,128]{3,2,1,0:T(8,128)S(1)}, f32[4,2,16,128]{3,2,1,0:T(8,128)S(1)}, u32[]{:S(2)}, u32[]{:S(2)}) collective-permute-start(f32[4,2,16,128]{3,2,1,0:T(8,128)S(1)} %fusion.refs_0_), channel_id=1, source_target_pairs={{0,3},{1,2},{2,1},{3,0},{4,7},{5,6},{6,5},{7,4},{8,11},{9,10},{10,... | collective-permute-start | bytes 196616 | tf_op jit(solution)/shard_map/ppermute | solution.py:608
  49.8 10.1 %copy-start.3 = (f32[6,64,64]{2,1,0:T(8,128)S(1)}, f32[6,64,64]{2,1,0:T(8,128)}, u32[]{:S(2)}) copy-start(f32[6,64,64]{2,1,0:T(8,128)} %top_ref.1) | copy-start | bytes 294916

commit v10 on v9

--- a/solution.py
+++ b/solution.py
@@ -650,11 +650,10 @@
     pair_part = pair_part + other_part
     tops = [pair_part] + [swapped(pair_part, "col", d) for d in range(1, cols)]
     middle = middle_products(sizes, at, pairs, cells, same_core, other_core)
-    ancestors, root = top_factors(at, tops, top_transfer, leaves)
-    middle, ancestors, root = lax.optimization_barrier((middle, ancestors, root))
     out0, out1 = outer_products(
         sizes, at, pairs, (counts0, counts1), middle, [rows, forwarded], orders
     )
+    ancestors, root = top_factors(at, tops, top_transfer, leaves)
     return (jnp.transpose(out0, (2, 0, 1)), jnp.transpose(out1, (2, 0, 1)), root, ancestors)
 
 

time: 75.1 us -> 71.9 us (0.957)
  waiting for transfers between devices: 10.9 us -> 7.74 us
    ppermute x12, waiting for transfers between devices: 10.9 us -> 7.74 us  [swapped(): lax.ppermute(x, axis, [(i, i ^ d) for i in range(lax.axis_size(axis))])]
  transfers between devices with their start and end apart: 12 -> 12, of which waited for: 5 -> 4; matrix products, arithmetic and copies ran while one was open for 0% -> 0% of each run, Pallas kernels for 32% -> 38%
where the time goes in v10:
time: 71.9 us; the launch traced here: 71.7 us
  Pallas kernels  46.6 us (65%)
  starting transfers between devices  15.1 us (21%)
  waiting for transfers between devices  7.74 us (11%)
  between operations  2.11 us (3%)
    ppermute x12, starting transfers between devices, swapped(): lax.ppermute(x, axis, [(i, i ^ d) for i in range(lax.axis_size(axis))])  15.1 us
    pallas_call x1, Pallas kernels, own_factors(): pl.pallas_call(functools.partial(factor_kernel, own, cols), out_shape=sha...  13.5 us
    pallas_call x1, Pallas kernels, outer_products(): pl.pallas_call(functools.partial(outer_kernel, groups, sizes, len(slots),...  9.03 us
    ppermute x12, waiting for transfers between devices, swapped(): lax.ppermute(x, axis, [(i, i ^ d) for i in range(lax.axis_size(axis))])  7.74 us
    pallas_call x1, Pallas kernels, turned_blocks(): pl.pallas_call(functools.partial(turn_kernel, groups), out_shape=jax.Shap...  6.65 us
    pallas_call x1, Pallas kernels, middle_products(): pl.pallas_call(functools.partial(middle_kernel, groups, sizes), out_shape...  6.36 us
    pallas_call x1, Pallas kernels, top_factors(): pl.pallas_call(functools.partial(top_kernel, leaves), out_shape=(jax.Shap...  5.8 us
    pallas_call x1, Pallas kernels, lifted_root(): pl.pallas_call(functools.partial(chain_kernel, own, cols), out_shape=jax....  5.16 us
  transfers between devices with their start and end apart: 12, of which 4 were waited for; matrix products, arithmetic and copies ran while one was open for 0% of the time, Pallas kernels for 38%

profile of v10, /device:TPU:0, one launch (start us, length us, event | category | flops | bytes accessed | tf_op | source)
XLA Modules:
  0.0 71.7 jit_solution(2580874865057717083)
XLA Ops:
  0.6 0.1 pad_add_fusion.at_ref
  0.7 13.5 %shard_map.120 = (bf16[12,80,128]{2,1,0:T(8,128)(2,1)S(1)}, f32[16,64,64]{2,1,0:T(8,128)S(1)}, bf16[15,16,128]{2,1,0:T(8,128)(2,1)S(1)}, bf16[15,16,128]{2,1,0:T...) custom-call(s32[2]{0:T(128)S(1)} %pad_add_fusion.at_ref, ...), custom_call_target="tpu_custom_call" | custom-call | flops 536870912 | bytes 8388608 | tf_op jit(solution)/shard_map/pallas_call | solution.py:258
  14.2 3.1 %collective-permute-start = (bf16[15,16,128]{2,1,0:T(8,128)(2,1)S(1)}, bf16[15,16,128]{2,1,0:T(8,128)(2,1)S(1)}, u32[]{:S(2)}, u32[]{:S(2)}) collective-permute-start(bf16[15,16,128]{2,1,0:T(8,128)(2,1)S(1)} %get-tuple-element.30), channel_id=1, source_target_pairs={{0,1},{1,0},{2,3},{3,2},{4,5},{5,4},{6,7},{7,6},{8,9},{9,8},{10,11... | collective-permute-start | bytes 184328 | tf_op jit(solution)/shard_map/ppermute | solution.py:608
  17.3 2.6 %collective-permute-start.1 = (bf16[15,16,128]{2,1,0:T(8,128)(2,1)S(1)}, bf16[15,16,128]{2,1,0:T(8,128)(2,1)S(1)}, u32[]{:S(2)}, u32[]{:S(2)}) collective-permute-start(bf16[15,16,128]{2,1,0:T(8,128)(2,1)S(1)} %get-tuple-element.31), channel_id=1, source_target_pairs={{0,2},{1,3},{2,0},{3,1},{4,6},{5,7},{6,4},{7,5},{8,10},{9,11},{10,... | collective-permute-start | bytes 184328 | tf_op jit(solution)/shard_map/ppermute | solution.py:608
  19.9 5.2 %shard_map.121.refs_4_ = bf16[6,16,128]{2,1,0:T(8,128)(2,1)S(1)} custom-call(s32[2]{0:T(128)S(1)} %pad_add_fusion.at_ref, f32[16,64,64]{2,1,0:T(8,128)S(1)} %get-tuple-element.33.gram1_ref, f32[64,64,255]{2,1,0:T(8,128)S(1)} %bitcast.11), custom_call_target="tpu_custom_call" | custom-call | flops 536870912 | bytes 4194304 | tf_op jit(solution)/shard_map/pallas_call | solution.py:320
  25.0 0.0 collective-permute-done.refs_1_
  25.0 0.0 collective-permute-done.1.refs_2_
  25.1 0.8 %collective-permute-done.2.refs_3_ = bf16[15,16,128]{2,1,0:T(8,128)(2,1)S(1)} collective-permute-done((bf16[15,16,128]{2,1,0:T(8,128)(2,1)S(1)}, bf16[15,16,128]{2,1,0:T(8,128)(2,1)S(1)}, u32[]{:S(2)}, u32[]{:S(2)}) %collective-permute-start.2) | collective-permute-done | bytes 61472 | tf_op jit(solution)/shard_map/ppermute | solution.py:608
  25.9 1.6 %collective-permute-start.3 = (bf16[66,16,128]{2,1,0:T(8,128)(2,1)S(1)}, bf16[66,16,128]{2,1,0:T(8,128)(2,1)S(1)}, u32[]{:S(2)}, u32[]{:S(2)}) collective-permute-start(bf16[66,16,128]{2,1,0:T(8,128)(2,1)S(1)} %shard_map.122.refs_0_), channel_id=1, source_target_pairs={{0,8},{4,12},{8,0},{12,4},{16,24},{20,28},{24,16},{28,20},{1,9},{5... | collective-permute-start | bytes 811016 | tf_op jit(solution)/shard_map/ppermute | solution.py:608
  27.5 1.5 %collective-permute-start.4 = (bf16[66,16,128]{2,1,0:T(8,128)(2,1)S(1)}, bf16[66,16,128]{2,1,0:T(8,128)(2,1)S(1)}, u32[]{:S(2)}, u32[]{:S(2)}) collective-permute-start(bf16[66,16,128]{2,1,0:T(8,128)(2,1)S(1)} %shard_map.122.refs_0_), channel_id=1, source_target_pairs={{0,16},{4,20},{8,24},{12,28},{16,0},{20,4},{24,8},{28,12},{1,17},{... | collective-permute-start | bytes 811016 | tf_op jit(solution)/shard_map/ppermute | solution.py:608
  29.0 0.5 collective-permute-start.5
  29.5 1.3 %collective-permute-start.6 = (bf16[12,80,128]{2,1,0:T(8,128)(2,1)S(1)}, bf16[12,80,128]{2,1,0:T(8,128)(2,1)S(1)}, u32[]{:S(2)}, u32[]{:S(2)}) collective-permute-start(bf16[12,80,128]{2,1,0:T(8,128)(2,1)S(1)} %get-tuple-element.39.refs_4_), channel_id=1, source_target_pairs={{0,2},{1,3},{2,0},{3,1},{4,6},{5,7},{6,4},{7,5},{8,10},{9,11},{10,... | collective-permute-start | bytes 737288 | tf_op jit(solution)/shard_map/ppermute | solution.py:608
  30.7 6.6 %shard_map.123.refs_2_ = bf16[384,64,64]{2,1,0:T(8,128)(2,1)S(1)} custom-call(bf16[64,64,256]{2,1,0:T(8,128)(2,1)S(1)} %bitcast.12, bf16[64,64,128]{2,1,0:T(8,128)(2,1)S(1)} %bitcast.14), custom_call_target="tpu_custom_call" | custom-call | flops 1048576 | bytes 1048576 | tf_op jit(solution)/shard_map/pallas_call | solution.py:414
  37.4 0.0 copy-start.4
  37.4 0.0 copy-start.5
  37.4 3.7 %collective-permute-done.6.refs_5_ = bf16[12,80,128]{2,1,0:T(8,128)(2,1)S(1)} collective-permute-done((bf16[12,80,128]{2,1,0:T(8,128)(2,1)S(1)}, bf16[12,80,128]{2,1,0:T(8,128)(2,1)S(1)}, u32[]{:S(2)}, u32[]{:S(2)}) %collective-permute-start.6) | collective-permute-done | bytes 245792 | tf_op jit(solution)/shard_map/ppermute | solution.py:608
  41.1 0.0 collective-permute-done.3.refs_1_
  41.1 0.0 collective-permute-done.4.refs_2_
  41.1 0.0 collective-permute-done.5.refs_3_
  41.1 0.1 shard_map.124
  41.2 0.1 collective-permute-start.7
  41.3 0.1 collective-permute-start.8
  41.4 2.6 %collective-permute-done.7.refs_4_ = bf16[264,16,128]{2,1,0:T(8,128)(2,1)S(1)} collective-permute-done((bf16[264,16,128]{2,1,0:T(8,128)(2,1)S(1)}, bf16[264,16,128]{2,1,0:T(8,128)(2,1)S(1)}, u32[]{:S(2)}, u32[]{:S(2)}) %collective-permute-start.7) | collective-permute-done | bytes 1081376 | tf_op jit(solution)/shard_map/ppermute | solution.py:608
  44.1 0.1 collective-permute-start.9
  44.1 3.1 %collective-permute-start.10 = (f32[4,2,16,128]{3,2,1,0:T(8,128)S(1)}, f32[4,2,16,128]{3,2,1,0:T(8,128)S(1)}, u32[]{:S(2)}, u32[]{:S(2)}) collective-permute-start(f32[4,2,16,128]{3,2,1,0:T(8,128)S(1)} %fusion.refs_0_), channel_id=1, source_target_pairs={{0,2},{1,3},{2,0},{3,1},{4,6},{5,7},{6,4},{7,5},{8,10},{9,11},{10,... | collective-permute-start | bytes 196616 | tf_op jit(solution)/shard_map/ppermute | solution.py:608
  47.2 1.3 %collective-permute-start.11 = (f32[4,2,16,128]{3,2,1,0:T(8,128)S(1)}, f32[4,2,16,128]{3,2,1,0:T(8,128)S(1)}, u32[]{:S(2)}, u32[]{:S(2)}) collective-permute-start(f32[4,2,16,128]{3,2,1,0:T(8,128)S(1)} %fusion.refs_0_), channel_id=1, source_target_pairs={{0,3},{1,2},{2,1},{3,0},{4,7},{5,6},{6,5},{7,4},{8,11},{9,10},{10,... | collective-permute-start | bytes 196616 | tf_op jit(solution)/shard_map/ppermute | solution.py:608
  49.8 6.4 %shard_map.125.refs_4_ = bf16[384,64,64]{2,1,0:T(8,128)(2,1)S(1)} custom-call(s32[2]{0:T(128)S(1)} %pad_add_fusion.at_ref, s32[2,256]{1,0:T(2,128)S(1)} %bitcast.15, s32[2,128]{1,0:T(2,128)S(1)} %bitcast.17, bf16[384,64,64]{2,1,0:T(8,128)(2,1)S(1)} %shard_map.123.refs_2_, bf16[264,16,128]{2,1,0:T(8,128)(2,1)S(1)} %get-tuple-element.47.refs_3_, ...), custom_call_target="tpu_custom_call" | custom-call | flops 201326592 | bytes 1048576 | tf_op jit(solution)/shard_map/pallas_call | solution.py:527
  56.2 0.0 copy-start.3
  56.2 0.6 collective-permute-done.8.refs_6_
  56.8 9.0 %shard_map.126 = (bf16[64,64,256]{2,1,0:T(8,128)(2,1)}, bf16[64,64,128]{2,1,0:T(8,128)(2,1)}) custom-call(s32[2]{0:T(128)S(1)} %pad_add_fusion.at_ref, s32[2,256]{1,0:T(2,128)S(1)} %bitcast.16, s32[2,128]{1,0:T(2,128)S(1)} %bitcast.18, s32[1]{0:T(128)S(6)} %copy.13.refs_2_, s32[1]{0:T(128)S(6)} %copy.14.refs_3_, ...), custom_call_target="tpu_custom_call" | custom-call | flops 201326592 | bytes 4194304 | tf_op jit(solution)/shard_map/pallas_call | solution.py:591
  65.9 0.0 collective-permute-done.9.refs_1_
  65.9 5.8 %shard_map.127 = (f32[1,3,64,64]{3,2,1,0:T(8,128)}, f32[64,64]{1,0:T(8,128)}) custom-call(s32[2]{0:T(128)S(1)} %pad_add_fusion.at_ref, f32[6,64,64]{2,1,0:T(8,128)S(1)} %copy-done.3, f32[4,2,16,128]{3,2,1,0:T(8,128)S(1)} %fusion.refs_0_, f32[4,2,16,128]{3,2,1,0:T(8,128)S(1)} %collective-permute-done.9.refs_1_, ...), custom_call_target="tpu_custom_call" | custom-call | flops 4194304 | bytes 131072 | tf_op jit(solution)/shard_map/pallas_call | solution.py:368
  (15 shorter events, 0.1 us)
Async XLA Ops:
  0.7 19.2 %copy-start = (f32[255,64,64]{0,2,1:T(8,128)S(1)}, f32[255,64,64]{0,2,1:T(8,128)}, u32[]{:S(2)}) copy-start(f32[255,64,64]{0,2,1:T(8,128)} %param.10) | copy-start | bytes 12533764
  14.2 10.8 %collective-permute-start = (bf16[15,16,128]{2,1,0:T(8,128)(2,1)S(1)}, bf16[15,16,128]{2,1,0:T(8,128)(2,1)S(1)}, u32[]{:S(2)}, u32[]{:S(2)}) collective-permute-start(bf16[15,16,128]{2,1,0:T(8,128)(2,1)S(1)} %get-tuple-element.30), channel_id=1, source_target_pairs={{0,1},{1,0},{2,3},{3,2},{4,5},{5,4},{6,7},{7,6},{8,9},{9,8},{10,11... | collective-permute-start | bytes 184328 | tf_op jit(solution)/shard_map/ppermute | solution.py:608
  17.3 7.8 %collective-permute-start.1 = (bf16[15,16,128]{2,1,0:T(8,128)(2,1)S(1)}, bf16[15,16,128]{2,1,0:T(8,128)(2,1)S(1)}, u32[]{:S(2)}, u32[]{:S(2)}) collective-permute-start(bf16[15,16,128]{2,1,0:T(8,128)(2,1)S(1)} %get-tuple-element.31), channel_id=1, source_target_pairs={{0,2},{1,3},{2,0},{3,1},{4,6},{5,7},{6,4},{7,5},{8,10},{9,11},{10,... | collective-permute-start | bytes 184328 | tf_op jit(solution)/shard_map/ppermute | solution.py:608
  19.9 6.0 %collective-permute-start.2 = (bf16[15,16,128]{2,1,0:T(8,128)(2,1)S(1)}, bf16[15,16,128]{2,1,0:T(8,128)(2,1)S(1)}, u32[]{:S(2)}, u32[]{:S(2)}) collective-permute-start(bf16[15,16,128]{2,1,0:T(8,128)(2,1)S(1)} %get-tuple-element.32), channel_id=1, source_target_pairs={{0,3},{1,2},{2,1},{3,0},{4,7},{5,6},{6,5},{7,4},{8,11},{9,10},{10,... | collective-permute-start | bytes 184328 | tf_op jit(solution)/shard_map/ppermute | solution.py:608
  19.9 10.9 %copy-start.1 = (bf16[256,64,64]{0,2,1:T(8,128)(2,1)S(1)}, bf16[256,64,64]{0,2,1:T(8,128)(2,1)}, u32[]{:S(2)}) copy-start(bf16[256,64,64]{0,2,1:T(8,128)(2,1)} %param.12) | copy-start | bytes 6291460
  19.9 10.9 %copy-start.2 = (bf16[128,64,64]{0,2,1:T(8,128)(2,1)S(1)}, bf16[128,64,64]{0,2,1:T(8,128)(2,1)}, u32[]{:S(2)}) copy-start(bf16[128,64,64]{0,2,1:T(8,128)(2,1)} %param.15) | copy-start | bytes 3145732
  25.9 15.2 %collective-permute-start.3 = (bf16[66,16,128]{2,1,0:T(8,128)(2,1)S(1)}, bf16[66,16,128]{2,1,0:T(8,128)(2,1)S(1)}, u32[]{:S(2)}, u32[]{:S(2)}) collective-permute-start(bf16[66,16,128]{2,1,0:T(8,128)(2,1)S(1)} %shard_map.122.refs_0_), channel_id=1, source_target_pairs={{0,8},{4,12},{8,0},{12,4},{16,24},{20,28},{24,16},{28,20},{1,9},{5... | collective-permute-start | bytes 811016 | tf_op jit(solution)/shard_map/ppermute | solution.py:608
  27.5 13.7 %collective-permute-start.4 = (bf16[66,16,128]{2,1,0:T(8,128)(2,1)S(1)}, bf16[66,16,128]{2,1,0:T(8,128)(2,1)S(1)}, u32[]{:S(2)}, u32[]{:S(2)}) collective-permute-start(bf16[66,16,128]{2,1,0:T(8,128)(2,1)S(1)} %shard_map.122.refs_0_), channel_id=1, source_target_pairs={{0,16},{4,20},{8,24},{12,28},{16,0},{20,4},{24,8},{28,12},{1,17},{... | collective-permute-start | bytes 811016 | tf_op jit(solution)/shard_map/ppermute | solution.py:608
  29.0 12.1 %collective-permute-start.5 = (bf16[66,16,128]{2,1,0:T(8,128)(2,1)S(1)}, bf16[66,16,128]{2,1,0:T(8,128)(2,1)S(1)}, u32[]{:S(2)}, u32[]{:S(2)}) collective-permute-start(bf16[66,16,128]{2,1,0:T(8,128)(2,1)S(1)} %shard_map.122.refs_0_), channel_id=1, source_target_pairs={{0,24},{4,28},{8,16},{12,20},{16,8},{20,12},{24,0},{28,4},{1,25},{... | collective-permute-start | bytes 811016 | tf_op jit(solution)/shard_map/ppermute | solution.py:608
  29.5 11.7 %collective-permute-start.6 = (bf16[12,80,128]{2,1,0:T(8,128)(2,1)S(1)}, bf16[12,80,128]{2,1,0:T(8,128)(2,1)S(1)}, u32[]{:S(2)}, u32[]{:S(2)}) collective-permute-start(bf16[12,80,128]{2,1,0:T(8,128)(2,1)S(1)} %get-tuple-element.39.refs_4_), channel_id=1, source_target_pairs={{0,2},{1,3},{2,0},{3,1},{4,6},{5,7},{6,4},{7,5},{8,10},{9,11},{10,... | collective-permute-start | bytes 737288 | tf_op jit(solution)/shard_map/ppermute | solution.py:608
  37.4 12.4 %copy-start.4 = (s32[256,2]{0,1:T(2,128)S(1)}, s32[256,2]{0,1:T(2,128)}, u32[]{:S(2)}) copy-start(s32[256,2]{0,1:T(2,128)} %param.13) | copy-start | bytes 6148
  37.4 12.4 %copy-start.5 = (s32[128,2]{0,1:T(2,128)S(1)}, s32[128,2]{0,1:T(2,128)}, u32[]{:S(2)}) copy-start(s32[128,2]{0,1:T(2,128)} %param.16) | copy-start | bytes 3076
  41.2 2.8 %collective-permute-start.7 = (bf16[264,16,128]{2,1,0:T(8,128)(2,1)S(1)}, bf16[264,16,128]{2,1,0:T(8,128)(2,1)S(1)}, u32[]{:S(2)}, u32[]{:S(2)}) collective-permute-start(bf16[264,16,128]{2,1,0:T(8,128)(2,1)S(1)} %get-tuple-element.47.refs_3_), channel_id=1, source_target_pairs={{0,4},{4,0},{8,12},{12,8},{16,20},{20,16},{24,28},{28,24},{1,5},{5... | collective-permute-start | bytes 3244040 | tf_op jit(solution)/shard_map/ppermute | solution.py:608
  41.3 15.5 %collective-permute-start.8 = (bf16[24,80,128]{2,1,0:T(8,128)(2,1)S(1)}, bf16[24,80,128]{2,1,0:T(8,128)(2,1)S(1)}, u32[]{:S(2)}, u32[]{:S(2)}) collective-permute-start(bf16[24,80,128]{2,1,0:T(8,128)(2,1)S(1)} %get-tuple-element.48.refs_5_), channel_id=1, source_target_pairs={{0,1},{1,0},{2,3},{3,2},{4,5},{5,4},{6,7},{7,6},{8,9},{9,8},{10,11... | collective-permute-start | bytes 1474568 | tf_op jit(solution)/shard_map/ppermute | solution.py:608
  44.1 21.8 %collective-permute-start.9 = (f32[4,2,16,128]{3,2,1,0:T(8,128)S(1)}, f32[4,2,16,128]{3,2,1,0:T(8,128)S(1)}, u32[]{:S(2)}, u32[]{:S(2)}) collective-permute-start(f32[4,2,16,128]{3,2,1,0:T(8,128)S(1)} %fusion.refs_0_), channel_id=1, source_target_pairs={{0,1},{1,0},{2,3},{3,2},{4,5},{5,4},{6,7},{7,6},{8,9},{9,8},{10,11... | collective-permute-start | bytes 196616 | tf_op jit(solution)/shard_map/ppermute | solution.py:608
  44.1 21.7 %collective-permute-start.10 = (f32[4,2,16,128]{3,2,1,0:T(8,128)S(1)}, f32[4,2,16,128]{3,2,1,0:T(8,128)S(1)}, u32[]{:S(2)}, u32[]{:S(2)}) collective-permute-start(f32[4,2,16,128]{3,2,1,0:T(8,128)S(1)} %fusion.refs_0_), channel_id=1, source_target_pairs={{0,2},{1,3},{2,0},{3,1},{4,6},{5,7},{6,4},{7,5},{8,10},{9,11},{10,... | collective-permute-start | bytes 196616 | tf_op jit(solution)/shard_map/ppermute | solution.py:608
  47.2 18.7 %collective-permute-start.11 = (f32[4,2,16,128]{3,2,1,0:T(8,128)S(1)}, f32[4,2,16,128]{3,2,1,0:T(8,128)S(1)}, u32[]{:S(2)}, u32[]{:S(2)}) collective-permute-start(f32[4,2,16,128]{3,2,1,0:T(8,128)S(1)} %fusion.refs_0_), channel_id=1, source_target_pairs={{0,3},{1,2},{2,1},{3,0},{4,7},{5,6},{6,5},{7,4},{8,11},{9,10},{10,... | collective-permute-start | bytes 196616 | tf_op jit(solution)/shard_map/ppermute | solution.py:608
  56.2 9.7 %copy-start.3 = (f32[6,64,64]{2,1,0:T(8,128)S(1)}, f32[6,64,64]{2,1,0:T(8,128)}, u32[]{:S(2)}) copy-start(f32[6,64,64]{2,1,0:T(8,128)} %top_ref.1) | copy-start | bytes 294916
